TPU v7x, 768 devices: a whole 4x8x12 slice. The times are simulated.
768 devices in a mesh: reg: 12 (over z), blk: 64 (over y, x, core).
Axes of the slice: x: 4, y: 8, z: 12, core: 2. Of those that a mesh axis runs over, the one named last changes fastest.
Arguments:
- assembly_rhs: float32 [12, 640, 320], P('reg', 'blk'), may hold values from -250 to 250
- source_slot: int32 [12, 384], P('reg', 'blk'), may hold values from 0 to 639, as said below
- diagonal_blocks: float32 [12, 384, 320, 320], P('reg', 'blk'), may hold values from -2.5 to 2.5
- jacobi_blocks: bfloat16 [12, 384, 320, 320], P('reg', 'blk'), may hold values from -1.5 to 1.5
- coupling: float32 [12, 384, 6, 80, 80], P('reg', 'blk'), may hold values from -0.3125 to 0.3125
- neighbor: int32 [384, 4], P('blk'), may hold values from 0 to 383, as said below
- neighbor_face: int32 [384, 4], P('blk'), may hold values from 0 to 3, as said below
- orientation: int32 [384, 4], P('blk'), may hold values from 0 to 1
Outputs:
- solution: float32 [12, 384, 320], P('reg', 'blk')
- residual: float32 [12, 384, 320], P('reg', 'blk')
Inputs may be any that keep to these rules, and one draw needn't show every extreme that they name: `source_slot`: within one layer the slots are distinct. The elements of one solver device come from at most 2 slots of any one assembly device, and this is reached; some assembly device holds 10 used slots. `neighbor`: the layer is a periodic quadrilateral mesh extruded across layers; the neighbour relation is symmetric. The side faces of one device's elements have neighbours on any one other device at most 3 times. `neighbor_face`: consistent with neighbor: the neighbour's face across face f faces back to this element.
All inputs are finite; a program needn't handle non-finite values.
Results may differ from a plain program's by a relative error of at most 0.0091.
Values sent between devices are 32-bit elements; how exact they have to be, the bound alone decides.
No kernel may reach another device: no remote copies, remote signals or barrier semaphores. Data moves between devices by JAX's collectives and lax.ppermute only.
A program may use at most 32 MiB of HBM per device.

v0:
```python
import jax
import jax.numpy as jnp
from jax import lax
from jax.sharding import PartitionSpec as P

NVAR = 5
NQ = 4
KRYLOV = 2


HIGHEST = lax.Precision.HIGHEST


def extended(cells, sides, width):
    for axis, dim in sides:
        count = lax.axis_size(axis)
        head = lax.slice_in_dim(cells, 0, width, axis=dim)
        tail = lax.slice_in_dim(cells, cells.shape[dim] - width, cells.shape[dim], axis=dim)
        cells = jnp.concatenate(
            [
                lax.ppermute(tail, axis, [(i, (i + 1) % count) for i in range(count)]),
                cells,
                lax.ppermute(head, axis, [((i + 1) % count, i) for i in range(count)]),
            ],
            axis=dim,
        )
    return cells


def face_traces(values_in):
    lead = values_in.shape[:-1]
    shaped = values_in.reshape(lead + (NVAR, NQ, NQ, NQ))
    face_list = (
        shaped[..., 0, :, :],
        shaped[..., -1, :, :],
        shaped[..., :, 0, :],
        shaped[..., :, -1, :],
        shaped[..., 0],
        shaped[..., -1],
    )
    return jnp.stack(
        [one_face.reshape(lead + (NVAR * NQ * NQ,)) for one_face in face_list], axis=-2
    )


def orient_traces(traces, orientation):
    shaped = traces.reshape(traces.shape[:-1] + (NVAR, NQ, NQ))
    flipped = shaped[..., ::-1, :].reshape(traces.shape)
    return jnp.where(orientation[..., None] == 1, flipped, traces)


def lift_faces(face_terms):
    lead = face_terms.shape[:-2]
    face_parts = face_terms.reshape(lead + (6, NVAR, NQ, NQ))
    element_cube = jnp.zeros(lead + (NVAR, NQ, NQ, NQ), face_terms.dtype)
    element_cube = element_cube.at[..., 0, :, :].add(face_parts[..., 0, :, :, :])
    element_cube = element_cube.at[..., -1, :, :].add(face_parts[..., 1, :, :, :])
    element_cube = element_cube.at[..., :, 0, :].add(face_parts[..., 2, :, :, :])
    element_cube = element_cube.at[..., :, -1, :].add(face_parts[..., 3, :, :, :])
    element_cube = element_cube.at[..., 0].add(face_parts[..., 4, :, :, :])
    element_cube = element_cube.at[..., -1].add(face_parts[..., 5, :, :, :])
    return element_cube.reshape(lead + (NVAR * NQ * NQ * NQ,))


def solve_small(gram_matrix, target):
    dimension = len(target)
    augmented = [
        list(gram_matrix[row_index]) + [target[row_index]] for row_index in range(dimension)
    ]
    for pivot_row in range(dimension):
        for lower_row in range(pivot_row + 1, dimension):
            factor = augmented[lower_row][pivot_row] / augmented[pivot_row][pivot_row]
            augmented[lower_row] = [
                augmented[lower_row][column] - factor * augmented[pivot_row][column]
                for column in range(dimension + 1)
            ]
    result = [None] * dimension
    for row_index in reversed(range(dimension)):
        value = augmented[row_index][dimension]
        for column in range(row_index + 1, dimension):
            value = value - augmented[row_index][column] * result[column]
        result[row_index] = value / augmented[row_index][row_index]
    return result


def per_device(
    assembly_rhs,
    source_slot,
    diagonal_blocks,
    jacobi_blocks,
    coupling,
    neighbor,
    neighbor_face,
    orientation,
):
    elements = diagonal_blocks.shape[1]
    slot_ids = source_slot[0]
    piece = lax.all_gather(assembly_rhs, "blk", axis=1, tiled=True)
    piece_rows = piece.shape[1]
    selector = (slot_ids[:, None] == jnp.arange(piece_rows, dtype=jnp.int32)[None, :]).astype(
        jnp.float32
    )
    start_vec = jnp.dot(selector, piece[0], precision=HIGHEST)
    side_rows = (neighbor * 4 + neighbor_face).reshape(-1)

    def precondition(values_in):
        return jnp.einsum(
            "eij,ej->ei",
            jacobi_blocks[0],
            values_in.astype(jnp.bfloat16),
            preferred_element_type=jnp.float32,
        )

    def newest_products(vectors):
        newest = vectors[-1]
        products = [jnp.sum(newest * vectors[inner]) for inner in range(1, len(vectors))]
        return jnp.stack(products + [jnp.sum(newest * start_vec)])

    vectors = [start_vec]
    summed = []
    for krylov_step in range(KRYLOV):
        apply_values_in = precondition(vectors[-1])
        traces = face_traces(apply_values_in)
        apply_side_traces = traces[:, :4].reshape(elements * 4, traces.shape[-1])
        all_sides = lax.all_gather(apply_side_traces, "blk", axis=0, tiled=True)
        picked = orient_traces(
            jnp.take(all_sides, side_rows, axis=0).reshape(elements, 4, -1), orientation
        )
        layers = jnp.stack([traces[:, 5], traces[:, 4]], axis=1)[None]
        padded = extended(layers, (("reg", 0),), 1)
        neighbor_traces = jnp.concatenate(
            [picked, padded[0, :, 0][:, None], padded[2, :, 1][:, None]], axis=1
        )
        face_terms = jnp.einsum("efij,efj->efi", coupling[0], neighbor_traces, precision=HIGHEST)
        diagonal_part = jnp.einsum(
            "eij,ej->ei", diagonal_blocks[0], apply_values_in, precision=HIGHEST
        )
        vectors.append(diagonal_part + lift_faces(face_terms))
    local_parts = [newest_products(vectors[: count_used + 2]) for count_used in range(KRYLOV)]
    joined = lax.psum(jnp.concatenate(local_parts), ("reg", "blk"))
    summed = []
    offset = 0
    for krylov_step in range(KRYLOV):
        summed.append(joined[offset : offset + krylov_step + 2])
        offset = offset + krylov_step + 2
    gram_matrix = [
        [summed[max(row_index, column)][min(row_index, column)] for column in range(KRYLOV)]
        for row_index in range(KRYLOV)
    ]
    target = [summed[row_index][row_index + 1] for row_index in range(KRYLOV)]
    weights_found = solve_small(gram_matrix, target)
    combined = weights_found[0] * vectors[0]
    remaining = start_vec - weights_found[0] * vectors[1]
    combined = combined + weights_found[1] * vectors[1]
    remaining = remaining - weights_found[1] * vectors[2]
    solution = precondition(combined)
    return (solution[None], remaining[None])


def solution(mesh):
    placed = (
        P("reg", "blk", None),
        P("reg", "blk"),
        P("reg", "blk", None, None),
        P("reg", "blk", None, None),
        P("reg", "blk", None, None, None),
        P("blk", None),
        P("blk", None),
        P("blk", None),
    )
    return jax.shard_map(
        per_device,
        mesh=mesh,
        in_specs=placed,
        out_specs=(P("reg", "blk", None), P("reg", "blk", None)),
        check_vma=False,
    )
```

profile of v0, /device:TPU:1, one launch (start us, length us, event | category | flops | bytes accessed | tf_op | source)
XLA Modules:
  0.0 400.2 jit_solution(13847430193854339159)
XLA Ops:
  0.7 63.9 %all_gather.9 = f32[1,640,320]{2,0,1:T(1,128)} all-gather(f32[1,10,320]{2,0,1:T(1,128)} %param.34), channel_id=1, replica_groups=mesh['reg'=12,'blk'=64] {'blk'}, dimensions={1}, use_global_device_ids=true | all-gather | bytes 832000 | tf_op jit(solution)/shard_map/all_gather | solution.py:98
  64.5 3.1 copy.59
  67.7 1.6 fusion.14
  69.3 1.9 fusion.12
  72.4 8.3 %collective-permute-start.1 = (f32[1,6,2,80]{3,2,1,0:T(2,128)S(1)}, f32[1,6,2,80]{3,2,1,0:T(2,128)S(1)}, u32[]{:S(2)}, u32[]{:S(2)}) collective-permute-start(f32[1,6,2,80]{3,2,1,0:T(2,128)S(1)} %maximum_bitcast_fusion.2), channel_id=1, source_target_pairs={{64,0},{128,64},{192,128},{256,192},{320,256},{384,320},{448,384},... | collective-permute-start | bytes 11528 | tf_op jit(solution)/shard_map/ppermute | solution.py:23
  80.7 1.9 collective-permute-start
  83.7 53.8 %all_gather.10 = f32[1536,80]{1,0:T(8,128)} all-gather(f32[24,80]{1,0:T(8,128)S(1)} %bitcast.133), channel_id=1, replica_groups=mesh['reg'=12,'blk'=64] {'blk'}, dimensions={0}, use_global_device_ids=true | all-gather | bytes 499200 | tf_op jit(solution)/shard_map/all_gather | solution.py:125
  137.5 1.7 gather_fusion
  140.1 2.7 fusion.2
  142.9 2.4 fusion.6
  147.4 1.7 copy.65
  149.1 1.5 copy.67
  150.7 3.2 scatter-add.41
  154.9 3.5 scatter-add.44
  158.4 1.5 copy.69
  161.0 11.3 %scatter-add.45 = f32[6,5,4,4,4]{3,2,1,0,4:T(4,128)S(1)} dynamic-update-slice(f32[6,5,4,4,4]{3,2,1,0,4:T(4,128)S(1)} %scatter-add.44, f32[6,5,4,1,4]{3,2,1,0,4:T(4,128)S(1)} %slice_add_fusion.2, s32[]{:T(128)} %constant.290.clone.1, s32[]{:T(128)} %constant.290.clone.1, s32[]{:T(128)} %constant.290.clone.1, s32[]{:T(128)} %constant.291.clone.1, s32[]{:T(128)} %constant.290.clone.1) | dynamic-update-slice | bytes 3844 | tf_op jit(solution)/shard_map/scatter-add | solution.py:59
  175.2 1.9 fusion.10
  179.8 4.8 %collective-permute-start.3 = (f32[1,6,2,80]{3,2,1,0:T(2,128)}, f32[1,6,2,80]{3,2,1,0:T(2,128)}, u32[]{:S(2)}, u32[]{:S(2)}) collective-permute-start(f32[1,6,2,80]{3,2,1,0:T(2,128)} %maximum_bitcast_fusion.3), channel_id=1, source_target_pairs={{64,0},{128,64},{192,128},{256,192},{320,256},{384,320},{448,384},... | collective-permute-start | bytes 11528 | tf_op jit(solution)/shard_map/ppermute | solution.py:23
  184.7 1.9 collective-permute-start.2
  187.9 53.6 %all_gather.11 = f32[1536,80]{1,0:T(8,128)} all-gather(f32[24,80]{1,0:T(8,128)S(1)} %bitcast.134), channel_id=1, replica_groups=mesh['reg'=12,'blk'=64] {'blk'}, dimensions={0}, use_global_device_ids=true | all-gather | bytes 499200 | tf_op jit(solution)/shard_map/all_gather | solution.py:125
  241.5 1.7 gather_fusion.1
  243.9 2.7 fusion
  248.1 2.4 fusion.4
  253.8 1.5 copy.78
  255.3 2.7 scatter-add.51
  259.0 3.5 scatter-add.54
  262.5 1.5 copy.80
  264.0 1.1 slice_add_fusion
  265.1 11.3 %scatter-add.55 = f32[6,5,4,4,4]{3,2,1,0,4:T(4,128)S(1)} dynamic-update-slice(f32[6,5,4,4,4]{3,2,1,0,4:T(4,128)S(1)} %scatter-add.54, f32[6,5,4,1,4]{3,2,1,0,4:T(4,128)S(1)} %slice_add_fusion, s32[]{:T(128)} %constant.290.clone.1, s32[]{:T(128)} %constant.290.clone.1, s32[]{:T(128)} %constant.290.clone.1, s32[]{:T(128)} %constant.291.clone.1, s32[]{:T(128)} %constant.290.clone.1) | dynamic-update-slice | bytes 3844 | tf_op jit(solution)/shard_map/scatter-add | solution.py:59
  280.0 3.3 concatenate.35
  283.2 107.4 %psum.7 = f32[5]{0:T(128)S(1)} all-reduce(f32[5]{0:T(128)S(1)} %concatenate.35), channel_id=1, replica_groups=mesh['reg'=12,'blk'=64] {'reg','blk'}, use_global_device_ids=true, to_apply=%region_5.7 | all-reduce | flops 5 | bytes 40 | tf_op jit(solution)/shard_map/psum | solution.py:140
  397.0 1.9 fusion.8
  (102 shorter events, 26.1 us)
Async XLA Ops:
  0.6 139.5 %copy-start = (f32[1,6,320,320]{3,2,1,0:T(8,128)S(1)}, f32[1,6,320,320]{3,2,1,0:T(8,128)}, u32[]{:S(2)}) copy-start(f32[1,6,320,320]{3,2,1,0:T(8,128)} %param.36) | copy-start | bytes 7372804
  0.6 67.0 %copy-start.8 = (s32[1,6]{1,0:T(1,128)S(1)}, s32[1,6]{1,0:T(1,128)}, u32[]{:S(2)}) copy-start(s32[1,6]{1,0:T(1,128)} %param.35) | copy-start | bytes 76
  69.3 13.8 %copy-start.5 = (s32[6,4]{0,1:T(4,128)S(1)}, s32[6,4]{0,1:T(4,128)}, u32[]{:S(2)}) copy-start(s32[6,4]{0,1:T(4,128)} %param.40) | copy-start | bytes 292
  69.3 13.8 %copy-start.6 = (s32[6,4]{0,1:T(4,128)S(1)}, s32[6,4]{0,1:T(4,128)}, u32[]{:S(2)}) copy-start(s32[6,4]{0,1:T(4,128)} %param.39) | copy-start | bytes 292
  72.1 67.8 %copy-start.7 = (s32[6,4]{0,1:T(4,128)S(1)}, s32[6,4]{0,1:T(4,128)}, u32[]{:S(2)}) copy-start(s32[6,4]{0,1:T(4,128)} %param.41) | copy-start | bytes 292
  72.4 70.5 %collective-permute-start.1 = (f32[1,6,2,80]{3,2,1,0:T(2,128)S(1)}, f32[1,6,2,80]{3,2,1,0:T(2,128)S(1)}, u32[]{:S(2)}, u32[]{:S(2)}) collective-permute-start(f32[1,6,2,80]{3,2,1,0:T(2,128)S(1)} %maximum_bitcast_fusion.2), channel_id=1, source_target_pairs={{64,0},{128,64},{192,128},{256,192},{320,256},{384,320},{448,384},... | collective-permute-start | bytes 11528 | tf_op jit(solution)/shard_map/ppermute | solution.py:23
  80.7 62.2 %collective-permute-start = (f32[1,6,2,80]{3,2,1,0:T(2,128)S(1)}, f32[1,6,2,80]{3,2,1,0:T(2,128)S(1)}, u32[]{:S(2)}, u32[]{:S(2)}) collective-permute-start(f32[1,6,2,80]{3,2,1,0:T(2,128)S(1)} %maximum_bitcast_fusion.2), channel_id=1, source_target_pairs={{0,64},{64,128},{128,192},{192,256},{256,320},{320,384},{384,448},... | collective-permute-start | bytes 11528 | tf_op jit(solution)/shard_map/ppermute | solution.py:21
  140.1 2.8 copy-start.1
  145.6 3.6 copy-start.4
  179.8 66.9 %collective-permute-start.3 = (f32[1,6,2,80]{3,2,1,0:T(2,128)}, f32[1,6,2,80]{3,2,1,0:T(2,128)}, u32[]{:S(2)}, u32[]{:S(2)}) collective-permute-start(f32[1,6,2,80]{3,2,1,0:T(2,128)} %maximum_bitcast_fusion.3), channel_id=1, source_target_pairs={{64,0},{128,64},{192,128},{256,192},{320,256},{384,320},{448,384},... | collective-permute-start | bytes 11528 | tf_op jit(solution)/shard_map/ppermute | solution.py:23
  184.7 62.7 %collective-permute-start.2 = (f32[1,6,2,80]{3,2,1,0:T(2,128)}, f32[1,6,2,80]{3,2,1,0:T(2,128)}, u32[]{:S(2)}, u32[]{:S(2)}) collective-permute-start(f32[1,6,2,80]{3,2,1,0:T(2,128)} %maximum_bitcast_fusion.3), channel_id=1, source_target_pairs={{0,64},{64,128},{128,192},{192,256},{256,320},{320,384},{384,448},... | collective-permute-start | bytes 11528 | tf_op jit(solution)/shard_map/ppermute | solution.py:21
  243.9 4.2 %copy-start.2 = (f32[1,6,6,80,80]{4,3,2,1,0:T(8,128)S(1)}, f32[1,6,6,80,80]{4,3,2,1,0:T(8,128)}, u32[]{:S(2)}) copy-start(f32[1,6,6,80,80]{4,3,2,1,0:T(8,128)} %param.38) | copy-start | bytes 2764804
  250.8 0.8 copy-start.3
where the time goes:
time: 402 us; the launch traced here: 400 us
  blocking collectives  279 us (69%)
  local copies, waits for them, and re-layouts  70.7 us (18%)
  matrix products  17.4 us (4%)
  starting transfers between devices  17 us (4%)
  other arithmetic  9.5 us (2%)
  between operations  6.79 us (2%)
    psum x1, blocking collectives, per_device(): joined = lax.psum(jnp.concatenate(local_parts), ('reg', 'blk'))  107 us
    all_gather x2, blocking collectives, per_device(): all_sides = lax.all_gather(apply_side_traces, 'blk', axis=0, tiled=True)  107 us
    all_gather x1, blocking collectives, per_device(): piece = lax.all_gather(assembly_rhs, 'blk', axis=1, tiled=True)  63.9 us
    scatter-add x2, local copies, waits for them, and re-layouts, lift_faces(): element_cube.at[..., :, -1, :].add(face_parts[..., 3, :, :, :])  22.7 us
    ppermute x2, starting transfers between devices, extended(): lax.ppermute(head, axis, [((i + 1) % count, i) for i in range(count)])  13.2 us
  transfers between devices with their start and end apart: 4, of which 0 were waited for; matrix products, arithmetic and copies ran while one was open for 3% of the time, Pallas kernels for 0%

commit v1 on v0

v1 whole, which is shorter than its diff:
```python
import functools

import jax
import jax.numpy as jnp
import numpy as np
from jax import lax
from jax.experimental import pallas as pl
from jax.experimental.pallas import tpu as pltpu
from jax.sharding import PartitionSpec as P

NVAR = 5
NQ = 4
DOF = NVAR * NQ**3
FDOF = NVAR * NQ**2
ELEMS = 6
PAD = 8
SLOTS = 10
PER_PAIR = 3
WIDTH = 256
WINDOW = 384
F32 = jnp.float32
BF16 = jnp.bfloat16


def face_index():
    cube = np.arange(DOF).reshape(NVAR, NQ, NQ, NQ)
    faces = (cube[:, 0], cube[:, -1], cube[:, :, 0], cube[:, :, -1], cube[..., 0], cube[..., -1])
    return np.stack([one.reshape(-1) for one in faces])


def trace_matrix():
    return (face_index()[:, :, None] == np.arange(DOF)[None, None, :]).astype(np.float32)


def params(megabytes):
    return pltpu.CompilerParams(vmem_limit_bytes=megabytes * 2**20)


def cost(flops, moved):
    return pl.CostEstimate(flops=flops, bytes_accessed=moved, transcendentals=0)


def vmem(count):
    return [pl.BlockSpec(memory_space=pltpu.VMEM)] * count


def smem():
    return pl.BlockSpec(memory_space=pltpu.SMEM)


def mul_t(rows, matrix):
    return lax.dot_general(rows, matrix, (((1,), (1,)), ((), ())), preferred_element_type=F32)


def mul(left, right):
    return lax.dot_general(left, right, (((1,), (0,)), ((), ())), preferred_element_type=F32)


def two_parts(values):
    high = values.astype(BF16)
    low = (values - high.astype(F32)).astype(BF16)
    return high, low


def stacked_parts(values):
    high = values.astype(BF16).astype(F32)
    return jnp.concatenate([high, values - high], axis=0).astype(BF16)


def own_row(result, element):
    row = lax.broadcasted_iota(jnp.int32, result[:PAD].shape, 0)
    return jnp.where(row == element, result[:PAD] + result[PAD:], 0.0)


def high_row(result, element):
    row = lax.broadcasted_iota(jnp.int32, result[:PAD].shape, 0)
    return jnp.where(row == element, result[:PAD], 0.0)


def pick_kernel(wanted_ref, rows_ref, out_ref):
    members = wanted_ref.shape[0]
    for member in range(members):
        for element in range(ELEMS):
            slot = wanted_ref[member, element]
            device = slot // SLOTS
            place = slot - device * SLOTS
            start = pl.multiple_of((place * 5 // 2) * 128, 128)
            out_ref[member, :, element * WINDOW : (element + 1) * WINDOW] = rows_ref[
                device // members, :, pl.ds(start, WINDOW)
            ]


def prepare_kernel(select_ref, jacobi_ref, coupling_ref, trace_rows_ref, high_ref, low_ref):
    for element in range(ELEMS):
        trace_rows_ref[element] = mul(select_ref[...], jacobi_ref[element]).astype(BF16)
    for block in range(6 * ELEMS):
        high, low = two_parts(coupling_ref[block])
        high_ref[block] = high
        low_ref[block] = low


def send_traces(vector, trace_rows_ref, pack_ref, send_ref, up_ref, down_ref, local_ref):
    parts = stacked_parts(vector)
    traces = []
    for face in range(6):
        rows = None
        for element in range(ELEMS):
            matrix = trace_rows_ref[element, face * FDOF : (face + 1) * FDOF, :]
            term = high_row(mul_t(parts, matrix), element)
            rows = term if rows is None else rows + term
        traces.append(rows)
    pad = jnp.zeros((PAD, 128 - FDOF), F32)
    down_ref[...] = jnp.concatenate([traces[4], pad], axis=1)
    up_ref[...] = jnp.concatenate([traces[5], pad], axis=1)
    sides = jnp.concatenate(
        [jnp.concatenate([one, jnp.zeros((PAD, WIDTH - FDOF), F32)], axis=1) for one in traces[:4]],
        axis=0,
    )
    local_ref[...] = sides[:, :128]
    spread = jnp.concatenate(
        [sides] + [pltpu.roll(sides, FDOF * place, 1) for place in range(1, PER_PAIR)], axis=0
    )
    high, low = two_parts(spread)
    send_ref[:, 0, :] = mul(pack_ref[...], high) + mul(pack_ref[...], low)


def first_kernel(
    slots_ref, rows_ref, trace_rows_ref, pack_ref,
    rhs_ref, send_ref, up_ref, down_ref, local_ref, held_ref,
):
    held_ref[...] = jnp.zeros(held_ref.shape, F32)
    for element in range(ELEMS):
        slot = slots_ref[0, element]
        device = slot // SLOTS
        place = slot - device * SLOTS
        members = rows_ref.shape[0]
        column = device - (device // members) * members
        window = rows_ref[column, :, element * WINDOW : (element + 1) * WINDOW]
        turned = pltpu.roll(window, WINDOW - 64, 1)
        odd = place - (place // 2) * 2
        held_ref[element : element + 1, :] = jnp.where(odd == 1, turned, window)
    rhs = held_ref[:, :DOF]
    rhs_ref[...] = rhs
    send_traces(rhs, trace_rows_ref, pack_ref, send_ref, up_ref, down_ref, local_ref)


def own_kernel(vector_ref, jacobi_ref, diagonal_ref, full_ref, product_ref):
    parts = stacked_parts(vector_ref[...])
    rounded = jnp.zeros((PAD, DOF), F32)
    full = jnp.zeros((PAD, DOF), F32)
    for element in range(ELEMS):
        result = mul_t(parts, jacobi_ref[element])
        rounded = rounded + high_row(result, element)
        full = full + own_row(result, element)
    full_ref[...] = full
    parts = stacked_parts(rounded)
    total = jnp.zeros((PAD, DOF), F32)
    for element in range(ELEMS):
        high, low = two_parts(diagonal_ref[element])
        total = total + own_row(mul_t(parts, high) + mul_t(parts, low), element)
    product_ref[...] = total


def add_neighbors(
    product_ref, recv_ref, below_ref, above_ref, local_ref, turn_ref,
    unpack_ref, here_ref, high_ref, low_ref, lift_ref,
):
    high, low = two_parts(recv_ref[:, 0, :])
    arrived = mul(unpack_ref[...], high) + mul(unpack_ref[...], low)
    count = 4 * PAD
    sides = arrived[:count, :128]
    for place in range(1, PER_PAIR):
        rows = arrived[place * count : (place + 1) * count]
        sides = sides + pltpu.roll(rows, WIDTH - FDOF * place, 1)[:, :128]
    high, low = two_parts(local_ref[...])
    sides = sides + mul(here_ref[...], high) + mul(here_ref[...], low)
    lane = lax.broadcasted_iota(jnp.int32, sides.shape, 1)
    step = (lane // 4) % 4
    turned = jnp.where(
        step == 0,
        pltpu.roll(sides, 128 - 12, 1),
        jnp.where(
            step == 1,
            pltpu.roll(sides, 128 - 4, 1),
            jnp.where(step == 2, pltpu.roll(sides, 4, 1), pltpu.roll(sides, 12, 1)),
        ),
    )
    sides = jnp.where(turn_ref[...] == 1, turned, sides)
    total = product_ref[...]
    for face in range(6):
        if face < 4:
            traces = sides[face * PAD : (face + 1) * PAD]
        else:
            traces = below_ref[...] if face == 4 else above_ref[...]
        parts = stacked_parts(traces[:, :FDOF])
        terms = jnp.zeros((PAD, FDOF), F32)
        for element in range(ELEMS):
            block = element * 6 + face
            terms = terms + own_row(mul_t(parts, high_ref[block]) + mul_t(parts, low_ref[block]), element)
        lifted = mul(stacked_parts(terms), lift_ref[face])
        total = total + lifted[:PAD] + lifted[PAD:]
    return total


def middle_kernel(*refs):
    operand, (trace_rows_ref, pack_ref), outs = refs[:11], refs[11:13], refs[13:]
    vector_ref, send_ref, up_ref, down_ref, local_ref = outs
    vector = add_neighbors(*operand)
    vector_ref[...] = vector
    send_traces(vector, trace_rows_ref, pack_ref, send_ref, up_ref, down_ref, local_ref)


def last_kernel(*refs):
    operand, (rhs_ref, first_ref, vector_ref, sums_ref) = refs[:11], refs[11:]
    second = add_neighbors(*operand)
    vector_ref[...] = second
    first, rhs = first_ref[...], rhs_ref[...]
    lane = lax.broadcasted_iota(jnp.int32, (1, 128), 1)
    sums = jnp.zeros((1, 128), F32)
    pairs = ((first, first), (first, second), (second, second), (first, rhs), (second, rhs))
    for place, (one, other) in enumerate(pairs):
        sums = jnp.where(lane == place, jnp.sum(one * other), sums)
    for copy in range(sums_ref.shape[0]):
        sums_ref[copy] = sums


def spread_kernel(parts_ref, sums_ref):
    total = parts_ref[0]
    for part in range(1, parts_ref.shape[0]):
        total = total + parts_ref[part]
    for copy in range(sums_ref.shape[0]):
        sums_ref[copy] = total


def finish_kernel(parts_ref, rhs_ref, first_ref, second_ref, full0_ref, full1_ref, solution_ref, residual_ref):
    total = parts_ref[0]
    for part in range(1, parts_ref.shape[0]):
        total = total + parts_ref[part]
    g11, g12, g22, t1, t2 = (total[:, place : place + 1] for place in range(5))
    factor = g12 / g11
    weight2 = (t2 - factor * t1) / (g22 - factor * g12)
    weight1 = (t1 - g12 * weight2) / g11
    solution_ref[0] = (weight1 * full0_ref[...] + weight2 * full1_ref[...])[:ELEMS]
    residual_ref[0] = (rhs_ref[...] - weight1 * first_ref[...] - weight2 * second_ref[...])[:ELEMS]


def shape(*dims, dtype=F32):
    return jax.ShapeDtypeStruct(dims, dtype)


def routes(neighbor, neighbor_face, orientation, devices):
    def sides(table, fill):
        padded = jnp.pad(table.T, ((0, 0), (0, PAD - ELEMS)), constant_values=fill)
        return padded.reshape(-1)

    own = lax.axis_index("blk").astype(jnp.int32)
    near = sides(neighbor, -ELEMS)
    face = sides(neighbor_face, 0)
    turn = sides(orientation, 0)
    count = 4 * PAD
    row = jnp.arange(count, dtype=jnp.int32)
    owner = near // ELEMS
    remote = (owner != own) & (near >= 0)
    local = owner == own
    same = owner[:, None] == owner[None, :]
    own_key = row % PAD * 4 + row // PAD
    near_key = near * 4 + face
    send_place = jnp.sum(same & (own_key[None, :] < own_key[:, None]), axis=1)
    near_place = jnp.sum(same & (near_key[None, :] < near_key[:, None]), axis=1)
    device = jnp.arange(devices, dtype=jnp.int32)
    place = jnp.arange(PER_PAIR, dtype=jnp.int32)
    to = (device[:, None] == owner[None, :]) & remote[None, :]
    pack = to[:, None, :] & (place[None, :, None] == send_place[None, None, :])
    unpack = to.T[None] & (place[:, None, None] == near_place[None, :, None])
    here = local[:, None] & (row[None, :] == (face * PAD + near % ELEMS)[:, None])
    return (
        pack.reshape(devices, PER_PAIR * count).astype(BF16),
        unpack.reshape(PER_PAIR * count, devices).astype(BF16),
        here.astype(BF16),
        jnp.broadcast_to(turn[:, None], (count, 128)),
    )


def per_device(
    columns, members,
    assembly_rhs, source_slot, diagonal_blocks, jacobi_blocks, coupling, neighbor, neighbor_face, orientation,
):
    devices = columns * members
    layers = lax.axis_size("reg")
    column_groups = [[member + members * y for y in range(columns)] for member in range(members)]
    member_groups = [[member + members * y for member in range(members)] for y in range(columns)]
    select = trace_matrix()
    diagonal, jacobi = diagonal_blocks[0], jacobi_blocks[0]

    own_rows = jnp.broadcast_to(assembly_rhs.reshape(1, 1, SLOTS * DOF), (columns, 1, SLOTS * DOF))
    own_slots = jnp.broadcast_to(source_slot[:, None, :], (members, 1, ELEMS))
    wanted = lax.all_to_all(own_slots, "blk", 0, 0, axis_index_groups=member_groups, tiled=True)
    rows = lax.all_to_all(own_rows, "blk", 0, 0, axis_index_groups=column_groups, tiled=True)

    pack, unpack, here, turn = routes(neighbor, neighbor_face, orientation, devices)
    trace_rows, high, low = pl.pallas_call(
        prepare_kernel,
        out_shape=(
            shape(ELEMS, 6 * FDOF, DOF, dtype=BF16),
            shape(6 * ELEMS, FDOF, FDOF, dtype=BF16),
            shape(6 * ELEMS, FDOF, FDOF, dtype=BF16),
        ),
        in_specs=vmem(3),
        out_specs=tuple(vmem(3)),
        compiler_params=params(16),
        cost_estimate=cost(6 * 2 * 480 * 320 * 320, 6 * 2**20),
        name="prepare",
    )(jnp.asarray(select.reshape(6 * FDOF, DOF), BF16), jacobi, coupling.reshape(6 * ELEMS, FDOF, FDOF))

    picked = pl.pallas_call(
        pick_kernel,
        out_shape=shape(members, 1, ELEMS * WINDOW),
        in_specs=[smem()] + vmem(1),
        out_specs=vmem(1)[0],
        cost_estimate=cost(1000, 2**17),
        name="pick",
    )(wanted.reshape(members, ELEMS), rows)
    mine = lax.all_to_all(picked, "blk", 0, 0, axis_index_groups=member_groups, tiled=True)

    sent = (
        shape(devices, 1, WIDTH),
        shape(PAD, 128),
        shape(PAD, 128),
        shape(4 * PAD, 128),
    )
    lift = jnp.asarray(select, BF16)

    def exchange(send, up, down):
        below = lax.ppermute(up, "reg", [(i, (i + 1) % layers) for i in range(layers)])
        above = lax.ppermute(down, "reg", [((i + 1) % layers, i) for i in range(layers)])
        return lax.all_to_all(send, "blk", 0, 0, tiled=True), below, above

    def own_part(vector):
        return pl.pallas_call(
            own_kernel,
            out_shape=(shape(PAD, DOF), shape(PAD, DOF)),
            in_specs=vmem(3),
            out_specs=tuple(vmem(2)),
            compiler_params=params(16),
            cost_estimate=cost(6 * 4 * 16 * 320 * 320, 4 * 2**20),
            name="own_part",
        )(vector, jacobi, diagonal)

    rhs, send, up, down, local = pl.pallas_call(
        first_kernel,
        out_shape=(shape(PAD, DOF),) + sent,
        in_specs=[smem()] + vmem(3),
        out_specs=tuple(vmem(5)),
        scratch_shapes=[pltpu.VMEM((PAD, WINDOW), F32)],
        compiler_params=params(16),
        cost_estimate=cost(6 * 2 * 16 * 480 * 320, 2**21),
        name="first",
    )(source_slot, mine, trace_rows, pack)
    recv, below, above = exchange(send, up, down)
    full0, product = own_part(rhs)

    first, send, up, down, local1 = pl.pallas_call(
        middle_kernel,
        out_shape=(shape(PAD, DOF),) + sent,
        in_specs=vmem(13),
        out_specs=tuple(vmem(5)),
        compiler_params=params(16),
        cost_estimate=cost(6 * 4 * 16 * 480 * 320, 4 * 2**20),
        name="middle",
    )(product, recv, below, above, local, turn, unpack, here, high, low, lift, trace_rows, pack)
    recv, below, above = exchange(send, up, down)
    full1, product = own_part(first)

    second, sums = pl.pallas_call(
        last_kernel,
        out_shape=(shape(PAD, DOF), shape(layers, 1, 128)),
        in_specs=vmem(13),
        out_specs=tuple(vmem(2)),
        compiler_params=params(16),
        cost_estimate=cost(6 * 2 * 16 * 480 * 320, 2**21),
        name="last",
    )(product, recv, below, above, local1, turn, unpack, here, high, low, lift, rhs, first)
    sums = lax.all_to_all(sums, "reg", 0, 0, tiled=True)
    sums = pl.pallas_call(
        spread_kernel,
        out_shape=shape(devices, 1, 128),
        in_specs=vmem(1),
        out_specs=vmem(1)[0],
        cost_estimate=cost(2000, 2**15),
        name="spread",
    )(sums)
    sums = lax.all_to_all(sums, "blk", 0, 0, tiled=True)
    return pl.pallas_call(
        finish_kernel,
        out_shape=(shape(1, ELEMS, DOF), shape(1, ELEMS, DOF)),
        in_specs=vmem(6),
        out_specs=tuple(vmem(2)),
        cost_estimate=cost(20000, 2**16),
        name="finish",
    )(sums, rhs, first, second, full0, full1)


def solution(mesh):
    placed = (
        P("reg", "blk", None),
        P("reg", "blk"),
        P("reg", "blk", None, None),
        P("reg", "blk", None, None),
        P("reg", "blk", None, None, None),
        P("blk", None),
        P("blk", None),
        P("blk", None),
    )
    members = 8
    return jax.shard_map(
        functools.partial(per_device, mesh.shape["blk"] // members, members),
        mesh=mesh,
        in_specs=placed,
        out_specs=(P("reg", "blk", None), P("reg", "blk", None)),
        check_vma=False,
    )
```

time: 402 us -> 144 us (0.36)
  blocking collectives: 279 us -> 35.3 us
  local copies, waits for them, and re-layouts: 70.7 us -> 19.5 us
  starting transfers between devices: 17 us -> 56.9 us
  Pallas kernels: 0 us -> 18.4 us
  matrix products: 17.4 us -> 0 us
  waiting for transfers between devices: 0.01 us -> 8.65 us
  other arithmetic: 9.5 us -> 2.7 us
  between operations: 6.79 us -> 0.91 us
    all_gather x3 -> x0, blocking collectives: 171 us -> none  [the longest x2 107 us: per_device(): all_sides = lax.all_gather(apply_side_traces, 'blk', axis=0, tiled=True)]
    psum x1 -> x0, blocking collectives: 107 us -> none  [per_device(): joined = lax.psum(jnp.concatenate(local_parts), ('reg', 'blk'))]
    all_to_all x0 -> x5, starting transfers between devices: none -> 38.4 us  [the longest x2 16 us: exchange(): return (lax.all_to_all(send, 'blk', 0, 0, tiled=True), below, above)]
    scatter-add x10 -> x0, local copies, waits for them, and re-layouts: 37.2 us -> none  [the longest x2 22.7 us: lift_faces(): element_cube.at[..., :, -1, :].add(face_parts[..., 3, :, :, :])]
    all_to_all x0 -> x2, blocking collectives: none -> 35.3 us  [the longest x1 22.1 us: per_device(): sums = lax.all_to_all(sums, 'blk', 0, 0, tiled=True)]
    pallas_call x0 -> x9, Pallas kernels: none -> 18.4 us  [the longest x1 3.66 us: per_device(): pl.pallas_call(middle_kernel, out_shape=(shape(PAD, DOF),) + sent, in_spe...]
    dot_general x8 -> x0, matrix products: 17.4 us -> none  [the longest x3 5.66 us: precondition(): jnp.einsum('eij,ej->ei', jacobi_blocks[0], values_in.astype(jnp.bfloat16)...]
    unnamed x19 -> x38, local copies, waits for them, and re-layouts: 0.71 us -> 13.8 us
  transfers between devices with their start and end apart: 4 -> 9, of which waited for: 0 -> 3; matrix products, arithmetic and copies ran while one was open for 3% -> 3% of each run, Pallas kernels for 0% -> 3%
where the time goes in v1:
time: 144 us; the launch traced here: 142 us
  starting transfers between devices  56.9 us (40%)
  blocking collectives  35.3 us (25%)
  local copies, waits for them, and re-layouts  19.5 us (14%)
  Pallas kernels  18.4 us (13%)
  waiting for transfers between devices  8.65 us (6%)
  other arithmetic  2.7 us (2%)
    all_to_all x1, blocking collectives, per_device(): sums = lax.all_to_all(sums, 'blk', 0, 0, tiled=True)  22.1 us
    all_to_all x2, starting transfers between devices, exchange(): return (lax.all_to_all(send, 'blk', 0, 0, tiled=True), below, above)  16 us
    ppermute x2, starting transfers between devices, exchange(): lax.ppermute(down, 'reg', [((i + 1) % layers, i) for i in range(layers)])  14.7 us
    unnamed x38, local copies, waits for them, and re-layouts  13.8 us
    all_to_all x1, starting transfers between devices, per_device(): lax.all_to_all(own_slots, 'blk', 0, 0, axis_index_groups=member_groups, t...  13.7 us
    all_to_all x1, blocking collectives, per_device(): sums = lax.all_to_all(sums, 'reg', 0, 0, tiled=True)  13.1 us
    all_to_all x1, waiting for transfers between devices, per_device(): lax.all_to_all(own_rows, 'blk', 0, 0, axis_index_groups=column_groups, ti...  7.39 us
    all_to_all x1, starting transfers between devices, per_device(): lax.all_to_all(picked, 'blk', 0, 0, axis_index_groups=member_groups, tile...  5.32 us
  transfers between devices with their start and end apart: 9, of which 3 were waited for; matrix products, arithmetic and copies ran while one was open for 3% of the time, Pallas kernels for 3%

profile of v1, /device:TPU:1, one launch (start us, length us, event | category | flops | bytes accessed | tf_op | source)
XLA Modules:
  0.0 142.3 jit_solution(4714850827373089020)
XLA Ops:
  0.6 1.3 broadcast_in_dim.13
  2.0 13.7 %all-to-all-start = ((s32[8,1,6]{2,1,0:T(1,128)}), s32[8,1,6]{2,1,0:T(1,128)S(1)}, u32[]{:S(2)}, u32[]{:S(2)}) async-start(s32[8,1,6]{2,1,0:T(1,128)} %broadcast_in_dim.13), calls=%async_computation | async-start | bytes 8192 | tf_op jit(solution)/shard_map/all_to_all | solution.py:297
  19.1 1.1 all-to-all-done
  20.9 3.4 %all-to-all-start.1 = ((f32[8,1,3200]{2,1,0:T(1,128)}), f32[8,1,3200]{2,1,0:T(1,128)S(1)}, u32[]{:S(2)}, u32[]{:S(2)}) async-start(f32[8,1,3200]{2,1,0:T(1,128)} %broadcast_in_dim.15), calls=%async_computation.1 | async-start | bytes 204800 | tf_op jit(solution)/shard_map/all_to_all | solution.py:298
  24.3 7.4 %all-to-all-done.1.rows_ref = f32[8,1,3200]{2,1,0:T(1,128)S(1)} async-done(((f32[8,1,3200]{2,1,0:T(1,128)}), f32[8,1,3200]{2,1,0:T(1,128)S(1)}, u32[]{:S(2)}, u32[]{:S(2)}) %all-to-all-start.1) | async-done | bytes 102432 | tf_op jit(solution)/shard_map/all_to_all | solution.py:298
  32.3 2.3 %pick.1 = f32[8,1,2304]{2,1,0:T(1,128)} custom-call(s32[8,6]{1,0:T(8,128)} %bitcast.23, f32[8,1,3200]{2,1,0:T(1,128)} %copy-done.16), custom_call_target="tpu_custom_call" | custom-call | flops 1000 | bytes 131072 | tf_op jit(solution)/shard_map/pick/pallas_call | solution.py:315
  34.6 5.3 %all-to-all-start.2 = ((f32[8,1,2304]{2,1,0:T(1,128)}), f32[8,1,2304]{2,1,0:T(1,128)S(1)}, u32[]{:S(2)}, u32[]{:S(2)}) async-start(f32[8,1,2304]{2,1,0:T(1,128)} %pick.1), calls=%async_computation.2 | async-start | bytes 147456 | tf_op jit(solution)/shard_map/all_to_all | solution.py:323
  40.0 1.4 copy-done
  41.4 1.4 copy-done.7
  43.7 1.7 %prepare.1 = (bf16[6,480,320]{2,1,0:T(8,128)(2,1)S(1)}, bf16[36,80,80]{2,1,0:T(8,128)(2,1)S(1)}, bf16[36,80,80]{2,1,0:T(8,128)(2,1)S(1)}) custom-call(bf16[480,320]{1,0:T(8,128)(2,1)S(1)} %copy-done.9, bf16[6,320,320]{2,1,0:T(8,128)(2,1)S(1)} %bitcast.15, f32[36,80,80]{2,1,0:T(8,128)S(1)} %bitcast.20), custom_call_target="tpu_custom_call" | custom-call | flops 589824000 | bytes 6291456 | tf_op jit(solution)/shard_map/prepare/pallas_call | solution.py:301
  45.5 1.4 copy-done.4
  46.8 1.6 %copy-done.5 = bf16[6,480,320]{2,1,0:T(8,128)(2,1)S(1)} copy-done((bf16[6,480,320]{2,1,0:T(8,128)(2,1)S(1)}, bf16[6,480,320]{2,1,0:T(8,128)(2,1)}, u32[]{:S(2)}) %copy-start.5) | copy-done | bytes 1843224
  48.5 2.2 %first.1 = (f32[8,320]{1,0:T(8,128)S(1)}, f32[64,1,256]{2,1,0:T(1,128)}, f32[8,128]{1,0:T(8,128)S(1)}, f32[8,128]{1,0:T(8,128)S(1)}, f32[32,128]{1,0:T(8,128)S(1)}) custom-call(s32[1,6]{1,0:T(1,128)S(1)} %copy-done.15, f32[8,1,2304]{2,1,0:T(1,128)S(1)} %all-to-all-done.2.rows_ref, bf16[6,480,320]{2,1,0:T(8,128)(2,1)S(1)} %copy-done.5, ...), custom_call_target="tpu_custom_call" | custom-call | flops 29491200 | bytes 2097152 | tf_op jit(solution)/shard_map/first/pallas_call | solution.py:349
  50.7 5.4 %all-to-all-start.3 = ((f32[64,1,256]{2,1,0:T(1,128)}), f32[64,1,256]{2,1,0:T(1,128)S(1)}, u32[]{:S(2)}, u32[]{:S(2)}) async-start(f32[64,1,256]{2,1,0:T(1,128)} %get-tuple-element.24), calls=%async_computation.3 | async-start | bytes 131072 | tf_op jit(solution)/shard_map/all_to_all | solution.py:336
  56.2 1.9 %collective-permute-start = (f32[8,128]{1,0:T(8,128)S(1)}, f32[8,128]{1,0:T(8,128)S(1)}, u32[]{:S(2)}, u32[]{:S(2)}) collective-permute-start(f32[8,128]{1,0:T(8,128)S(1)} %get-tuple-element.25), channel_id=1, source_target_pairs={{0,64},{64,128},{128,192},{192,256},{256,320},{320,384},{384,448},... | collective-permute-start | bytes 12296 | tf_op jit(solution)/shard_map/ppermute | solution.py:334
  58.1 10.1 %collective-permute-start.1 = (f32[8,128]{1,0:T(8,128)S(1)}, f32[8,128]{1,0:T(8,128)S(1)}, u32[]{:S(2)}, u32[]{:S(2)}) collective-permute-start(f32[8,128]{1,0:T(8,128)S(1)} %get-tuple-element.26), channel_id=1, source_target_pairs={{64,0},{128,64},{192,128},{256,192},{320,256},{384,320},{448,384},... | collective-permute-start | bytes 12296 | tf_op jit(solution)/shard_map/ppermute | solution.py:335
  68.4 1.8 %copy-done.2 = f32[1,6,320,320]{3,2,1,0:T(8,128)S(1)} copy-done((f32[1,6,320,320]{3,2,1,0:T(8,128)S(1)}, f32[1,6,320,320]{3,2,1,0:T(8,128)}, u32[]{:S(2)}) %copy-start.2) | copy-done | bytes 2457624
  70.2 1.5 %own_part.2 = (f32[8,320]{1,0:T(8,128)S(1)}, f32[8,320]{1,0:T(8,128)S(1)}) custom-call(f32[8,320]{1,0:T(8,128)S(1)} %get-tuple-element.22.vector_ref.refs_11_.rhs_ref, bf16[6,320,320]{2,1,0:T(8,128)(2,1)S(1)} %bitcast.16, f32[6,320,320]{2,1,0:T(8,128)S(1)} %bitcast.18), custom_call_target="tpu_custom_call" | custom-call | flops 39321600 | bytes 4194304 | tf_op jit(solution)/shard_map/own_part/pallas_call | solution.py:339
  72.4 1.6 %copy-done.6 = bf16[6,480,320]{2,1,0:T(8,128)(2,1)S(1)} copy-done((bf16[6,480,320]{2,1,0:T(8,128)(2,1)S(1)}, bf16[6,480,320]{2,1,0:T(8,128)(2,1)}, u32[]{:S(2)}) %copy-start.6) | copy-done | bytes 1843224
  74.0 3.7 %middle.1 = (f32[8,320]{1,0:T(8,128)S(1)}, f32[64,1,256]{2,1,0:T(1,128)}, f32[8,128]{1,0:T(8,128)S(1)}, f32[8,128]{1,0:T(8,128)S(1)}, f32[32,128]{1,0:T(8,128)S(1)}) custom-call(f32[8,320]{1,0:T(8,128)S(1)} %get-tuple-element.23.refs_0_, f32[64,1,256]{2,1,0:T(1,128)S(1)} %all-to-all-done.3.refs_1_, f32[8,128]{1,0:T(8,128)S(1)} %collective-permute-done.refs_2_, ...), custom_call_target="tpu_custom_call" | custom-call | flops 58982400 | bytes 4194304 | tf_op jit(solution)/shard_map/middle/pallas_call | solution.py:362
  77.7 10.6 %all-to-all-start.4 = ((f32[64,1,256]{2,1,0:T(1,128)}), f32[64,1,256]{2,1,0:T(1,128)S(1)}, u32[]{:S(2)}, u32[]{:S(2)}) async-start(f32[64,1,256]{2,1,0:T(1,128)} %get-tuple-element.32), calls=%async_computation.4 | async-start | bytes 131072 | tf_op jit(solution)/shard_map/all_to_all | solution.py:336
  88.3 1.9 %collective-permute-start.2 = (f32[8,128]{1,0:T(8,128)S(1)}, f32[8,128]{1,0:T(8,128)S(1)}, u32[]{:S(2)}, u32[]{:S(2)}) collective-permute-start(f32[8,128]{1,0:T(8,128)S(1)} %get-tuple-element.33), channel_id=1, source_target_pairs={{0,64},{64,128},{128,192},{192,256},{256,320},{320,384},{384,448},... | collective-permute-start | bytes 12296 | tf_op jit(solution)/shard_map/ppermute | solution.py:334
  90.2 4.6 %collective-permute-start.3 = (f32[8,128]{1,0:T(8,128)S(1)}, f32[8,128]{1,0:T(8,128)S(1)}, u32[]{:S(2)}, u32[]{:S(2)}) collective-permute-start(f32[8,128]{1,0:T(8,128)S(1)} %get-tuple-element.34), channel_id=1, source_target_pairs={{64,0},{128,64},{192,128},{256,192},{320,256},{384,320},{448,384},... | collective-permute-start | bytes 12296 | tf_op jit(solution)/shard_map/ppermute | solution.py:335
  94.8 1.8 %copy-done.3 = f32[1,6,320,320]{3,2,1,0:T(8,128)S(1)} copy-done((f32[1,6,320,320]{3,2,1,0:T(8,128)S(1)}, f32[1,6,320,320]{3,2,1,0:T(8,128)}, u32[]{:S(2)}) %copy-start.3) | copy-done | bytes 2457624
  96.6 1.5 %own_part.3 = (f32[8,320]{1,0:T(8,128)S(1)}, f32[8,320]{1,0:T(8,128)S(1)}) custom-call(f32[8,320]{1,0:T(8,128)S(1)} %get-tuple-element.30.vector_ref.refs_12_.first_ref, bf16[6,320,320]{2,1,0:T(8,128)(2,1)S(1)} %bitcast.17, f32[6,320,320]{2,1,0:T(8,128)S(1)} %bitcast.19), custom_call_target="tpu_custom_call" | custom-call | flops 39321600 | bytes 4194304 | tf_op jit(solution)/shard_map/own_part/pallas_call | solution.py:339
  98.4 2.2 %last.1 = (f32[8,320]{1,0:T(8,128)S(1)}, f32[12,1,128]{2,1,0:T(1,128)S(1)}) custom-call(f32[8,320]{1,0:T(8,128)S(1)} %get-tuple-element.31.refs_0_, f32[64,1,256]{2,1,0:T(1,128)S(1)} %all-to-all-done.4.refs_1_, f32[8,128]{1,0:T(8,128)S(1)} %collective-permute-done.2.refs_2_, f32[8,128]{1,0:T(8,128)S(1)} %collective-permute-done.3.refs_3_, ...), custom_call_target="tpu_custom_call" | custom-call | flops 29491200 | bytes 2097152 | tf_op jit(solution)/shard_map/last/pallas_call | solution.py:374
  101.2 13.1 %all_to_all.35.parts_ref = f32[12,1,128]{2,1,0:T(1,128)} all-to-all(f32[12,1,128]{2,1,0:T(1,128)S(1)} %get-tuple-element.36), channel_id=1, replica_groups=mesh['reg'=12,'blk'=64] {'reg'}, dimensions={0} | all-to-all | bytes 12288 | tf_op jit(solution)/shard_map/all_to_all | solution.py:383
  114.3 1.3 spread.1
  115.7 22.1 %all_to_all.36.parts_ref = f32[64,1,128]{2,1,0:T(1,128)} all-to-all(f32[64,1,128]{2,1,0:T(1,128)} %spread.1), channel_id=1, replica_groups=mesh['reg'=12,'blk'=64] {'blk'}, dimensions={0} | all-to-all | bytes 65536 | tf_op jit(solution)/shard_map/all_to_all | solution.py:392
  137.8 1.9 %finish.1 = (f32[1,6,320]{2,1,0:T(8,128)}, f32[1,6,320]{2,1,0:T(8,128)}) custom-call(f32[64,1,128]{2,1,0:T(1,128)} %all_to_all.36.parts_ref, f32[8,320]{1,0:T(8,128)} %copy-done.10, f32[8,320]{1,0:T(8,128)} %copy-done.11, f32[8,320]{1,0:T(8,128)} %copy-done.14, f32[8,320]{1,0:T(8,128)} %copy-done.12, f32[8,320]{1,0:T(8,128)} %copy-done.13), custom_call_target="tpu_custom_call" | custom-call | flops 20000 | bytes 65536 | tf_op jit(solution)/shard_map/finish/pallas_call | solution.py:393
  139.7 1.3 copy.21
  141.0 1.3 copy.22
  (71 shorter events, 7.5 us)
Async XLA Ops:
  0.6 46.2 %copy-start.15 = (s32[1,6]{1,0:T(1,128)S(1)}, s32[1,6]{1,0:T(1,128)}, u32[]{:S(2)}) copy-start(s32[1,6]{1,0:T(1,128)} %slots_ref.1) | copy-start | bytes 76
  2.0 18.2 %all-to-all-start = ((s32[8,1,6]{2,1,0:T(1,128)}), s32[8,1,6]{2,1,0:T(1,128)S(1)}, u32[]{:S(2)}, u32[]{:S(2)}) async-start(s32[8,1,6]{2,1,0:T(1,128)} %broadcast_in_dim.13), calls=%async_computation | async-start | bytes 8192 | tf_op jit(solution)/shard_map/all_to_all | solution.py:297
  20.2 11.5 %copy-start.17 = (s32[8,1,6]{2,1,0:T(1,128)}, s32[8,1,6]{2,1,0:T(1,128)S(1)}, u32[]{:S(2)}) copy-start(s32[8,1,6]{2,1,0:T(1,128)S(1)} %all-to-all-done) | copy-start | bytes 580
  20.9 10.8 %all-to-all-start.1 = ((f32[8,1,3200]{2,1,0:T(1,128)}), f32[8,1,3200]{2,1,0:T(1,128)S(1)}, u32[]{:S(2)}, u32[]{:S(2)}) async-start(f32[8,1,3200]{2,1,0:T(1,128)} %broadcast_in_dim.15), calls=%async_computation.1 | async-start | bytes 204800 | tf_op jit(solution)/shard_map/all_to_all | solution.py:298
  31.7 0.6 copy-start.16
  34.6 12.2 %all-to-all-start.2 = ((f32[8,1,2304]{2,1,0:T(1,128)}), f32[8,1,2304]{2,1,0:T(1,128)S(1)}, u32[]{:S(2)}, u32[]{:S(2)}) async-start(f32[8,1,2304]{2,1,0:T(1,128)} %pick.1), calls=%async_computation.2 | async-start | bytes 147456 | tf_op jit(solution)/shard_map/all_to_all | solution.py:323
  40.0 1.4 copy-start
  41.4 1.4 copy-start.7
  42.7 1.0 copy-start.9
  43.7 24.4 %copy-start.18 = (s32[6,4]{0,1:T(4,128)S(1)}, s32[6,4]{0,1:T(4,128)}, u32[]{:S(2)}) copy-start(s32[6,4]{0,1:T(4,128)} %param.17) | copy-start | bytes 292
  43.7 24.6 %copy-start.1 = (bf16[1,6,320,320]{3,2,1,0:T(8,128)(2,1)S(1)}, bf16[1,6,320,320]{3,2,1,0:T(8,128)(2,1)}, u32[]{:S(2)}) copy-start(bf16[1,6,320,320]{3,2,1,0:T(8,128)(2,1)} %param.13) | copy-start | bytes 3686404
  45.4 1.4 copy-start.4
  46.8 1.6 %copy-start.5 = (bf16[6,480,320]{2,1,0:T(8,128)(2,1)S(1)}, bf16[6,480,320]{2,1,0:T(8,128)(2,1)}, u32[]{:S(2)}) copy-start(bf16[6,480,320]{2,1,0:T(8,128)(2,1)} %copy-done.4) | copy-start | bytes 5529604
  50.7 47.7 %copy-start.10 = (f32[8,320]{1,0:T(8,128)}, f32[8,320]{1,0:T(8,128)S(1)}, u32[]{:S(2)}) copy-start(f32[8,320]{1,0:T(8,128)S(1)} %get-tuple-element.22.vector_ref.refs_11_.rhs_ref) | copy-start | bytes 30724
  50.7 21.1 %all-to-all-start.3 = ((f32[64,1,256]{2,1,0:T(1,128)}), f32[64,1,256]{2,1,0:T(1,128)S(1)}, u32[]{:S(2)}, u32[]{:S(2)}) async-start(f32[64,1,256]{2,1,0:T(1,128)} %get-tuple-element.24), calls=%async_computation.3 | async-start | bytes 131072 | tf_op jit(solution)/shard_map/all_to_all | solution.py:336
  56.2 15.6 %collective-permute-start = (f32[8,128]{1,0:T(8,128)S(1)}, f32[8,128]{1,0:T(8,128)S(1)}, u32[]{:S(2)}, u32[]{:S(2)}) collective-permute-start(f32[8,128]{1,0:T(8,128)S(1)} %get-tuple-element.25), channel_id=1, source_target_pairs={{0,64},{64,128},{128,192},{192,256},{256,320},{320,384},{384,448},... | collective-permute-start | bytes 12296 | tf_op jit(solution)/shard_map/ppermute | solution.py:334
  58.1 13.7 %collective-permute-start.1 = (f32[8,128]{1,0:T(8,128)S(1)}, f32[8,128]{1,0:T(8,128)S(1)}, u32[]{:S(2)}, u32[]{:S(2)}) collective-permute-start(f32[8,128]{1,0:T(8,128)S(1)} %get-tuple-element.26), channel_id=1, source_target_pairs={{64,0},{128,64},{192,128},{256,192},{320,256},{384,320},{448,384},... | collective-permute-start | bytes 12296 | tf_op jit(solution)/shard_map/ppermute | solution.py:335
  68.4 1.8 %copy-start.2 = (f32[1,6,320,320]{3,2,1,0:T(8,128)S(1)}, f32[1,6,320,320]{3,2,1,0:T(8,128)}, u32[]{:S(2)}) copy-start(f32[1,6,320,320]{3,2,1,0:T(8,128)} %param.12) | copy-start | bytes 7372804
  70.2 2.2 %copy-start.8 = (bf16[6,80,320]{2,1,0:T(8,128)(2,1)S(1)}, bf16[6,80,320]{2,1,0:T(8,128)(2,1)}, u32[]{:S(2)}) copy-start(bf16[6,80,320]{2,1,0:T(8,128)(2,1)} %constant.64.clone.refs_10_) | copy-start | bytes 921604
  71.8 0.6 copy-start.12
  72.4 1.6 %copy-start.6 = (bf16[6,480,320]{2,1,0:T(8,128)(2,1)S(1)}, bf16[6,480,320]{2,1,0:T(8,128)(2,1)}, u32[]{:S(2)}) copy-start(bf16[6,480,320]{2,1,0:T(8,128)(2,1)} %copy-done.4) | copy-start | bytes 5529604
  77.7 20.7 %copy-start.11 = (f32[8,320]{1,0:T(8,128)}, f32[8,320]{1,0:T(8,128)S(1)}, u32[]{:S(2)}) copy-start(f32[8,320]{1,0:T(8,128)S(1)} %get-tuple-element.30.vector_ref.refs_12_.first_ref) | copy-start | bytes 30724
  77.7 20.7 %all-to-all-start.4 = ((f32[64,1,256]{2,1,0:T(1,128)}), f32[64,1,256]{2,1,0:T(1,128)S(1)}, u32[]{:S(2)}, u32[]{:S(2)}) async-start(f32[64,1,256]{2,1,0:T(1,128)} %get-tuple-element.32), calls=%async_computation.4 | async-start | bytes 131072 | tf_op jit(solution)/shard_map/all_to_all | solution.py:336
  88.3 9.9 %collective-permute-start.2 = (f32[8,128]{1,0:T(8,128)S(1)}, f32[8,128]{1,0:T(8,128)S(1)}, u32[]{:S(2)}, u32[]{:S(2)}) collective-permute-start(f32[8,128]{1,0:T(8,128)S(1)} %get-tuple-element.33), channel_id=1, source_target_pairs={{0,64},{64,128},{128,192},{192,256},{256,320},{320,384},{384,448},... | collective-permute-start | bytes 12296 | tf_op jit(solution)/shard_map/ppermute | solution.py:334
  90.2 8.0 %collective-permute-start.3 = (f32[8,128]{1,0:T(8,128)S(1)}, f32[8,128]{1,0:T(8,128)S(1)}, u32[]{:S(2)}, u32[]{:S(2)}) collective-permute-start(f32[8,128]{1,0:T(8,128)S(1)} %get-tuple-element.34), channel_id=1, source_target_pairs={{64,0},{128,64},{192,128},{256,192},{320,256},{384,320},{448,384},... | collective-permute-start | bytes 12296 | tf_op jit(solution)/shard_map/ppermute | solution.py:335
  94.8 1.8 %copy-start.3 = (f32[1,6,320,320]{3,2,1,0:T(8,128)S(1)}, f32[1,6,320,320]{3,2,1,0:T(8,128)}, u32[]{:S(2)}) copy-start(f32[1,6,320,320]{3,2,1,0:T(8,128)} %param.12) | copy-start | bytes 7372804
  98.1 39.7 %copy-start.13 = (f32[8,320]{1,0:T(8,128)}, f32[8,320]{1,0:T(8,128)S(1)}, u32[]{:S(2)}) copy-start(f32[8,320]{1,0:T(8,128)S(1)} %get-tuple-element.39.full1_ref) | copy-start | bytes 30724
  100.6 0.6 copy-start.14

commit v2 on v1

v2 whole, which is shorter than its diff:
```python
import jax
import jax.numpy as jnp
import numpy as np
from jax import lax
from jax.experimental import pallas as pl
from jax.experimental.pallas import tpu as pltpu
from jax.sharding import PartitionSpec as P

NVAR = 5
NQ = 4
DOF = NVAR * NQ**3
FDOF = NVAR * NQ**2
ELEMS = 6
PAD = 8
SLOTS = 10
PER_PAIR = 3
WIDTH = 256
F32 = jnp.float32
BF16 = jnp.bfloat16


def face_index():
    cube = np.arange(DOF).reshape(NVAR, NQ, NQ, NQ)
    faces = (cube[:, 0], cube[:, -1], cube[:, :, 0], cube[:, :, -1], cube[..., 0], cube[..., -1])
    return np.stack([one.reshape(-1) for one in faces])


def trace_matrix():
    return (face_index()[:, :, None] == np.arange(DOF)[None, None, :]).astype(np.float32)


def params(megabytes):
    return pltpu.CompilerParams(vmem_limit_bytes=megabytes * 2**20)


def cost(flops, moved):
    return pl.CostEstimate(flops=flops, bytes_accessed=moved, transcendentals=0)


def vmem(count):
    return [pl.BlockSpec(memory_space=pltpu.VMEM)] * count


def anywhere(count):
    return [pl.BlockSpec(memory_space=pl.ANY)] * count


def in_hbm(array):
    return pltpu.with_memory_space_constraint(array, pltpu.HBM)


def smem():
    return pl.BlockSpec(memory_space=pltpu.SMEM)


def mul_t(rows, matrix):
    return lax.dot_general(rows, matrix, (((1,), (1,)), ((), ())), preferred_element_type=F32)


def mul(left, right):
    return lax.dot_general(left, right, (((1,), (0,)), ((), ())), preferred_element_type=F32)


def two_parts(values):
    high = values.astype(BF16)
    low = (values - high.astype(F32)).astype(BF16)
    return high, low


def stacked_parts(values):
    high = values.astype(BF16).astype(F32)
    return jnp.concatenate([high, values - high], axis=0).astype(BF16)


def own_row(result, element):
    row = lax.broadcasted_iota(jnp.int32, result[:PAD].shape, 0)
    return jnp.where(row == element, result[:PAD] + result[PAD:], 0.0)


def high_row(result, element):
    row = lax.broadcasted_iota(jnp.int32, result[:PAD].shape, 0)
    return jnp.where(row == element, result[:PAD], 0.0)


def precondition(vector, jacobi_ref, arrive):
    parts = stacked_parts(vector)
    rounded = jnp.zeros((PAD, DOF), F32)
    full = jnp.zeros((PAD, DOF), F32)
    for element in range(ELEMS):
        arrive(element)
        result = mul_t(parts, jacobi_ref[element])
        rounded = rounded + high_row(result, element)
        full = full + own_row(result, element)
    return rounded, full


def send_traces(values, select_ref, pack_ref, send_ref, up_ref, down_ref, local_ref):
    both = mul(stacked_parts(values), select_ref[...])
    traces = both[:PAD] + both[PAD:]
    traces = [traces[:, 128 * face : 128 * (face + 1)] for face in range(6)]
    down_ref[...] = traces[4]
    up_ref[...] = traces[5]
    sides = jnp.concatenate(traces[:4], axis=0)
    local_ref[...] = sides
    sides = jnp.concatenate([sides, jnp.zeros((4 * PAD, WIDTH - 128), F32)], axis=1)
    spread = jnp.concatenate(
        [sides] + [pltpu.roll(sides, FDOF * place, 1) for place in range(1, PER_PAIR)], axis=0
    )
    high, low = two_parts(spread)
    send_ref[:, 0, :] = mul(pack_ref[...], high) + mul(pack_ref[...], low)


def repeat_kernel(rows_ref, out_ref):
    for chip in range(out_ref.shape[0] // SLOTS):
        out_ref[chip * SLOTS : (chip + 1) * SLOTS] = rows_ref[...]


def first_kernel(
    place_ref, same_ref, other_ref, jacobi_ref, select_ref, pack_ref,
    rhs_ref, values_ref, full_ref, send_ref, up_ref, down_ref, local_ref,
):
    rhs_ref[...] = jnp.zeros(rhs_ref.shape, F32)
    for element in range(ELEMS):
        place = place_ref[0, element]
        rhs_ref[element : element + 1, :] = jnp.where(
            place_ref[1, element] == 1, other_ref[place], same_ref[place]
        )
    rounded, full = precondition(rhs_ref[...], jacobi_ref, lambda element: None)
    values_ref[...] = rounded
    full_ref[...] = full
    send_traces(rounded, select_ref, pack_ref, send_ref, up_ref, down_ref, local_ref)


def fetch(source_ref, target_ref, semaphores, width):
    copies = [
        pltpu.make_async_copy(
            source_ref.at[pl.ds(element * width, width)],
            target_ref.at[pl.ds(element * width, width)],
            semaphores.at[element],
        )
        for element in range(ELEMS)
    ]
    for copy in copies:
        copy.start()
    return lambda element: copies[element].wait()


def diagonal_kernel(values_ref, diagonal_ref, product_ref, held_ref, semaphores):
    arrive = fetch(diagonal_ref, held_ref, semaphores, 1)
    parts = stacked_parts(values_ref[...])
    total = jnp.zeros((PAD, DOF), F32)
    for element in range(ELEMS):
        arrive(element)
        high, low = two_parts(held_ref[element])
        total = total + own_row(mul_t(parts, high) + mul_t(parts, low), element)
    product_ref[...] = total


def add_neighbors(
    product_ref, recv_ref, below_ref, above_ref, local_ref, turn_ref, unpack_ref, here_ref, lift_ref,
    coupling_ref, arrive,
):
    high, low = two_parts(recv_ref[:, 0, :])
    arrived = mul(unpack_ref[...], high) + mul(unpack_ref[...], low)
    count = 4 * PAD
    sides = arrived[:count, :128]
    for place in range(1, PER_PAIR):
        rows = arrived[place * count : (place + 1) * count]
        sides = sides + pltpu.roll(rows, WIDTH - FDOF * place, 1)[:, :128]
    high, low = two_parts(local_ref[...])
    sides = sides + mul(here_ref[...], high) + mul(here_ref[...], low)
    lane = lax.broadcasted_iota(jnp.int32, sides.shape, 1)
    step = (lane // 4) % 4
    turned = jnp.where(
        step == 0,
        pltpu.roll(sides, 128 - 12, 1),
        jnp.where(
            step == 1,
            pltpu.roll(sides, 128 - 4, 1),
            jnp.where(step == 2, pltpu.roll(sides, 4, 1), pltpu.roll(sides, 12, 1)),
        ),
    )
    sides = jnp.where(turn_ref[...] == 1, turned, sides)
    traces = [sides[face * PAD : (face + 1) * PAD] for face in range(4)] + [below_ref[...], above_ref[...]]
    parts = [stacked_parts(one[:, :FDOF]) for one in traces]
    terms = [jnp.zeros((PAD, FDOF), F32)] * 6
    for element in range(ELEMS):
        arrive(element)
        for face in range(6):
            high, low = two_parts(coupling_ref[element * 6 + face])
            terms[face] = terms[face] + own_row(mul_t(parts[face], high) + mul_t(parts[face], low), element)
    total = product_ref[...]
    for face in range(6):
        lifted = mul(stacked_parts(terms[face]), lift_ref[face])
        total = total + lifted[:PAD] + lifted[PAD:]
    return total


def middle_kernel(
    product_ref, recv_ref, below_ref, above_ref, local_ref, turn_ref, unpack_ref, here_ref, lift_ref,
    select_ref, pack_ref, coupling_ref, jacobi_ref,
    vector_ref, values_ref, full_ref, send_ref, up_ref, down_ref, new_local_ref,
    held_coupling_ref, held_jacobi_ref, coupling_semaphores, jacobi_semaphores,
):
    coupling_arrive = fetch(coupling_ref, held_coupling_ref, coupling_semaphores, 6)
    jacobi_arrive = fetch(jacobi_ref, held_jacobi_ref, jacobi_semaphores, 1)
    vector = add_neighbors(
        product_ref, recv_ref, below_ref, above_ref, local_ref, turn_ref, unpack_ref, here_ref, lift_ref,
        held_coupling_ref, coupling_arrive,
    )
    vector_ref[...] = vector
    rounded, full = precondition(vector, held_jacobi_ref, jacobi_arrive)
    values_ref[...] = rounded
    full_ref[...] = full
    send_traces(rounded, select_ref, pack_ref, send_ref, up_ref, down_ref, new_local_ref)


def last_kernel(
    product_ref, recv_ref, below_ref, above_ref, local_ref, turn_ref, unpack_ref, here_ref, lift_ref,
    rhs_ref, first_ref, coupling_ref,
    vector_ref, sums_ref,
    held_coupling_ref, coupling_semaphores,
):
    arrive = fetch(coupling_ref, held_coupling_ref, coupling_semaphores, 6)
    second = add_neighbors(
        product_ref, recv_ref, below_ref, above_ref, local_ref, turn_ref, unpack_ref, here_ref, lift_ref,
        held_coupling_ref, arrive,
    )
    vector_ref[...] = second
    first, rhs = first_ref[...], rhs_ref[...]
    lane = lax.broadcasted_iota(jnp.int32, (1, 128), 1)
    sums = jnp.zeros((1, 128), F32)
    pairs = ((first, first), (first, second), (second, second), (first, rhs), (second, rhs))
    for place, (one, other) in enumerate(pairs):
        sums = jnp.where(lane == place, jnp.sum(one * other), sums)
    for copy in range(sums_ref.shape[0]):
        sums_ref[copy] = sums


def spread_kernel(parts_ref, sums_ref):
    total = parts_ref[0]
    for part in range(1, parts_ref.shape[0]):
        total = total + parts_ref[part]
    for copy in range(sums_ref.shape[0]):
        sums_ref[copy] = total


def finish_kernel(parts_ref, rhs_ref, first_ref, second_ref, full0_ref, full1_ref, solution_ref, residual_ref):
    totals = [parts_ref[part] for part in range(parts_ref.shape[0])]
    while len(totals) > 1:
        totals = [one + other for one, other in zip(totals[::2], totals[1::2])] + totals[len(totals) // 2 * 2 :]
    g11, g12, g22, t1, t2 = (totals[0][:, place : place + 1] for place in range(5))
    factor = g12 / g11
    weight2 = (t2 - factor * t1) / (g22 - factor * g12)
    weight1 = (t1 - g12 * weight2) / g11
    answer = weight1 * full0_ref[...] + weight2 * full1_ref[...]
    remaining = rhs_ref[...] - weight1 * first_ref[...] - weight2 * second_ref[...]
    for element in range(ELEMS):
        solution_ref[element] = answer[element : element + 1]
        residual_ref[element] = remaining[element : element + 1]


def shape(*dims, dtype=F32):
    return jax.ShapeDtypeStruct(dims, dtype)


def routes(neighbor, neighbor_face, orientation, devices):
    def sides(table, fill):
        padded = jnp.pad(table.T, ((0, 0), (0, PAD - ELEMS)), constant_values=fill)
        return padded.reshape(-1)

    own = lax.axis_index("blk").astype(jnp.int32)
    near = sides(neighbor, -ELEMS)
    face = sides(neighbor_face, 0)
    turn = sides(orientation, 0)
    count = 4 * PAD
    row = jnp.arange(count, dtype=jnp.int32)
    owner = near // ELEMS
    remote = (owner != own) & (near >= 0)
    local = owner == own
    same = owner[:, None] == owner[None, :]
    own_key = row % PAD * 4 + row // PAD
    near_key = near * 4 + face
    send_place = jnp.sum(same & (own_key[None, :] < own_key[:, None]), axis=1)
    near_place = jnp.sum(same & (near_key[None, :] < near_key[:, None]), axis=1)
    device = jnp.arange(devices, dtype=jnp.int32)
    place = jnp.arange(PER_PAIR, dtype=jnp.int32)
    to = (device[:, None] == owner[None, :]) & remote[None, :]
    pack = to[:, None, :] & (place[None, :, None] == send_place[None, None, :])
    unpack = to.T[None] & (place[:, None, None] == near_place[None, :, None])
    here = local[:, None] & (row[None, :] == (face * PAD + near % ELEMS)[:, None])
    return (
        pack.reshape(devices, PER_PAIR * count).astype(BF16),
        unpack.reshape(PER_PAIR * count, devices).astype(BF16),
        here.astype(BF16),
        jnp.broadcast_to(turn[:, None], (count, 128)),
    )


def per_device(
    assembly_rhs, source_slot, diagonal_blocks, jacobi_blocks, coupling, neighbor, neighbor_face, orientation
):
    devices, layers = lax.axis_size("blk"), lax.axis_size("reg")
    chips = devices // 2
    select = trace_matrix()
    wide = np.zeros((6, 128, DOF), np.float32)
    wide[:, :FDOF] = select
    wide = jnp.asarray(wide.reshape(6 * 128, DOF).T, BF16)
    lift = jnp.asarray(select, BF16)
    diagonal, jacobi = diagonal_blocks[0], jacobi_blocks[0]
    coupling = coupling.reshape(6 * ELEMS, FDOF, FDOF)

    rows = jnp.transpose(assembly_rhs, (1, 0, 2))
    rows = pl.pallas_call(
        repeat_kernel,
        out_shape=shape(chips * SLOTS, 1, DOF),
        in_specs=vmem(1),
        out_specs=vmem(1)[0],
        compiler_params=params(8),
        cost_estimate=cost(1000, 2**19),
        name="repeat",
    )(rows)
    same_core = [[2 * chip + core for chip in range(chips)] for core in range(2)]
    same = lax.all_to_all(rows, "blk", 0, 0, axis_index_groups=same_core, tiled=True)
    other = lax.ppermute(same, "blk", [(device, device ^ 1) for device in range(devices)])

    owner = source_slot // SLOTS
    place = owner // 2 * SLOTS + source_slot % SLOTS
    crossed = (owner % 2 != lax.axis_index("blk") % 2).astype(jnp.int32)
    place = jnp.concatenate([place, crossed], axis=0)
    pack, unpack, here, turn = routes(neighbor, neighbor_face, orientation, devices)

    vector = shape(PAD, DOF)
    sent = (shape(devices, 1, WIDTH), shape(PAD, 128), shape(PAD, 128), shape(4 * PAD, 128))

    def exchange(send, up, down):
        below = lax.ppermute(up, "reg", [(i, (i + 1) % layers) for i in range(layers)])
        above = lax.ppermute(down, "reg", [((i + 1) % layers, i) for i in range(layers)])
        return lax.all_to_all(send, "blk", 0, 0, tiled=True), below, above

    def diagonal_part(values):
        return pl.pallas_call(
            diagonal_kernel,
            out_shape=vector,
            in_specs=vmem(1) + anywhere(1),
            out_specs=vmem(1)[0],
            scratch_shapes=[pltpu.VMEM((ELEMS, DOF, DOF), F32), pltpu.SemaphoreType.DMA((ELEMS,))],
            compiler_params=params(16),
            cost_estimate=cost(6 * 4 * 16 * 320 * 320, 4 * 2**20),
            name="diagonal_part",
        )(values, in_hbm(diagonal))

    rhs, values, full0, send, up, down, local = pl.pallas_call(
        first_kernel,
        out_shape=(vector,) * 3 + sent,
        in_specs=[smem()] + vmem(5),
        out_specs=tuple(vmem(7)),
        compiler_params=params(16),
        cost_estimate=cost(6 * 2 * 16 * 480 * 320, 2**21),
        name="first",
    )(place, same, other, jacobi, wide, pack)
    recv, below, above = exchange(send, up, down)
    product = diagonal_part(values)

    first, values, full1, send, up, down, local1 = pl.pallas_call(
        middle_kernel,
        out_shape=(vector,) * 3 + sent,
        in_specs=vmem(11) + anywhere(2),
        out_specs=tuple(vmem(7)),
        scratch_shapes=[
            pltpu.VMEM((6 * ELEMS, FDOF, FDOF), F32),
            pltpu.VMEM((ELEMS, DOF, DOF), BF16),
            pltpu.SemaphoreType.DMA((ELEMS,)),
            pltpu.SemaphoreType.DMA((ELEMS,)),
        ],
        compiler_params=params(16),
        cost_estimate=cost(6 * 4 * 16 * 480 * 320, 4 * 2**20),
        name="middle",
    )(product, recv, below, above, local, turn, unpack, here, lift, wide, pack, in_hbm(coupling), in_hbm(jacobi))
    recv, below, above = exchange(send, up, down)
    product = diagonal_part(values)

    second, sums = pl.pallas_call(
        last_kernel,
        out_shape=(vector, shape(layers, 1, 128)),
        in_specs=vmem(11) + anywhere(1),
        out_specs=tuple(vmem(2)),
        scratch_shapes=[
            pltpu.VMEM((6 * ELEMS, FDOF, FDOF), F32),
            pltpu.SemaphoreType.DMA((ELEMS,)),
        ],
        compiler_params=params(16),
        cost_estimate=cost(6 * 2 * 16 * 480 * 320, 2**21),
        name="last",
    )(product, recv, below, above, local1, turn, unpack, here, lift, rhs, first, in_hbm(coupling))
    sums = lax.all_to_all(sums, "reg", 0, 0, tiled=True)
    sums = pl.pallas_call(
        spread_kernel,
        out_shape=shape(devices, 1, 128),
        in_specs=vmem(1),
        out_specs=vmem(1)[0],
        compiler_params=params(8),
        cost_estimate=cost(2000, 2**15),
        name="spread",
    )(sums)
    sums = lax.all_to_all(sums, "blk", 0, 0, tiled=True)
    answer, remaining = pl.pallas_call(
        finish_kernel,
        out_shape=(shape(ELEMS, 1, DOF), shape(ELEMS, 1, DOF)),
        in_specs=vmem(6),
        out_specs=tuple(vmem(2)),
        compiler_params=params(8),
        cost_estimate=cost(20000, 2**16),
        name="finish",
    )(sums, rhs, first, second, full0, full1)
    return jnp.transpose(answer, (1, 0, 2)), jnp.transpose(remaining, (1, 0, 2))


def solution(mesh):
    placed = (
        P("reg", "blk", None),
        P("reg", "blk"),
        P("reg", "blk", None, None),
        P("reg", "blk", None, None),
        P("reg", "blk", None, None, None),
        P("blk", None),
        P("blk", None),
        P("blk", None),
    )
    return jax.shard_map(
        per_device,
        mesh=mesh,
        in_specs=placed,
        out_specs=(P("reg", "blk", None), P("reg", "blk", None)),
        check_vma=False,
    )
```

time: 144 us -> 128 us (0.89)
  local copies, waits for them, and re-layouts: 19.5 us -> 2.91 us
  waiting for transfers between devices: 8.65 us -> 12.7 us
  other arithmetic: 2.7 us -> 0.61 us
    unnamed x38 -> x18, local copies, waits for them, and re-layouts: 13.8 us -> 1.88 us
    all_to_all x3 -> x1, starting transfers between devices: 22.4 us -> 10.5 us  [per_device(): lax.all_to_all(rows, 'blk', 0, 0, axis_index_groups=same_core, tiled=True)]
    ppermute x0 -> x1, starting transfers between devices: none -> 7.96 us  [per_device(): lax.ppermute(same, 'blk', [(device, device ^ 1) for device in range(devic...]
    pallas_call x2 -> x0, local copies, waits for them, and re-layouts: 2.63 us -> none  [per_device(): pl.pallas_call(finish_kernel, out_shape=(shape(1, ELEMS, DOF), shape(1, E...]
    all_to_all x3 -> x1, waiting for transfers between devices: 8.44 us -> 11 us  [per_device(): lax.all_to_all(rows, 'blk', 0, 0, axis_index_groups=same_core, tiled=True)]
    ppermute x2, starting transfers between devices: 14.7 us -> 16.8 us  [exchange(): lax.ppermute(down, 'reg', [((i + 1) % layers, i) for i in range(layers)])]
    ppermute x2, starting transfers between devices: 3.83 us -> 5.91 us  [exchange(): lax.ppermute(up, 'reg', [(i, (i + 1) % layers) for i in range(layers)])]
    broadcast_in_dim x3 -> x0, local copies, waits for them, and re-layouts: 2.08 us -> none  [the longest x1 1.31 us: per_device(): own_slots = jnp.broadcast_to(source_slot[:, None, :], (members, 1, ELEMS))]
  transfers between devices with their start and end apart: 9 -> 8, of which waited for: 3 -> 3; matrix products, arithmetic and copies ran while one was open for 3% -> 1% of each run, Pallas kernels for 3% -> 5%
where the time goes in v2:
time: 128 us
  starting transfers between devices  56.4 us (44%)
  blocking collectives  35.1 us (27%)
  Pallas kernels  18.9 us (15%)
  waiting for transfers between devices  12.7 us (10%)
  local copies, waits for them, and re-layouts  2.91 us (2%)
    all_to_all x1, blocking collectives, per_device(): sums = lax.all_to_all(sums, 'blk', 0, 0, tiled=True)  21.5 us
    ppermute x2, starting transfers between devices, exchange(): lax.ppermute(down, 'reg', [((i + 1) % layers, i) for i in range(layers)])  16.8 us
    all_to_all x2, starting transfers between devices, exchange(): return (lax.all_to_all(send, 'blk', 0, 0, tiled=True), below, above)  15.3 us
    all_to_all x1, blocking collectives, per_device(): sums = lax.all_to_all(sums, 'reg', 0, 0, tiled=True)  13.5 us
    all_to_all x1, waiting for transfers between devices, per_device(): lax.all_to_all(rows, 'blk', 0, 0, axis_index_groups=same_core, tiled=True)  11 us
    all_to_all x1, starting transfers between devices, per_device(): lax.all_to_all(rows, 'blk', 0, 0, axis_index_groups=same_core, tiled=True)  10.5 us
    ppermute x1, starting transfers between devices, per_device(): lax.ppermute(same, 'blk', [(device, device ^ 1) for device in range(devic...  7.96 us
    pallas_call x2, Pallas kernels, diagonal_part(): pl.pallas_call(diagonal_kernel, out_shape=vector, in_specs=vmem(1) + anyw...  6.69 us
  transfers between devices with their start and end apart: 8, of which 3 were waited for; matrix products, arithmetic and copies ran while one was open for 1% of the time, Pallas kernels for 5%

profile of v2, /device:TPU:1, one launch (start us, length us, event | category | flops | bytes accessed | tf_op | source)
XLA Modules:
  0.0 127.6 jit_solution(8266413743062618852)
XLA Ops:
  0.7 0.8 copy-done.4
  1.5 0.9 repeat.1
  2.4 10.5 %all-to-all-start = ((f32[320,1,320]{2,1,0:T(1,128)}), f32[320,1,320]{2,1,0:T(1,128)S(1)}, u32[]{:S(2)}, u32[]{:S(2)}) async-start(f32[320,1,320]{2,1,0:T(1,128)} %repeat.1), calls=%async_computation | async-start | bytes 983040 | tf_op jit(solution)/shard_map/all_to_all | solution.py:324
  13.0 0.1 rem.109
  13.1 0.1 div.48
  13.1 0.1 ne.167
  13.3 0.1 ge.12
  13.5 0.2 convert_reduce_fusion
  13.8 0.1 eq.129
  13.9 0.1 eq.118
  14.0 0.1 copy.13
  14.1 0.1 mul.41
  14.3 11.0 %all-to-all-done.same_ref = f32[320,1,320]{2,1,0:T(1,128)S(1)} async-done(((f32[320,1,320]{2,1,0:T(1,128)}), f32[320,1,320]{2,1,0:T(1,128)S(1)}, u32[]{:S(2)}, u32[]{:S(2)}) %all-to-all-start) | async-done | bytes 409632 | tf_op jit(solution)/shard_map/all_to_all | solution.py:324
  25.3 8.0 %collective-permute-start = (f32[320,1,320]{2,1,0:T(1,128)S(1)}, f32[320,1,320]{2,1,0:T(1,128)S(1)}, u32[]{:S(2)}, u32[]{:S(2)}) collective-permute-start(f32[320,1,320]{2,1,0:T(1,128)S(1)} %all-to-all-done.same_ref), channel_id=1, source_target_pairs={{0,1},{1,0},{2,3},{3,2},{4,5},{5,4},{6,7},{7,6},{8,9},{9,8},{10,11... | collective-permute-start | bytes 1228808 | tf_op jit(solution)/shard_map/ppermute | solution.py:325
  33.3 1.4 %collective-permute-done.other_ref = f32[320,1,320]{2,1,0:T(1,128)S(1)} collective-permute-done((f32[320,1,320]{2,1,0:T(1,128)S(1)}, f32[320,1,320]{2,1,0:T(1,128)S(1)}, u32[]{:S(2)}, u32[]{:S(2)}) %collective-permute-start) | collective-permute-done | bytes 409632 | tf_op jit(solution)/shard_map/ppermute | solution.py:325
  34.8 1.0 copy-done.1
  35.8 2.1 %first.1 = (f32[8,320]{1,0:T(8,128)S(1)}, f32[8,320]{1,0:T(8,128)S(1)}, f32[8,320]{1,0:T(8,128)S(1)}, f32[64,1,256]{2,1,0:T(1,128)}, f32[8,128]{1,0:T(8,128)S(1)...) custom-call(s32[2,6]{1,0:T(2,128)S(1)} %pad_add_fusion.place_ref, f32[320,1,320]{2,1,0:T(1,128)S(1)} %all-to-all-done.same_ref, ...), custom_call_target="tpu_custom_call" | custom-call | flops 29491200 | bytes 2097152 | tf_op jit(solution)/shard_map/first/pallas_call | solution.py:353
  37.9 4.7 %all-to-all-start.1 = ((f32[64,1,256]{2,1,0:T(1,128)}), f32[64,1,256]{2,1,0:T(1,128)S(1)}, u32[]{:S(2)}, u32[]{:S(2)}) async-start(f32[64,1,256]{2,1,0:T(1,128)} %get-tuple-element.21), calls=%async_computation.1 | async-start | bytes 131072 | tf_op jit(solution)/shard_map/all_to_all | solution.py:339
  42.6 4.0 %collective-permute-start.1 = (f32[8,128]{1,0:T(8,128)S(1)}, f32[8,128]{1,0:T(8,128)S(1)}, u32[]{:S(2)}, u32[]{:S(2)}) collective-permute-start(f32[8,128]{1,0:T(8,128)S(1)} %get-tuple-element.22), channel_id=1, source_target_pairs={{0,64},{64,128},{128,192},{192,256},{256,320},{320,384},{384,448},... | collective-permute-start | bytes 12296 | tf_op jit(solution)/shard_map/ppermute | solution.py:337
  46.6 12.2 %collective-permute-start.2 = (f32[8,128]{1,0:T(8,128)S(1)}, f32[8,128]{1,0:T(8,128)S(1)}, u32[]{:S(2)}, u32[]{:S(2)}) collective-permute-start(f32[8,128]{1,0:T(8,128)S(1)} %get-tuple-element.23), channel_id=1, source_target_pairs={{64,0},{128,64},{192,128},{256,192},{320,256},{384,320},{448,384},... | collective-permute-start | bytes 12296 | tf_op jit(solution)/shard_map/ppermute | solution.py:338
  58.9 0.1 broadcast_in_dim.4
  59.1 3.4 %diagonal_part.2.product_ref = f32[8,320]{1,0:T(8,128)S(1)} custom-call(f32[8,320]{1,0:T(8,128)S(1)} %get-tuple-element.20.values_ref, f32[6,320,320]{2,1,0:T(8,128)} %bitcast.19), custom_call_target="tpu_custom_call" | custom-call | flops 39321600 | bytes 4194304 | tf_op jit(solution)/shard_map/diagonal_part/pallas_call | solution.py:342
  62.6 5.4 %middle.1 = (f32[8,320]{1,0:T(8,128)S(1)}, f32[8,320]{1,0:T(8,128)S(1)}, f32[8,320]{1,0:T(8,128)S(1)}, f32[64,1,256]{2,1,0:T(1,128)}, f32[8,128]{1,0:T(8,128)S(1...) custom-call(f32[8,320]{1,0:T(8,128)S(1)} %diagonal_part.2.product_ref, f32[64,1,256]{2,1,0:T(1,128)S(1)} %all-to-all-done.1.recv_ref, ...), custom_call_target="tpu_custom_call" | custom-call | flops 58982400 | bytes 4194304 | tf_op jit(solution)/shard_map/middle/pallas_call | solution.py:365
  68.0 10.6 %all-to-all-start.2 = ((f32[64,1,256]{2,1,0:T(1,128)}), f32[64,1,256]{2,1,0:T(1,128)S(1)}, u32[]{:S(2)}, u32[]{:S(2)}) async-start(f32[64,1,256]{2,1,0:T(1,128)} %get-tuple-element.26), calls=%async_computation.2 | async-start | bytes 131072 | tf_op jit(solution)/shard_map/all_to_all | solution.py:339
  78.6 1.9 %collective-permute-start.3 = (f32[8,128]{1,0:T(8,128)S(1)}, f32[8,128]{1,0:T(8,128)S(1)}, u32[]{:S(2)}, u32[]{:S(2)}) collective-permute-start(f32[8,128]{1,0:T(8,128)S(1)} %get-tuple-element.27), channel_id=1, source_target_pairs={{0,64},{64,128},{128,192},{192,256},{256,320},{320,384},{384,448},... | collective-permute-start | bytes 12296 | tf_op jit(solution)/shard_map/ppermute | solution.py:337
  80.5 4.6 %collective-permute-start.4 = (f32[8,128]{1,0:T(8,128)S(1)}, f32[8,128]{1,0:T(8,128)S(1)}, u32[]{:S(2)}, u32[]{:S(2)}) collective-permute-start(f32[8,128]{1,0:T(8,128)S(1)} %get-tuple-element.28), channel_id=1, source_target_pairs={{64,0},{128,64},{192,128},{256,192},{320,256},{384,320},{448,384},... | collective-permute-start | bytes 12296 | tf_op jit(solution)/shard_map/ppermute | solution.py:338
  85.1 3.3 %diagonal_part.3.product_ref = f32[8,320]{1,0:T(8,128)S(1)} custom-call(f32[8,320]{1,0:T(8,128)S(1)} %get-tuple-element.25.values_ref, f32[6,320,320]{2,1,0:T(8,128)} %bitcast.20), custom_call_target="tpu_custom_call" | custom-call | flops 39321600 | bytes 4194304 | tf_op jit(solution)/shard_map/diagonal_part/pallas_call | solution.py:342
  88.4 0.2 all-to-all-done.2.recv_ref
  88.7 2.8 %last.1 = (f32[8,320]{1,0:T(8,128)S(1)}, f32[12,1,128]{2,1,0:T(1,128)S(1)}) custom-call(f32[8,320]{1,0:T(8,128)S(1)} %diagonal_part.3.product_ref, f32[64,1,256]{2,1,0:T(1,128)S(1)} %all-to-all-done.2.recv_ref, f32[8,128]{1,0:T(8,128)S(1)} %collective-permute-done.3.below_ref, f32[8,128]{1,0:T(8,128)S(1)} %collective-permute-done.4.above_ref, ...), custom_call_target="tpu_custom_call" | custom-call | flops 29491200 | bytes 2097152 | tf_op jit(solution)/shard_map/last/pallas_call | solution.py:383
  91.4 13.5 %all_to_all.25.parts_ref = f32[12,1,128]{2,1,0:T(1,128)S(1)} all-to-all(f32[12,1,128]{2,1,0:T(1,128)S(1)} %get-tuple-element.32), channel_id=1, replica_groups=mesh['reg'=12,'blk'=64] {'reg'}, dimensions={0} | all-to-all | bytes 12288 | tf_op jit(solution)/shard_map/all_to_all | solution.py:396
  105.0 21.5 %all_to_all.26.parts_ref = f32[64,1,128]{2,1,0:T(1,128)S(1)} all-to-all(f32[64,1,128]{2,1,0:T(1,128)S(1)} %spread.1), channel_id=1, replica_groups=mesh['reg'=12,'blk'=64] {'blk'}, dimensions={0} | all-to-all | bytes 65536 | tf_op jit(solution)/shard_map/all_to_all | solution.py:406
  126.5 1.1 finish.1
  (45 shorter events, 0.8 us)
Async XLA Ops:
  0.6 34.1 %copy-start = (bf16[1,6,320,320]{3,2,1,0:T(8,128)(2,1)S(1)}, bf16[1,6,320,320]{3,2,1,0:T(8,128)(2,1)}, u32[]{:S(2)}) copy-start(bf16[1,6,320,320]{3,2,1,0:T(8,128)(2,1)} %param.13) | copy-start | bytes 3686404
  0.6 0.8 copy-start.4
  1.5 11.4 %copy-start.8 = (s32[1,6]{1,0:T(1,128)S(1)}, s32[1,6]{1,0:T(1,128)}, u32[]{:S(2)}) copy-start(s32[1,6]{1,0:T(1,128)} %param.11) | copy-start | bytes 76
  1.5 11.5 %copy-start.5 = (s32[6,4]{0,1:T(4,128)S(1)}, s32[6,4]{0,1:T(4,128)}, u32[]{:S(2)}) copy-start(s32[6,4]{0,1:T(4,128)} %param.15) | copy-start | bytes 292
  1.5 11.5 %copy-start.7 = (s32[6,4]{0,1:T(4,128)S(1)}, s32[6,4]{0,1:T(4,128)}, u32[]{:S(2)}) copy-start(s32[6,4]{0,1:T(4,128)} %param.16) | copy-start | bytes 292
  2.4 23.0 %all-to-all-start = ((f32[320,1,320]{2,1,0:T(1,128)}), f32[320,1,320]{2,1,0:T(1,128)S(1)}, u32[]{:S(2)}, u32[]{:S(2)}) async-start(f32[320,1,320]{2,1,0:T(1,128)} %repeat.1), calls=%async_computation | async-start | bytes 983040 | tf_op jit(solution)/shard_map/all_to_all | solution.py:324
  25.3 9.4 %collective-permute-start = (f32[320,1,320]{2,1,0:T(1,128)S(1)}, f32[320,1,320]{2,1,0:T(1,128)S(1)}, u32[]{:S(2)}, u32[]{:S(2)}) collective-permute-start(f32[320,1,320]{2,1,0:T(1,128)S(1)} %all-to-all-done.same_ref), channel_id=1, source_target_pairs={{0,1},{1,0},{2,3},{3,2},{4,5},{5,4},{6,7},{7,6},{8,9},{9,8},{10,11... | collective-permute-start | bytes 1228808 | tf_op jit(solution)/shard_map/ppermute | solution.py:325
  34.8 1.0 copy-start.1
  35.8 23.1 %copy-start.6 = (s32[6,4]{0,1:T(4,128)S(1)}, s32[6,4]{0,1:T(4,128)}, u32[]{:S(2)}) copy-start(s32[6,4]{0,1:T(4,128)} %param.17) | copy-start | bytes 292
  37.9 24.6 %all-to-all-start.1 = ((f32[64,1,256]{2,1,0:T(1,128)}), f32[64,1,256]{2,1,0:T(1,128)S(1)}, u32[]{:S(2)}, u32[]{:S(2)}) async-start(f32[64,1,256]{2,1,0:T(1,128)} %get-tuple-element.21), calls=%async_computation.1 | async-start | bytes 131072 | tf_op jit(solution)/shard_map/all_to_all | solution.py:339
  42.6 19.8 %collective-permute-start.1 = (f32[8,128]{1,0:T(8,128)S(1)}, f32[8,128]{1,0:T(8,128)S(1)}, u32[]{:S(2)}, u32[]{:S(2)}) collective-permute-start(f32[8,128]{1,0:T(8,128)S(1)} %get-tuple-element.22), channel_id=1, source_target_pairs={{0,64},{64,128},{128,192},{192,256},{256,320},{320,384},{384,448},... | collective-permute-start | bytes 12296 | tf_op jit(solution)/shard_map/ppermute | solution.py:337
  46.6 15.9 %collective-permute-start.2 = (f32[8,128]{1,0:T(8,128)S(1)}, f32[8,128]{1,0:T(8,128)S(1)}, u32[]{:S(2)}, u32[]{:S(2)}) collective-permute-start(f32[8,128]{1,0:T(8,128)S(1)} %get-tuple-element.23), channel_id=1, source_target_pairs={{64,0},{128,64},{192,128},{256,192},{320,256},{384,320},{448,384},... | collective-permute-start | bytes 12296 | tf_op jit(solution)/shard_map/ppermute | solution.py:338
  59.1 3.5 %copy-start.2 = (bf16[320,768]{1,0:T(8,128)(2,1)S(1)}, bf16[320,768]{1,0:T(8,128)(2,1)}, u32[]{:S(2)}) copy-start(bf16[320,768]{1,0:T(8,128)(2,1)} %constant.105.clone.select_ref) | copy-start | bytes 1474564
  59.1 3.5 %copy-start.3 = (bf16[6,80,320]{2,1,0:T(8,128)(2,1)S(1)}, bf16[6,80,320]{2,1,0:T(8,128)(2,1)}, u32[]{:S(2)}) copy-start(bf16[6,80,320]{2,1,0:T(8,128)(2,1)} %constant.106.clone.lift_ref) | copy-start | bytes 921604
  68.0 20.7 %all-to-all-start.2 = ((f32[64,1,256]{2,1,0:T(1,128)}), f32[64,1,256]{2,1,0:T(1,128)S(1)}, u32[]{:S(2)}, u32[]{:S(2)}) async-start(f32[64,1,256]{2,1,0:T(1,128)} %get-tuple-element.26), calls=%async_computation.2 | async-start | bytes 131072 | tf_op jit(solution)/shard_map/all_to_all | solution.py:339
  78.6 9.8 %collective-permute-start.3 = (f32[8,128]{1,0:T(8,128)S(1)}, f32[8,128]{1,0:T(8,128)S(1)}, u32[]{:S(2)}, u32[]{:S(2)}) collective-permute-start(f32[8,128]{1,0:T(8,128)S(1)} %get-tuple-element.27), channel_id=1, source_target_pairs={{0,64},{64,128},{128,192},{192,256},{256,320},{320,384},{384,448},... | collective-permute-start | bytes 12296 | tf_op jit(solution)/shard_map/ppermute | solution.py:337
  80.5 7.9 %collective-permute-start.4 = (f32[8,128]{1,0:T(8,128)S(1)}, f32[8,128]{1,0:T(8,128)S(1)}, u32[]{:S(2)}, u32[]{:S(2)}) collective-permute-start(f32[8,128]{1,0:T(8,128)S(1)} %get-tuple-element.28), channel_id=1, source_target_pairs={{64,0},{128,64},{192,128},{256,192},{320,256},{384,320},{448,384},... | collective-permute-start | bytes 12296 | tf_op jit(solution)/shard_map/ppermute | solution.py:338

commit v3 on v2

--- a/solution.py
+++ b/solution.py
@@ -13,6 +13,7 @@
 ELEMS = 6
 PAD = 8
 SLOTS = 10
+WINDOW = 384
 PER_PAIR = 3
 WIDTH = 256
 F32 = jnp.float32
@@ -82,12 +83,11 @@
     return jnp.where(row == element, result[:PAD], 0.0)
 
 
-def precondition(vector, jacobi_ref, arrive):
+def precondition(vector, jacobi_ref):
     parts = stacked_parts(vector)
     rounded = jnp.zeros((PAD, DOF), F32)
     full = jnp.zeros((PAD, DOF), F32)
     for element in range(ELEMS):
-        arrive(element)
         result = mul_t(parts, jacobi_ref[element])
         rounded = rounded + high_row(result, element)
         full = full + own_row(result, element)
@@ -95,9 +95,12 @@
 
 
 def send_traces(values, select_ref, pack_ref, send_ref, up_ref, down_ref, local_ref):
-    both = mul(stacked_parts(values), select_ref[...])
+    both = mul_t(stacked_parts(values), select_ref[...])
     traces = both[:PAD] + both[PAD:]
-    traces = [traces[:, 128 * face : 128 * (face + 1)] for face in range(6)]
+    pad = jnp.zeros((PAD, 128 - FDOF), F32)
+    traces = [
+        jnp.concatenate([traces[:, FDOF * face : FDOF * (face + 1)], pad], axis=1) for face in range(6)
+    ]
     down_ref[...] = traces[4]
     up_ref[...] = traces[5]
     sides = jnp.concatenate(traces[:4], axis=0)
@@ -111,33 +114,36 @@
 
 
 def repeat_kernel(rows_ref, out_ref):
-    for chip in range(out_ref.shape[0] // SLOTS):
-        out_ref[chip * SLOTS : (chip + 1) * SLOTS] = rows_ref[...]
+    flat = jnp.concatenate([rows_ref[slot] for slot in range(SLOTS)], axis=1)
+    for chip in range(out_ref.shape[0]):
+        out_ref[chip] = flat
+
+
+def hold_kernel(far_ref, near_ref):
+    near_ref[...] = far_ref[...]
 
 
 def first_kernel(
-    place_ref, same_ref, other_ref, jacobi_ref, select_ref, pack_ref,
-    rhs_ref, values_ref, full_ref, send_ref, up_ref, down_ref, local_ref,
+    place_ref, same_ref, other_ref, jacobi_ref, pack_ref, select_ref,
+    rhs_ref, values_ref, full_ref, send_ref, up_ref, down_ref, local_ref, held_ref,
 ):
-    rhs_ref[...] = jnp.zeros(rhs_ref.shape, F32)
+    held_ref[...] = jnp.zeros(held_ref.shape, F32)
     for element in range(ELEMS):
-        place = place_ref[0, element]
-        rhs_ref[element : element + 1, :] = jnp.where(
-            place_ref[1, element] == 1, other_ref[place], same_ref[place]
-        )
-    rounded, full = precondition(rhs_ref[...], jacobi_ref, lambda element: None)
+        chip, slot = place_ref[0, element], place_ref[1, element]
+        lanes = pl.ds(pl.multiple_of((slot * 5 // 2) * 128, 128), WINDOW)
+        window = jnp.where(place_ref[2, element] == 1, other_ref[chip, :, lanes], same_ref[chip, :, lanes])
+        turned = pltpu.roll(window, WINDOW - 64, 1)
+        held_ref[element : element + 1, :] = jnp.where(slot % 2 == 1, turned, window)
+    rhs_ref[...] = held_ref[:, :DOF]
+    rounded, full = precondition(rhs_ref[...], jacobi_ref)
     values_ref[...] = rounded
     full_ref[...] = full
     send_traces(rounded, select_ref, pack_ref, send_ref, up_ref, down_ref, local_ref)
 
 
-def fetch(source_ref, target_ref, semaphores, width):
+def fetch(source_ref, target_ref, semaphores):
     copies = [
-        pltpu.make_async_copy(
-            source_ref.at[pl.ds(element * width, width)],
-            target_ref.at[pl.ds(element * width, width)],
-            semaphores.at[element],
-        )
+        pltpu.make_async_copy(source_ref.at[element], target_ref.at[element], semaphores.at[element])
         for element in range(ELEMS)
     ]
     for copy in copies:
@@ -146,7 +152,7 @@
 
 
 def diagonal_kernel(values_ref, diagonal_ref, product_ref, held_ref, semaphores):
-    arrive = fetch(diagonal_ref, held_ref, semaphores, 1)
+    arrive = fetch(diagonal_ref, held_ref, semaphores)
     parts = stacked_parts(values_ref[...])
     total = jnp.zeros((PAD, DOF), F32)
     for element in range(ELEMS):
@@ -157,8 +163,8 @@
 
 
 def add_neighbors(
-    product_ref, recv_ref, below_ref, above_ref, local_ref, turn_ref, unpack_ref, here_ref, lift_ref,
-    coupling_ref, arrive,
+    product_ref, recv_ref, below_ref, above_ref, local_ref, turn_ref, unpack_ref, here_ref, coupling_ref,
+    select_ref, copy,
 ):
     high, low = two_parts(recv_ref[:, 0, :])
     arrived = mul(unpack_ref[...], high) + mul(unpack_ref[...], low)
@@ -184,47 +190,51 @@
     traces = [sides[face * PAD : (face + 1) * PAD] for face in range(4)] + [below_ref[...], above_ref[...]]
     parts = [stacked_parts(one[:, :FDOF]) for one in traces]
     terms = [jnp.zeros((PAD, FDOF), F32)] * 6
-    for element in range(ELEMS):
-        arrive(element)
-        for face in range(6):
-            high, low = two_parts(coupling_ref[element * 6 + face])
-            terms[face] = terms[face] + own_row(mul_t(parts[face], high) + mul_t(parts[face], low), element)
+    for face in range(6):
+        blocks = jnp.concatenate([coupling_ref[element * 6 + face] for element in range(ELEMS)], axis=0)
+        high, low = two_parts(blocks)
+        result = mul_t(parts[face], high) + mul_t(parts[face], low)
+        for element in range(ELEMS):
+            own = result[:, element * FDOF : (element + 1) * FDOF]
+            terms[face] = terms[face] + own_row(own, element)
+    copy.wait()
     total = product_ref[...]
     for face in range(6):
-        lifted = mul(stacked_parts(terms[face]), lift_ref[face])
+        lifted = mul(stacked_parts(terms[face]), select_ref[face * FDOF : (face + 1) * FDOF, :])
         total = total + lifted[:PAD] + lifted[PAD:]
     return total
 
 
 def middle_kernel(
-    product_ref, recv_ref, below_ref, above_ref, local_ref, turn_ref, unpack_ref, here_ref, lift_ref,
-    select_ref, pack_ref, coupling_ref, jacobi_ref,
+    product_ref, recv_ref, below_ref, above_ref, local_ref, turn_ref, unpack_ref, here_ref, coupling_ref,
+    pack_ref, jacobi_ref, far_select_ref,
     vector_ref, values_ref, full_ref, send_ref, up_ref, down_ref, new_local_ref,
-    held_coupling_ref, held_jacobi_ref, coupling_semaphores, jacobi_semaphores,
+    select_ref, semaphore,
 ):
-    coupling_arrive = fetch(coupling_ref, held_coupling_ref, coupling_semaphores, 6)
-    jacobi_arrive = fetch(jacobi_ref, held_jacobi_ref, jacobi_semaphores, 1)
+    copy = pltpu.make_async_copy(far_select_ref, select_ref, semaphore)
+    copy.start()
     vector = add_neighbors(
-        product_ref, recv_ref, below_ref, above_ref, local_ref, turn_ref, unpack_ref, here_ref, lift_ref,
-        held_coupling_ref, coupling_arrive,
+        product_ref, recv_ref, below_ref, above_ref, local_ref, turn_ref, unpack_ref, here_ref, coupling_ref,
+        select_ref, copy,
     )
     vector_ref[...] = vector
-    rounded, full = precondition(vector, held_jacobi_ref, jacobi_arrive)
+    rounded, full = precondition(vector, jacobi_ref)
     values_ref[...] = rounded
     full_ref[...] = full
     send_traces(rounded, select_ref, pack_ref, send_ref, up_ref, down_ref, new_local_ref)
 
 
 def last_kernel(
-    product_ref, recv_ref, below_ref, above_ref, local_ref, turn_ref, unpack_ref, here_ref, lift_ref,
-    rhs_ref, first_ref, coupling_ref,
+    product_ref, recv_ref, below_ref, above_ref, local_ref, turn_ref, unpack_ref, here_ref, coupling_ref,
+    rhs_ref, first_ref, far_select_ref,
     vector_ref, sums_ref,
-    held_coupling_ref, coupling_semaphores,
+    select_ref, semaphore,
 ):
-    arrive = fetch(coupling_ref, held_coupling_ref, coupling_semaphores, 6)
+    copy = pltpu.make_async_copy(far_select_ref, select_ref, semaphore)
+    copy.start()
     second = add_neighbors(
-        product_ref, recv_ref, below_ref, above_ref, local_ref, turn_ref, unpack_ref, here_ref, lift_ref,
-        held_coupling_ref, arrive,
+        product_ref, recv_ref, below_ref, above_ref, local_ref, turn_ref, unpack_ref, here_ref, coupling_ref,
+        select_ref, copy,
     )
     vector_ref[...] = second
     first, rhs = first_ref[...], rhs_ref[...]
@@ -302,18 +312,25 @@
 ):
     devices, layers = lax.axis_size("blk"), lax.axis_size("reg")
     chips = devices // 2
-    select = trace_matrix()
-    wide = np.zeros((6, 128, DOF), np.float32)
-    wide[:, :FDOF] = select
-    wide = jnp.asarray(wide.reshape(6 * 128, DOF).T, BF16)
-    lift = jnp.asarray(select, BF16)
+    select = jnp.asarray(trace_matrix().reshape(6 * FDOF, DOF), BF16)
+    near_select = pl.pallas_call(
+        hold_kernel,
+        out_shape=shape(6 * FDOF, DOF, dtype=BF16),
+        in_specs=vmem(1),
+        out_specs=vmem(1)[0],
+        compiler_params=params(8),
+        cost_estimate=cost(100000, 2**20),
+        name="hold",
+    )(select)
+    select = in_hbm(select)
+    held_select = [pltpu.VMEM((6 * FDOF, DOF), BF16), pltpu.SemaphoreType.DMA]
     diagonal, jacobi = diagonal_blocks[0], jacobi_blocks[0]
     coupling = coupling.reshape(6 * ELEMS, FDOF, FDOF)
 
     rows = jnp.transpose(assembly_rhs, (1, 0, 2))
     rows = pl.pallas_call(
         repeat_kernel,
-        out_shape=shape(chips * SLOTS, 1, DOF),
+        out_shape=shape(chips, 1, SLOTS * DOF),
         in_specs=vmem(1),
         out_specs=vmem(1)[0],
         compiler_params=params(8),
@@ -325,9 +342,8 @@
     other = lax.ppermute(same, "blk", [(device, device ^ 1) for device in range(devices)])
 
     owner = source_slot // SLOTS
-    place = owner // 2 * SLOTS + source_slot % SLOTS
     crossed = (owner % 2 != lax.axis_index("blk") % 2).astype(jnp.int32)
-    place = jnp.concatenate([place, crossed], axis=0)
+    place = jnp.concatenate([owner // 2, source_slot % SLOTS, crossed], axis=0)
     pack, unpack, here, turn = routes(neighbor, neighbor_face, orientation, devices)
 
     vector = shape(PAD, DOF)
@@ -354,29 +370,25 @@
         first_kernel,
         out_shape=(vector,) * 3 + sent,
         in_specs=[smem()] + vmem(5),
+        scratch_shapes=[pltpu.VMEM((PAD, WINDOW), F32)],
         out_specs=tuple(vmem(7)),
         compiler_params=params(16),
         cost_estimate=cost(6 * 2 * 16 * 480 * 320, 2**21),
         name="first",
-    )(place, same, other, jacobi, wide, pack)
+    )(place, same, other, jacobi, pack, near_select)
     recv, below, above = exchange(send, up, down)
     product = diagonal_part(values)
 
     first, values, full1, send, up, down, local1 = pl.pallas_call(
         middle_kernel,
         out_shape=(vector,) * 3 + sent,
-        in_specs=vmem(11) + anywhere(2),
+        in_specs=vmem(11) + anywhere(1),
+        scratch_shapes=held_select,
         out_specs=tuple(vmem(7)),
-        scratch_shapes=[
-            pltpu.VMEM((6 * ELEMS, FDOF, FDOF), F32),
-            pltpu.VMEM((ELEMS, DOF, DOF), BF16),
-            pltpu.SemaphoreType.DMA((ELEMS,)),
-            pltpu.SemaphoreType.DMA((ELEMS,)),
-        ],
         compiler_params=params(16),
         cost_estimate=cost(6 * 4 * 16 * 480 * 320, 4 * 2**20),
         name="middle",
-    )(product, recv, below, above, local, turn, unpack, here, lift, wide, pack, in_hbm(coupling), in_hbm(jacobi))
+    )(product, recv, below, above, local, turn, unpack, here, coupling, pack, jacobi, select)
     recv, below, above = exchange(send, up, down)
     product = diagonal_part(values)
 
@@ -384,15 +396,12 @@
         last_kernel,
         out_shape=(vector, shape(layers, 1, 128)),
         in_specs=vmem(11) + anywhere(1),
+        scratch_shapes=held_select,
         out_specs=tuple(vmem(2)),
-        scratch_shapes=[
-            pltpu.VMEM((6 * ELEMS, FDOF, FDOF), F32),
-            pltpu.SemaphoreType.DMA((ELEMS,)),
-        ],
         compiler_params=params(16),
         cost_estimate=cost(6 * 2 * 16 * 480 * 320, 2**21),
         name="last",
-    )(product, recv, below, above, local1, turn, unpack, here, lift, rhs, first, in_hbm(coupling))
+    )(product, recv, below, above, local1, turn, unpack, here, coupling, rhs, first, select)
     sums = lax.all_to_all(sums, "reg", 0, 0, tiled=True)
     sums = pl.pallas_call(
         spread_kernel,

time: 128 us -> 124 us (0.969)
  waiting for transfers between devices: 12.7 us -> 9.8 us
  other arithmetic: 0.61 us -> 2.64 us
  Pallas kernels: 18.9 us -> 17.3 us
    all_to_all x1, waiting for transfers between devices: 11 us -> 8.22 us  [per_device(): lax.all_to_all(rows, 'blk', 0, 0, axis_index_groups=same_core, tiled=True)]
    pallas_call x1, Pallas kernels: 5.4 us -> 3.81 us  [per_device(): pl.pallas_call(middle_kernel, out_shape=(vector,) * 3 + sent, in_specs=vm...]
  transfers between devices with their start and end apart: 8 -> 8, of which waited for: 3 -> 3; matrix products, arithmetic and copies ran while one was open for 1% -> 3% of each run, Pallas kernels for 5% -> 5%
where the time goes in v3:
time: 124 us; the launch traced here: 123 us
  starting transfers between devices  55.4 us (45%)
  blocking collectives  35.1 us (28%)
  Pallas kernels  17.3 us (14%)
  waiting for transfers between devices  9.8 us (8%)
  other arithmetic  2.64 us (2%)
  local copies, waits for them, and re-layouts  1.89 us (2%)
    all_to_all x1, blocking collectives, per_device(): sums = lax.all_to_all(sums, 'blk', 0, 0, tiled=True)  21.5 us
    ppermute x2, starting transfers between devices, exchange(): lax.ppermute(down, 'reg', [((i + 1) % layers, i) for i in range(layers)])  16.8 us
    all_to_all x2, starting transfers between devices, exchange(): return (lax.all_to_all(send, 'blk', 0, 0, tiled=True), below, above)  15.2 us
    all_to_all x1, blocking collectives, per_device(): sums = lax.all_to_all(sums, 'reg', 0, 0, tiled=True)  13.5 us
    all_to_all x1, starting transfers between devices, per_device(): lax.all_to_all(rows, 'blk', 0, 0, axis_index_groups=same_core, tiled=True)  10.5 us
    all_to_all x1, waiting for transfers between devices, per_device(): lax.all_to_all(rows, 'blk', 0, 0, axis_index_groups=same_core, tiled=True)  8.22 us
    ppermute x1, starting transfers between devices, per_device(): lax.ppermute(same, 'blk', [(device, device ^ 1) for device in range(devic...  7.02 us
    pallas_call x2, Pallas kernels, diagonal_part(): pl.pallas_call(diagonal_kernel, out_shape=vector, in_specs=vmem(1) + anyw...  6.73 us
  transfers between devices with their start and end apart: 8, of which 3 were waited for; matrix products, arithmetic and copies ran while one was open for 3% of the time, Pallas kernels for 5%

profile of v3, /device:TPU:1, one launch (start us, length us, event | category | flops | bytes accessed | tf_op | source)
XLA Modules:
  0.0 123.1 jit_solution(14491646245192966151)
XLA Ops:
  0.7 0.8 copy-done.3
  1.5 0.9 repeat.1
  2.4 10.5 %all-to-all-start = ((f32[32,1,3200]{2,1,0:T(1,128)}), f32[32,1,3200]{2,1,0:T(1,128)S(1)}, u32[]{:S(2)}, u32[]{:S(2)}) async-start(f32[32,1,3200]{2,1,0:T(1,128)} %repeat.1), calls=%async_computation | async-start | bytes 819200 | tf_op jit(solution)/shard_map/all_to_all | solution.py:341
  12.9 0.7 and_select_fusion.6
  13.6 0.7 pad_compare_fusion
  14.3 0.7 pad_multiply_fusion
  15.0 0.1 rem.109
  15.1 0.1 ne.167
  15.3 0.1 ge.12
  15.5 0.2 convert_reduce_fusion
  15.9 0.1 eq.129
  15.9 0.1 eq.118
  16.0 0.1 copy.12
  16.3 8.2 %all-to-all-done.same_ref = f32[32,1,3200]{2,1,0:T(1,128)S(1)} async-done(((f32[32,1,3200]{2,1,0:T(1,128)}), f32[32,1,3200]{2,1,0:T(1,128)S(1)}, u32[]{:S(2)}, u32[]{:S(2)}) %all-to-all-start) | async-done | bytes 409632 | tf_op jit(solution)/shard_map/all_to_all | solution.py:341
  24.6 7.0 %collective-permute-start = (f32[32,1,3200]{2,1,0:T(1,128)S(1)}, f32[32,1,3200]{2,1,0:T(1,128)S(1)}, u32[]{:S(2)}, u32[]{:S(2)}) collective-permute-start(f32[32,1,3200]{2,1,0:T(1,128)S(1)} %all-to-all-done.same_ref), channel_id=1, source_target_pairs={{0,1},{1,0},{2,3},{3,2},{4,5},{5,4},{6,7},{7,6},{8,9},{9,8},{10,11... | collective-permute-start | bytes 1228808 | tf_op jit(solution)/shard_map/ppermute | solution.py:342
  31.6 1.3 %collective-permute-done.other_ref = f32[32,1,3200]{2,1,0:T(1,128)S(1)} collective-permute-done((f32[32,1,3200]{2,1,0:T(1,128)S(1)}, f32[32,1,3200]{2,1,0:T(1,128)S(1)}, u32[]{:S(2)}, u32[]{:S(2)}) %collective-permute-start) | collective-permute-done | bytes 409632 | tf_op jit(solution)/shard_map/ppermute | solution.py:342
  32.9 2.3 %first.1 = (f32[8,320]{1,0:T(8,128)S(1)}, f32[8,320]{1,0:T(8,128)S(1)}, f32[8,320]{1,0:T(8,128)S(1)}, f32[64,1,256]{2,1,0:T(1,128)}, f32[8,128]{1,0:T(8,128)S(1)...) custom-call(s32[3,6]{1,0:T(4,128)S(1)} %pad_add_fusion.place_ref, f32[32,1,3200]{2,1,0:T(1,128)S(1)} %all-to-all-done.same_ref, ...), custom_call_target="tpu_custom_call" | custom-call | flops 29491200 | bytes 2097152 | tf_op jit(solution)/shard_map/first/pallas_call | solution.py:369
  35.3 4.6 %all-to-all-start.1 = ((f32[64,1,256]{2,1,0:T(1,128)}), f32[64,1,256]{2,1,0:T(1,128)S(1)}, u32[]{:S(2)}, u32[]{:S(2)}) async-start(f32[64,1,256]{2,1,0:T(1,128)} %get-tuple-element.21), calls=%async_computation.1 | async-start | bytes 131072 | tf_op jit(solution)/shard_map/all_to_all | solution.py:355
  40.0 4.0 %collective-permute-start.1 = (f32[8,128]{1,0:T(8,128)S(1)}, f32[8,128]{1,0:T(8,128)S(1)}, u32[]{:S(2)}, u32[]{:S(2)}) collective-permute-start(f32[8,128]{1,0:T(8,128)S(1)} %get-tuple-element.22), channel_id=1, source_target_pairs={{0,64},{64,128},{128,192},{192,256},{256,320},{320,384},{384,448},... | collective-permute-start | bytes 12296 | tf_op jit(solution)/shard_map/ppermute | solution.py:353
  44.0 12.2 %collective-permute-start.2 = (f32[8,128]{1,0:T(8,128)S(1)}, f32[8,128]{1,0:T(8,128)S(1)}, u32[]{:S(2)}, u32[]{:S(2)}) collective-permute-start(f32[8,128]{1,0:T(8,128)S(1)} %get-tuple-element.23), channel_id=1, source_target_pairs={{64,0},{128,64},{192,128},{256,192},{320,256},{384,320},{448,384},... | collective-permute-start | bytes 12296 | tf_op jit(solution)/shard_map/ppermute | solution.py:354
  56.2 0.1 broadcast_in_dim.4
  56.4 3.4 %diagonal_part.2.product_ref = f32[8,320]{1,0:T(8,128)S(1)} custom-call(f32[8,320]{1,0:T(8,128)S(1)} %get-tuple-element.20.values_ref, f32[6,320,320]{2,1,0:T(8,128)} %bitcast.21), custom_call_target="tpu_custom_call" | custom-call | flops 39321600 | bytes 4194304 | tf_op jit(solution)/shard_map/diagonal_part/pallas_call | solution.py:358
  59.9 3.8 %middle.1 = (f32[8,320]{1,0:T(8,128)S(1)}, f32[8,320]{1,0:T(8,128)S(1)}, f32[8,320]{1,0:T(8,128)S(1)}, f32[64,1,256]{2,1,0:T(1,128)}, f32[8,128]{1,0:T(8,128)S(1...) custom-call(f32[8,320]{1,0:T(8,128)S(1)} %diagonal_part.2.product_ref, f32[64,1,256]{2,1,0:T(1,128)S(1)} %all-to-all-done.1.recv_ref, ...), custom_call_target="tpu_custom_call" | custom-call | flops 58982400 | bytes 4194304 | tf_op jit(solution)/shard_map/middle/pallas_call | solution.py:382
  63.8 10.6 %all-to-all-start.2 = ((f32[64,1,256]{2,1,0:T(1,128)}), f32[64,1,256]{2,1,0:T(1,128)S(1)}, u32[]{:S(2)}, u32[]{:S(2)}) async-start(f32[64,1,256]{2,1,0:T(1,128)} %get-tuple-element.26), calls=%async_computation.2 | async-start | bytes 131072 | tf_op jit(solution)/shard_map/all_to_all | solution.py:355
  74.3 1.9 %collective-permute-start.3 = (f32[8,128]{1,0:T(8,128)S(1)}, f32[8,128]{1,0:T(8,128)S(1)}, u32[]{:S(2)}, u32[]{:S(2)}) collective-permute-start(f32[8,128]{1,0:T(8,128)S(1)} %get-tuple-element.27), channel_id=1, source_target_pairs={{0,64},{64,128},{128,192},{192,256},{256,320},{320,384},{384,448},... | collective-permute-start | bytes 12296 | tf_op jit(solution)/shard_map/ppermute | solution.py:353
  76.3 4.6 %collective-permute-start.4 = (f32[8,128]{1,0:T(8,128)S(1)}, f32[8,128]{1,0:T(8,128)S(1)}, u32[]{:S(2)}, u32[]{:S(2)}) collective-permute-start(f32[8,128]{1,0:T(8,128)S(1)} %get-tuple-element.28), channel_id=1, source_target_pairs={{64,0},{128,64},{192,128},{256,192},{320,256},{384,320},{448,384},... | collective-permute-start | bytes 12296 | tf_op jit(solution)/shard_map/ppermute | solution.py:354
  80.9 3.3 %diagonal_part.3.product_ref = f32[8,320]{1,0:T(8,128)S(1)} custom-call(f32[8,320]{1,0:T(8,128)S(1)} %get-tuple-element.25.values_ref, f32[6,320,320]{2,1,0:T(8,128)} %bitcast.22), custom_call_target="tpu_custom_call" | custom-call | flops 39321600 | bytes 4194304 | tf_op jit(solution)/shard_map/diagonal_part/pallas_call | solution.py:358
  84.2 0.2 all-to-all-done.2.recv_ref
  84.4 2.5 %last.1 = (f32[8,320]{1,0:T(8,128)S(1)}, f32[12,1,128]{2,1,0:T(1,128)S(1)}) custom-call(f32[8,320]{1,0:T(8,128)S(1)} %diagonal_part.3.product_ref, f32[64,1,256]{2,1,0:T(1,128)S(1)} %all-to-all-done.2.recv_ref, f32[8,128]{1,0:T(8,128)S(1)} %collective-permute-done.3.below_ref, f32[8,128]{1,0:T(8,128)S(1)} %collective-permute-done.4.above_ref, ...), custom_call_target="tpu_custom_call" | custom-call | flops 29491200 | bytes 2097152 | tf_op jit(solution)/shard_map/last/pallas_call | solution.py:395
  87.0 13.5 %all_to_all.25.parts_ref = f32[12,1,128]{2,1,0:T(1,128)S(1)} all-to-all(f32[12,1,128]{2,1,0:T(1,128)S(1)} %get-tuple-element.32), channel_id=1, replica_groups=mesh['reg'=12,'blk'=64] {'reg'}, dimensions={0} | all-to-all | bytes 12288 | tf_op jit(solution)/shard_map/all_to_all | solution.py:405
  100.5 21.5 %all_to_all.26.parts_ref = f32[64,1,128]{2,1,0:T(1,128)S(1)} all-to-all(f32[64,1,128]{2,1,0:T(1,128)S(1)} %spread.1), channel_id=1, replica_groups=mesh['reg'=12,'blk'=64] {'blk'}, dimensions={0} | all-to-all | bytes 65536 | tf_op jit(solution)/shard_map/all_to_all | solution.py:415
  122.0 1.1 finish.1
  (38 shorter events, 0.9 us)
Async XLA Ops:
  0.6 15.1 %copy-start.2 = (bf16[480,320]{1,0:T(8,128)(2,1)S(1)}, bf16[480,320]{1,0:T(8,128)(2,1)}, u32[]{:S(2)}) copy-start(bf16[480,320]{1,0:T(8,128)(2,1)} %constant.102.clone.far_ref.far_select_ref) | copy-start | bytes 921604
  0.6 32.3 %copy-start = (bf16[1,6,320,320]{3,2,1,0:T(8,128)(2,1)S(1)}, bf16[1,6,320,320]{3,2,1,0:T(8,128)(2,1)}, u32[]{:S(2)}) copy-start(bf16[1,6,320,320]{3,2,1,0:T(8,128)(2,1)} %param.12) | copy-start | bytes 3686404
  0.7 0.8 copy-start.3
  2.4 22.2 %all-to-all-start = ((f32[32,1,3200]{2,1,0:T(1,128)}), f32[32,1,3200]{2,1,0:T(1,128)S(1)}, u32[]{:S(2)}, u32[]{:S(2)}) async-start(f32[32,1,3200]{2,1,0:T(1,128)} %repeat.1), calls=%async_computation | async-start | bytes 819200 | tf_op jit(solution)/shard_map/all_to_all | solution.py:341
  15.7 40.5 %copy-start.4 = (s32[6,4]{0,1:T(4,128)S(1)}, s32[6,4]{0,1:T(4,128)}, u32[]{:S(2)}) copy-start(s32[6,4]{0,1:T(4,128)} %param.16) | copy-start | bytes 292
  24.6 8.4 %collective-permute-start = (f32[32,1,3200]{2,1,0:T(1,128)S(1)}, f32[32,1,3200]{2,1,0:T(1,128)S(1)}, u32[]{:S(2)}, u32[]{:S(2)}) collective-permute-start(f32[32,1,3200]{2,1,0:T(1,128)S(1)} %all-to-all-done.same_ref), channel_id=1, source_target_pairs={{0,1},{1,0},{2,3},{3,2},{4,5},{5,4},{6,7},{7,6},{8,9},{9,8},{10,11... | collective-permute-start | bytes 1228808 | tf_op jit(solution)/shard_map/ppermute | solution.py:342
  35.3 24.6 %all-to-all-start.1 = ((f32[64,1,256]{2,1,0:T(1,128)}), f32[64,1,256]{2,1,0:T(1,128)S(1)}, u32[]{:S(2)}, u32[]{:S(2)}) async-start(f32[64,1,256]{2,1,0:T(1,128)} %get-tuple-element.21), calls=%async_computation.1 | async-start | bytes 131072 | tf_op jit(solution)/shard_map/all_to_all | solution.py:355
  40.0 19.9 %collective-permute-start.1 = (f32[8,128]{1,0:T(8,128)S(1)}, f32[8,128]{1,0:T(8,128)S(1)}, u32[]{:S(2)}, u32[]{:S(2)}) collective-permute-start(f32[8,128]{1,0:T(8,128)S(1)} %get-tuple-element.22), channel_id=1, source_target_pairs={{0,64},{64,128},{128,192},{192,256},{256,320},{320,384},{384,448},... | collective-permute-start | bytes 12296 | tf_op jit(solution)/shard_map/ppermute | solution.py:353
  44.0 15.9 %collective-permute-start.2 = (f32[8,128]{1,0:T(8,128)S(1)}, f32[8,128]{1,0:T(8,128)S(1)}, u32[]{:S(2)}, u32[]{:S(2)}) collective-permute-start(f32[8,128]{1,0:T(8,128)S(1)} %get-tuple-element.23), channel_id=1, source_target_pairs={{64,0},{128,64},{192,128},{256,192},{320,256},{384,320},{448,384},... | collective-permute-start | bytes 12296 | tf_op jit(solution)/shard_map/ppermute | solution.py:354
  56.4 3.5 %copy-start.1 = (f32[1,6,6,80,80]{4,3,2,1,0:T(8,128)S(1)}, f32[1,6,6,80,80]{4,3,2,1,0:T(8,128)}, u32[]{:S(2)}) copy-start(f32[1,6,6,80,80]{4,3,2,1,0:T(8,128)} %param.13) | copy-start | bytes 2764804
  63.8 20.7 %all-to-all-start.2 = ((f32[64,1,256]{2,1,0:T(1,128)}), f32[64,1,256]{2,1,0:T(1,128)S(1)}, u32[]{:S(2)}, u32[]{:S(2)}) async-start(f32[64,1,256]{2,1,0:T(1,128)} %get-tuple-element.26), calls=%async_computation.2 | async-start | bytes 131072 | tf_op jit(solution)/shard_map/all_to_all | solution.py:355
  74.3 9.8 %collective-permute-start.3 = (f32[8,128]{1,0:T(8,128)S(1)}, f32[8,128]{1,0:T(8,128)S(1)}, u32[]{:S(2)}, u32[]{:S(2)}) collective-permute-start(f32[8,128]{1,0:T(8,128)S(1)} %get-tuple-element.27), channel_id=1, source_target_pairs={{0,64},{64,128},{128,192},{192,256},{256,320},{320,384},{384,448},... | collective-permute-start | bytes 12296 | tf_op jit(solution)/shard_map/ppermute | solution.py:353
  76.3 7.9 %collective-permute-start.4 = (f32[8,128]{1,0:T(8,128)S(1)}, f32[8,128]{1,0:T(8,128)S(1)}, u32[]{:S(2)}, u32[]{:S(2)}) collective-permute-start(f32[8,128]{1,0:T(8,128)S(1)} %get-tuple-element.28), channel_id=1, source_target_pairs={{64,0},{128,64},{192,128},{256,192},{320,256},{384,320},{448,384},... | collective-permute-start | bytes 12296 | tf_op jit(solution)/shard_map/ppermute | solution.py:354

commit v4 on v3

--- a/solution.py
+++ b/solution.py
@@ -1,6 +1,5 @@
 import jax
 import jax.numpy as jnp
-import numpy as np
 from jax import lax
 from jax.experimental import pallas as pl
 from jax.experimental.pallas import tpu as pltpu
@@ -20,14 +19,18 @@
 BF16 = jnp.bfloat16
 
 
-def face_index():
-    cube = np.arange(DOF).reshape(NVAR, NQ, NQ, NQ)
-    faces = (cube[:, 0], cube[:, -1], cube[:, :, 0], cube[:, :, -1], cube[..., 0], cube[..., -1])
-    return np.stack([one.reshape(-1) for one in faces])
-
-
-def trace_matrix():
-    return (face_index()[:, :, None] == np.arange(DOF)[None, None, :]).astype(np.float32)
+def fill_select(select_ref):
+    row = lax.broadcasted_iota(jnp.int32, (FDOF, DOF), 0)
+    entry = lax.broadcasted_iota(jnp.int32, (FDOF, DOF), 1)
+    variable = (row >> 4) << 6
+    first, second = (row >> 2) & 3, row & 3
+    along_i = variable + (row & 15)
+    along_j = variable + (first << 4) + second
+    along_k = variable + ((row & 15) << 2)
+    last = NQ - 1
+    places = (along_i, along_i + 16 * last, along_j, along_j + 4 * last, along_k, along_k + last)
+    for face, place in enumerate(places):
+        select_ref[face * FDOF : (face + 1) * FDOF, :] = jnp.where(entry == place, 1.0, 0.0).astype(BF16)
 
 
 def params(megabytes):
@@ -119,14 +122,18 @@
         out_ref[chip] = flat
 
 
-def hold_kernel(far_ref, near_ref):
-    near_ref[...] = far_ref[...]
+def hold_kernel(far_ref, near_ref, semaphore):
+    copy = pltpu.make_async_copy(far_ref, near_ref, semaphore)
+    copy.start()
+    copy.wait()
 
 
 def first_kernel(
-    place_ref, same_ref, other_ref, jacobi_ref, pack_ref, select_ref,
-    rhs_ref, values_ref, full_ref, send_ref, up_ref, down_ref, local_ref, held_ref,
+    place_ref, same_ref, other_ref, jacobi_ref, pack_ref,
+    rhs_ref, values_ref, full_ref, send_ref, up_ref, down_ref, local_ref,
+    select_ref, held_ref,
 ):
+    fill_select(select_ref)
     held_ref[...] = jnp.zeros(held_ref.shape, F32)
     for element in range(ELEMS):
         chip, slot = place_ref[0, element], place_ref[1, element]
@@ -164,7 +171,7 @@
 
 def add_neighbors(
     product_ref, recv_ref, below_ref, above_ref, local_ref, turn_ref, unpack_ref, here_ref, coupling_ref,
-    select_ref, copy,
+    select_ref,
 ):
     high, low = two_parts(recv_ref[:, 0, :])
     arrived = mul(unpack_ref[...], high) + mul(unpack_ref[...], low)
@@ -197,7 +204,6 @@
         for element in range(ELEMS):
             own = result[:, element * FDOF : (element + 1) * FDOF]
             terms[face] = terms[face] + own_row(own, element)
-    copy.wait()
     total = product_ref[...]
     for face in range(6):
         lifted = mul(stacked_parts(terms[face]), select_ref[face * FDOF : (face + 1) * FDOF, :])
@@ -207,15 +213,14 @@
 
 def middle_kernel(
     product_ref, recv_ref, below_ref, above_ref, local_ref, turn_ref, unpack_ref, here_ref, coupling_ref,
-    pack_ref, jacobi_ref, far_select_ref,
+    pack_ref, jacobi_ref,
     vector_ref, values_ref, full_ref, send_ref, up_ref, down_ref, new_local_ref,
-    select_ref, semaphore,
+    select_ref,
 ):
-    copy = pltpu.make_async_copy(far_select_ref, select_ref, semaphore)
-    copy.start()
+    fill_select(select_ref)
     vector = add_neighbors(
         product_ref, recv_ref, below_ref, above_ref, local_ref, turn_ref, unpack_ref, here_ref, coupling_ref,
-        select_ref, copy,
+        select_ref,
     )
     vector_ref[...] = vector
     rounded, full = precondition(vector, jacobi_ref)
@@ -226,15 +231,14 @@
 
 def last_kernel(
     product_ref, recv_ref, below_ref, above_ref, local_ref, turn_ref, unpack_ref, here_ref, coupling_ref,
-    rhs_ref, first_ref, far_select_ref,
+    rhs_ref, first_ref,
     vector_ref, sums_ref,
-    select_ref, semaphore,
+    select_ref,
 ):
-    copy = pltpu.make_async_copy(far_select_ref, select_ref, semaphore)
-    copy.start()
+    fill_select(select_ref)
     second = add_neighbors(
         product_ref, recv_ref, below_ref, above_ref, local_ref, turn_ref, unpack_ref, here_ref, coupling_ref,
-        select_ref, copy,
+        select_ref,
     )
     vector_ref[...] = second
     first, rhs = first_ref[...], rhs_ref[...]
@@ -312,19 +316,18 @@
 ):
     devices, layers = lax.axis_size("blk"), lax.axis_size("reg")
     chips = devices // 2
-    select = jnp.asarray(trace_matrix().reshape(6 * FDOF, DOF), BF16)
-    near_select = pl.pallas_call(
+    jacobi = pl.pallas_call(
         hold_kernel,
-        out_shape=shape(6 * FDOF, DOF, dtype=BF16),
-        in_specs=vmem(1),
+        out_shape=shape(ELEMS, DOF, DOF, dtype=BF16),
+        in_specs=anywhere(1),
         out_specs=vmem(1)[0],
+        scratch_shapes=[pltpu.SemaphoreType.DMA],
         compiler_params=params(8),
-        cost_estimate=cost(100000, 2**20),
+        cost_estimate=cost(100000, 2**21),
         name="hold",
-    )(select)
-    select = in_hbm(select)
-    held_select = [pltpu.VMEM((6 * FDOF, DOF), BF16), pltpu.SemaphoreType.DMA]
-    diagonal, jacobi = diagonal_blocks[0], jacobi_blocks[0]
+    )(in_hbm(jacobi_blocks[0]))
+    held_select = [pltpu.VMEM((6 * FDOF, DOF), BF16)]
+    diagonal = diagonal_blocks[0]
     coupling = coupling.reshape(6 * ELEMS, FDOF, FDOF)
 
     rows = jnp.transpose(assembly_rhs, (1, 0, 2))
@@ -369,39 +372,39 @@
     rhs, values, full0, send, up, down, local = pl.pallas_call(
         first_kernel,
         out_shape=(vector,) * 3 + sent,
-        in_specs=[smem()] + vmem(5),
-        scratch_shapes=[pltpu.VMEM((PAD, WINDOW), F32)],
+        in_specs=[smem()] + vmem(4),
+        scratch_shapes=held_select + [pltpu.VMEM((PAD, WINDOW), F32)],
         out_specs=tuple(vmem(7)),
         compiler_params=params(16),
         cost_estimate=cost(6 * 2 * 16 * 480 * 320, 2**21),
         name="first",
-    )(place, same, other, jacobi, pack, near_select)
+    )(place, same, other, jacobi, pack)
     recv, below, above = exchange(send, up, down)
     product = diagonal_part(values)
 
     first, values, full1, send, up, down, local1 = pl.pallas_call(
         middle_kernel,
         out_shape=(vector,) * 3 + sent,
-        in_specs=vmem(11) + anywhere(1),
+        in_specs=vmem(11),
         scratch_shapes=held_select,
         out_specs=tuple(vmem(7)),
         compiler_params=params(16),
         cost_estimate=cost(6 * 4 * 16 * 480 * 320, 4 * 2**20),
         name="middle",
-    )(product, recv, below, above, local, turn, unpack, here, coupling, pack, jacobi, select)
+    )(product, recv, below, above, local, turn, unpack, here, coupling, pack, jacobi)
     recv, below, above = exchange(send, up, down)
     product = diagonal_part(values)
 
     second, sums = pl.pallas_call(
         last_kernel,
         out_shape=(vector, shape(layers, 1, 128)),
-        in_specs=vmem(11) + anywhere(1),
+        in_specs=vmem(11),
         scratch_shapes=held_select,
         out_specs=tuple(vmem(2)),
         compiler_params=params(16),
         cost_estimate=cost(6 * 2 * 16 * 480 * 320, 2**21),
         name="last",
-    )(product, recv, below, above, local1, turn, unpack, here, coupling, rhs, first, select)
+    )(product, recv, below, above, local1, turn, unpack, here, coupling, rhs, first)
     sums = lax.all_to_all(sums, "reg", 0, 0, tiled=True)
     sums = pl.pallas_call(
         spread_kernel,

time: 124 us -> 122 us (0.984)
  waiting for transfers between devices: 9.8 us -> 8.45 us
    pallas_call x1, Pallas kernels: 0.03 us -> 1.39 us  [per_device(): pl.pallas_call(hold_kernel, out_shape=shape(ELEMS, DOF, DOF, dtype=BF16),...]
    all_to_all x1, waiting for transfers between devices: 8.22 us -> 6.87 us  [per_device(): lax.all_to_all(rows, 'blk', 0, 0, axis_index_groups=same_core, tiled=True)]
  transfers between devices with their start and end apart: 8 -> 8, of which waited for: 3 -> 3; matrix products, arithmetic and copies ran while one was open for 3% -> 3% of each run, Pallas kernels for 5% -> 7%
where the time goes in v4:
time: 122 us; the launch traced here: 121 us
  starting transfers between devices  55.4 us (45%)
  blocking collectives  35.1 us (29%)
  Pallas kernels  17 us (14%)
  waiting for transfers between devices  8.45 us (7%)
  other arithmetic  2.64 us (2%)
  local copies, waits for them, and re-layouts  1.75 us (1%)
    all_to_all x1, blocking collectives, per_device(): sums = lax.all_to_all(sums, 'blk', 0, 0, tiled=True)  21.6 us
    ppermute x2, starting transfers between devices, exchange(): lax.ppermute(down, 'reg', [((i + 1) % layers, i) for i in range(layers)])  16.8 us
    all_to_all x2, starting transfers between devices, exchange(): return (lax.all_to_all(send, 'blk', 0, 0, tiled=True), below, above)  15.2 us
    all_to_all x1, blocking collectives, per_device(): sums = lax.all_to_all(sums, 'reg', 0, 0, tiled=True)  13.5 us
    all_to_all x1, starting transfers between devices, per_device(): lax.all_to_all(rows, 'blk', 0, 0, axis_index_groups=same_core, tiled=True)  10.5 us
    ppermute x1, starting transfers between devices, per_device(): lax.ppermute(same, 'blk', [(device, device ^ 1) for device in range(devic...  7.02 us
    all_to_all x1, waiting for transfers between devices, per_device(): lax.all_to_all(rows, 'blk', 0, 0, axis_index_groups=same_core, tiled=True)  6.87 us
    pallas_call x2, Pallas kernels, diagonal_part(): pl.pallas_call(diagonal_kernel, out_shape=vector, in_specs=vmem(1) + anyw...  6.73 us
  transfers between devices with their start and end apart: 8, of which 3 were waited for; matrix products, arithmetic and copies ran while one was open for 3% of the time, Pallas kernels for 7%

profile of v4, /device:TPU:1, one launch (start us, length us, event | category | flops | bytes accessed | tf_op | source)
XLA Modules:
  0.0 121.2 jit_solution(9144835918652662919)
XLA Ops:
  0.6 0.7 copy-done.1
  1.3 0.9 repeat.1
  2.2 10.5 %all-to-all-start = ((f32[32,1,3200]{2,1,0:T(1,128)}), f32[32,1,3200]{2,1,0:T(1,128)S(1)}, u32[]{:S(2)}, u32[]{:S(2)}) async-start(f32[32,1,3200]{2,1,0:T(1,128)} %repeat.1), calls=%async_computation | async-start | bytes 819200 | tf_op jit(solution)/shard_map/all_to_all | solution.py:344
  12.7 0.7 and_select_fusion.6
  13.4 0.7 pad_compare_fusion
  14.1 0.7 pad_multiply_fusion
  14.8 0.1 rem.109
  15.0 0.1 ne.167
  15.2 0.1 ge.12
  15.3 0.2 convert_reduce_fusion
  15.5 1.4 %hold.1.jacobi_ref = bf16[6,320,320]{2,1,0:T(8,128)(2,1)S(1)} custom-call(bf16[6,320,320]{2,1,0:T(8,128)(2,1)} %bitcast.21), custom_call_target="tpu_custom_call" | custom-call | flops 100000 | bytes 2097152 | tf_op jit(solution)/shard_map/hold/pallas_call | solution.py:319
  17.0 0.1 eq.129
  17.1 0.1 eq.118
  17.2 0.1 copy.11
  17.5 6.9 %all-to-all-done.same_ref = f32[32,1,3200]{2,1,0:T(1,128)S(1)} async-done(((f32[32,1,3200]{2,1,0:T(1,128)}), f32[32,1,3200]{2,1,0:T(1,128)S(1)}, u32[]{:S(2)}, u32[]{:S(2)}) %all-to-all-start) | async-done | bytes 409632 | tf_op jit(solution)/shard_map/all_to_all | solution.py:344
  24.4 7.0 %collective-permute-start = (f32[32,1,3200]{2,1,0:T(1,128)S(1)}, f32[32,1,3200]{2,1,0:T(1,128)S(1)}, u32[]{:S(2)}, u32[]{:S(2)}) collective-permute-start(f32[32,1,3200]{2,1,0:T(1,128)S(1)} %all-to-all-done.same_ref), channel_id=1, source_target_pairs={{0,1},{1,0},{2,3},{3,2},{4,5},{5,4},{6,7},{7,6},{8,9},{9,8},{10,11... | collective-permute-start | bytes 1228808 | tf_op jit(solution)/shard_map/ppermute | solution.py:345
  31.5 1.3 %collective-permute-done.other_ref = f32[32,1,3200]{2,1,0:T(1,128)S(1)} collective-permute-done((f32[32,1,3200]{2,1,0:T(1,128)S(1)}, f32[32,1,3200]{2,1,0:T(1,128)S(1)}, u32[]{:S(2)}, u32[]{:S(2)}) %collective-permute-start) | collective-permute-done | bytes 409632 | tf_op jit(solution)/shard_map/ppermute | solution.py:345
  32.8 2.3 %first.1 = (f32[8,320]{1,0:T(8,128)S(1)}, f32[8,320]{1,0:T(8,128)S(1)}, f32[8,320]{1,0:T(8,128)S(1)}, f32[64,1,256]{2,1,0:T(1,128)}, f32[8,128]{1,0:T(8,128)S(1)...) custom-call(s32[3,6]{1,0:T(4,128)S(1)} %pad_add_fusion.place_ref, f32[32,1,3200]{2,1,0:T(1,128)S(1)} %all-to-all-done.same_ref, ...), custom_call_target="tpu_custom_call" | custom-call | flops 29491200 | bytes 2097152 | tf_op jit(solution)/shard_map/first/pallas_call | solution.py:372
  35.1 4.6 %all-to-all-start.1 = ((f32[64,1,256]{2,1,0:T(1,128)}), f32[64,1,256]{2,1,0:T(1,128)S(1)}, u32[]{:S(2)}, u32[]{:S(2)}) async-start(f32[64,1,256]{2,1,0:T(1,128)} %get-tuple-element.21), calls=%async_computation.1 | async-start | bytes 131072 | tf_op jit(solution)/shard_map/all_to_all | solution.py:358
  39.8 4.0 %collective-permute-start.1 = (f32[8,128]{1,0:T(8,128)S(1)}, f32[8,128]{1,0:T(8,128)S(1)}, u32[]{:S(2)}, u32[]{:S(2)}) collective-permute-start(f32[8,128]{1,0:T(8,128)S(1)} %get-tuple-element.22), channel_id=1, source_target_pairs={{0,64},{64,128},{128,192},{192,256},{256,320},{320,384},{384,448},... | collective-permute-start | bytes 12296 | tf_op jit(solution)/shard_map/ppermute | solution.py:356
  43.8 12.2 %collective-permute-start.2 = (f32[8,128]{1,0:T(8,128)S(1)}, f32[8,128]{1,0:T(8,128)S(1)}, u32[]{:S(2)}, u32[]{:S(2)}) collective-permute-start(f32[8,128]{1,0:T(8,128)S(1)} %get-tuple-element.23), channel_id=1, source_target_pairs={{64,0},{128,64},{192,128},{256,192},{320,256},{384,320},{448,384},... | collective-permute-start | bytes 12296 | tf_op jit(solution)/shard_map/ppermute | solution.py:357
  56.3 3.4 %diagonal_part.2.product_ref = f32[8,320]{1,0:T(8,128)S(1)} custom-call(f32[8,320]{1,0:T(8,128)S(1)} %get-tuple-element.20.values_ref, f32[6,320,320]{2,1,0:T(8,128)} %bitcast.19), custom_call_target="tpu_custom_call" | custom-call | flops 39321600 | bytes 4194304 | tf_op jit(solution)/shard_map/diagonal_part/pallas_call | solution.py:361
  59.8 3.1 %middle.1 = (f32[8,320]{1,0:T(8,128)S(1)}, f32[8,320]{1,0:T(8,128)S(1)}, f32[8,320]{1,0:T(8,128)S(1)}, f32[64,1,256]{2,1,0:T(1,128)}, f32[8,128]{1,0:T(8,128)S(1...) custom-call(f32[8,320]{1,0:T(8,128)S(1)} %diagonal_part.2.product_ref, f32[64,1,256]{2,1,0:T(1,128)S(1)} %all-to-all-done.1.recv_ref, ...), custom_call_target="tpu_custom_call" | custom-call | flops 58982400 | bytes 4194304 | tf_op jit(solution)/shard_map/middle/pallas_call | solution.py:385
  62.9 10.6 %all-to-all-start.2 = ((f32[64,1,256]{2,1,0:T(1,128)}), f32[64,1,256]{2,1,0:T(1,128)S(1)}, u32[]{:S(2)}, u32[]{:S(2)}) async-start(f32[64,1,256]{2,1,0:T(1,128)} %get-tuple-element.26), calls=%async_computation.2 | async-start | bytes 131072 | tf_op jit(solution)/shard_map/all_to_all | solution.py:358
  73.4 1.9 %collective-permute-start.3 = (f32[8,128]{1,0:T(8,128)S(1)}, f32[8,128]{1,0:T(8,128)S(1)}, u32[]{:S(2)}, u32[]{:S(2)}) collective-permute-start(f32[8,128]{1,0:T(8,128)S(1)} %get-tuple-element.27), channel_id=1, source_target_pairs={{0,64},{64,128},{128,192},{192,256},{256,320},{320,384},{384,448},... | collective-permute-start | bytes 12296 | tf_op jit(solution)/shard_map/ppermute | solution.py:356
  75.4 4.6 %collective-permute-start.4 = (f32[8,128]{1,0:T(8,128)S(1)}, f32[8,128]{1,0:T(8,128)S(1)}, u32[]{:S(2)}, u32[]{:S(2)}) collective-permute-start(f32[8,128]{1,0:T(8,128)S(1)} %get-tuple-element.28), channel_id=1, source_target_pairs={{64,0},{128,64},{192,128},{256,192},{320,256},{384,320},{448,384},... | collective-permute-start | bytes 12296 | tf_op jit(solution)/shard_map/ppermute | solution.py:357
  79.9 3.3 %diagonal_part.3.product_ref = f32[8,320]{1,0:T(8,128)S(1)} custom-call(f32[8,320]{1,0:T(8,128)S(1)} %get-tuple-element.25.values_ref, f32[6,320,320]{2,1,0:T(8,128)} %bitcast.20), custom_call_target="tpu_custom_call" | custom-call | flops 39321600 | bytes 4194304 | tf_op jit(solution)/shard_map/diagonal_part/pallas_call | solution.py:361
  83.3 0.2 all-to-all-done.2.recv_ref
  83.5 1.5 %last.1 = (f32[8,320]{1,0:T(8,128)S(1)}, f32[12,1,128]{2,1,0:T(1,128)S(1)}) custom-call(f32[8,320]{1,0:T(8,128)S(1)} %diagonal_part.3.product_ref, f32[64,1,256]{2,1,0:T(1,128)S(1)} %all-to-all-done.2.recv_ref, f32[8,128]{1,0:T(8,128)S(1)} %collective-permute-done.3.below_ref, f32[8,128]{1,0:T(8,128)S(1)} %collective-permute-done.4.above_ref, ...), custom_call_target="tpu_custom_call" | custom-call | flops 29491200 | bytes 2097152 | tf_op jit(solution)/shard_map/last/pallas_call | solution.py:398
  85.1 13.5 %all_to_all.25.parts_ref = f32[12,1,128]{2,1,0:T(1,128)S(1)} all-to-all(f32[12,1,128]{2,1,0:T(1,128)S(1)} %get-tuple-element.32), channel_id=1, replica_groups=mesh['reg'=12,'blk'=64] {'reg'}, dimensions={0} | all-to-all | bytes 12288 | tf_op jit(solution)/shard_map/all_to_all | solution.py:408
  98.6 21.6 %all_to_all.26.parts_ref = f32[64,1,128]{2,1,0:T(1,128)S(1)} all-to-all(f32[64,1,128]{2,1,0:T(1,128)S(1)} %spread.1), channel_id=1, replica_groups=mesh['reg'=12,'blk'=64] {'blk'}, dimensions={0} | all-to-all | bytes 65536 | tf_op jit(solution)/shard_map/all_to_all | solution.py:418
  120.2 1.1 finish.1
  (34 shorter events, 0.9 us)
Async XLA Ops:
  0.6 0.7 copy-start.1
  2.2 22.2 %all-to-all-start = ((f32[32,1,3200]{2,1,0:T(1,128)}), f32[32,1,3200]{2,1,0:T(1,128)S(1)}, u32[]{:S(2)}, u32[]{:S(2)}) async-start(f32[32,1,3200]{2,1,0:T(1,128)} %repeat.1), calls=%async_computation | async-start | bytes 819200 | tf_op jit(solution)/shard_map/all_to_all | solution.py:344
  16.9 39.1 %copy-start.2 = (s32[6,4]{0,1:T(4,128)S(1)}, s32[6,4]{0,1:T(4,128)}, u32[]{:S(2)}) copy-start(s32[6,4]{0,1:T(4,128)} %param.15) | copy-start | bytes 292
  24.4 8.4 %collective-permute-start = (f32[32,1,3200]{2,1,0:T(1,128)S(1)}, f32[32,1,3200]{2,1,0:T(1,128)S(1)}, u32[]{:S(2)}, u32[]{:S(2)}) collective-permute-start(f32[32,1,3200]{2,1,0:T(1,128)S(1)} %all-to-all-done.same_ref), channel_id=1, source_target_pairs={{0,1},{1,0},{2,3},{3,2},{4,5},{5,4},{6,7},{7,6},{8,9},{9,8},{10,11... | collective-permute-start | bytes 1228808 | tf_op jit(solution)/shard_map/ppermute | solution.py:345
  35.1 24.6 %all-to-all-start.1 = ((f32[64,1,256]{2,1,0:T(1,128)}), f32[64,1,256]{2,1,0:T(1,128)S(1)}, u32[]{:S(2)}, u32[]{:S(2)}) async-start(f32[64,1,256]{2,1,0:T(1,128)} %get-tuple-element.21), calls=%async_computation.1 | async-start | bytes 131072 | tf_op jit(solution)/shard_map/all_to_all | solution.py:358
  39.8 19.9 %collective-permute-start.1 = (f32[8,128]{1,0:T(8,128)S(1)}, f32[8,128]{1,0:T(8,128)S(1)}, u32[]{:S(2)}, u32[]{:S(2)}) collective-permute-start(f32[8,128]{1,0:T(8,128)S(1)} %get-tuple-element.22), channel_id=1, source_target_pairs={{0,64},{64,128},{128,192},{192,256},{256,320},{320,384},{384,448},... | collective-permute-start | bytes 12296 | tf_op jit(solution)/shard_map/ppermute | solution.py:356
  43.8 15.9 %collective-permute-start.2 = (f32[8,128]{1,0:T(8,128)S(1)}, f32[8,128]{1,0:T(8,128)S(1)}, u32[]{:S(2)}, u32[]{:S(2)}) collective-permute-start(f32[8,128]{1,0:T(8,128)S(1)} %get-tuple-element.23), channel_id=1, source_target_pairs={{64,0},{128,64},{192,128},{256,192},{320,256},{384,320},{448,384},... | collective-permute-start | bytes 12296 | tf_op jit(solution)/shard_map/ppermute | solution.py:357
  56.3 3.5 %copy-start = (f32[1,6,6,80,80]{4,3,2,1,0:T(8,128)S(1)}, f32[1,6,6,80,80]{4,3,2,1,0:T(8,128)}, u32[]{:S(2)}) copy-start(f32[1,6,6,80,80]{4,3,2,1,0:T(8,128)} %param.12) | copy-start | bytes 2764804
  62.9 20.7 %all-to-all-start.2 = ((f32[64,1,256]{2,1,0:T(1,128)}), f32[64,1,256]{2,1,0:T(1,128)S(1)}, u32[]{:S(2)}, u32[]{:S(2)}) async-start(f32[64,1,256]{2,1,0:T(1,128)} %get-tuple-element.26), calls=%async_computation.2 | async-start | bytes 131072 | tf_op jit(solution)/shard_map/all_to_all | solution.py:358
  73.4 9.8 %collective-permute-start.3 = (f32[8,128]{1,0:T(8,128)S(1)}, f32[8,128]{1,0:T(8,128)S(1)}, u32[]{:S(2)}, u32[]{:S(2)}) collective-permute-start(f32[8,128]{1,0:T(8,128)S(1)} %get-tuple-element.27), channel_id=1, source_target_pairs={{0,64},{64,128},{128,192},{192,256},{256,320},{320,384},{384,448},... | collective-permute-start | bytes 12296 | tf_op jit(solution)/shard_map/ppermute | solution.py:356
  75.4 7.9 %collective-permute-start.4 = (f32[8,128]{1,0:T(8,128)S(1)}, f32[8,128]{1,0:T(8,128)S(1)}, u32[]{:S(2)}, u32[]{:S(2)}) collective-permute-start(f32[8,128]{1,0:T(8,128)S(1)} %get-tuple-element.28), channel_id=1, source_target_pairs={{64,0},{128,64},{192,128},{256,192},{320,256},{384,320},{448,384},... | collective-permute-start | bytes 12296 | tf_op jit(solution)/shard_map/ppermute | solution.py:357

commit v5 on v4

--- a/solution.py
+++ b/solution.py
@@ -251,19 +251,22 @@
         sums_ref[copy] = sums
 
 
-def spread_kernel(parts_ref, sums_ref):
-    total = parts_ref[0]
-    for part in range(1, parts_ref.shape[0]):
-        total = total + parts_ref[part]
-    for copy in range(sums_ref.shape[0]):
-        sums_ref[copy] = total
-
-
-def finish_kernel(parts_ref, rhs_ref, first_ref, second_ref, full0_ref, full1_ref, solution_ref, residual_ref):
+def add_parts(parts_ref):
     totals = [parts_ref[part] for part in range(parts_ref.shape[0])]
     while len(totals) > 1:
         totals = [one + other for one, other in zip(totals[::2], totals[1::2])] + totals[len(totals) // 2 * 2 :]
-    g11, g12, g22, t1, t2 = (totals[0][:, place : place + 1] for place in range(5))
+    return totals[0]
+
+
+def spread_kernel(parts_ref, sums_ref):
+    total = add_parts(parts_ref)
+    for copy in range(sums_ref.shape[0]):
+        sums_ref[copy] = total
+
+
+def finish_kernel(parts_ref, rhs_ref, first_ref, second_ref, full0_ref, full1_ref, solution_ref, residual_ref):
+    total = add_parts(parts_ref)
+    g11, g12, g22, t1, t2 = (total[:, place : place + 1] for place in range(5))
     factor = g12 / g11
     weight2 = (t2 - factor * t1) / (g22 - factor * g12)
     weight1 = (t1 - g12 * weight2) / g11
@@ -397,7 +400,7 @@
 
     second, sums = pl.pallas_call(
         last_kernel,
-        out_shape=(vector, shape(layers, 1, 128)),
+        out_shape=(vector, shape(devices, 1, 128)),
         in_specs=vmem(11),
         scratch_shapes=held_select,
         out_specs=tuple(vmem(2)),
@@ -405,17 +408,17 @@
         cost_estimate=cost(6 * 2 * 16 * 480 * 320, 2**21),
         name="last",
     )(product, recv, below, above, local1, turn, unpack, here, coupling, rhs, first)
-    sums = lax.all_to_all(sums, "reg", 0, 0, tiled=True)
+    sums = lax.all_to_all(sums, "blk", 0, 0, tiled=True)
     sums = pl.pallas_call(
         spread_kernel,
-        out_shape=shape(devices, 1, 128),
+        out_shape=shape(layers, 1, 128),
         in_specs=vmem(1),
         out_specs=vmem(1)[0],
         compiler_params=params(8),
         cost_estimate=cost(2000, 2**15),
         name="spread",
     )(sums)
-    sums = lax.all_to_all(sums, "blk", 0, 0, tiled=True)
+    sums = lax.all_to_all(sums, "reg", 0, 0, tiled=True)
     answer, remaining = pl.pallas_call(
         finish_kernel,
         out_shape=(shape(ELEMS, 1, DOF), shape(ELEMS, 1, DOF)),

time: 122 us -> 120 us (0.984)
  blocking collectives: 35.1 us -> 33.6 us
    all_to_all x1, blocking collectives: 21.6 us -> 19.8 us  [per_device(): sums = lax.all_to_all(sums, 'blk', 0, 0, tiled=True)]
where the time goes in v5:
time: 120 us
  starting transfers between devices  55.4 us (46%)
  blocking collectives  33.6 us (28%)
  Pallas kernels  17 us (14%)
  waiting for transfers between devices  8.45 us (7%)
  other arithmetic  2.64 us (2%)
  local copies, waits for them, and re-layouts  1.75 us (1%)
    all_to_all x1, blocking collectives, per_device(): sums = lax.all_to_all(sums, 'blk', 0, 0, tiled=True)  19.8 us
    ppermute x2, starting transfers between devices, exchange(): lax.ppermute(down, 'reg', [((i + 1) % layers, i) for i in range(layers)])  16.8 us
    all_to_all x2, starting transfers between devices, exchange(): return (lax.all_to_all(send, 'blk', 0, 0, tiled=True), below, above)  15.2 us
    all_to_all x1, blocking collectives, per_device(): sums = lax.all_to_all(sums, 'reg', 0, 0, tiled=True)  13.8 us
    all_to_all x1, starting transfers between devices, per_device(): lax.all_to_all(rows, 'blk', 0, 0, axis_index_groups=same_core, tiled=True)  10.5 us
    ppermute x1, starting transfers between devices, per_device(): lax.ppermute(same, 'blk', [(device, device ^ 1) for device in range(devic...  7.02 us
    all_to_all x1, waiting for transfers between devices, per_device(): lax.all_to_all(rows, 'blk', 0, 0, axis_index_groups=same_core, tiled=True)  6.87 us
    pallas_call x2, Pallas kernels, diagonal_part(): pl.pallas_call(diagonal_kernel, out_shape=vector, in_specs=vmem(1) + anyw...  6.73 us
  transfers between devices with their start and end apart: 8, of which 3 were waited for; matrix products, arithmetic and copies ran while one was open for 3% of the time, Pallas kernels for 7%

profile of v5, /device:TPU:1, one launch (start us, length us, event | category | flops | bytes accessed | tf_op | source)
XLA Modules:
  0.0 119.8 jit_solution(12135508573363933333)
XLA Ops:
  0.6 0.7 copy-done.1
  1.3 0.9 repeat.1
  2.2 10.5 %all-to-all-start = ((f32[32,1,3200]{2,1,0:T(1,128)}), f32[32,1,3200]{2,1,0:T(1,128)S(1)}, u32[]{:S(2)}, u32[]{:S(2)}) async-start(f32[32,1,3200]{2,1,0:T(1,128)} %repeat.1), calls=%async_computation | async-start | bytes 819200 | tf_op jit(solution)/shard_map/all_to_all | solution.py:347
  12.7 0.7 and_select_fusion.6
  13.4 0.7 pad_compare_fusion
  14.1 0.7 pad_multiply_fusion
  14.8 0.1 rem.109
  15.0 0.1 ne.167
  15.2 0.1 ge.12
  15.3 0.2 convert_reduce_fusion
  15.5 1.4 %hold.1.jacobi_ref = bf16[6,320,320]{2,1,0:T(8,128)(2,1)S(1)} custom-call(bf16[6,320,320]{2,1,0:T(8,128)(2,1)} %bitcast.21), custom_call_target="tpu_custom_call" | custom-call | flops 100000 | bytes 2097152 | tf_op jit(solution)/shard_map/hold/pallas_call | solution.py:322
  17.0 0.1 eq.129
  17.1 0.1 eq.118
  17.2 0.1 copy.11
  17.5 6.9 %all-to-all-done.same_ref = f32[32,1,3200]{2,1,0:T(1,128)S(1)} async-done(((f32[32,1,3200]{2,1,0:T(1,128)}), f32[32,1,3200]{2,1,0:T(1,128)S(1)}, u32[]{:S(2)}, u32[]{:S(2)}) %all-to-all-start) | async-done | bytes 409632 | tf_op jit(solution)/shard_map/all_to_all | solution.py:347
  24.4 7.0 %collective-permute-start = (f32[32,1,3200]{2,1,0:T(1,128)S(1)}, f32[32,1,3200]{2,1,0:T(1,128)S(1)}, u32[]{:S(2)}, u32[]{:S(2)}) collective-permute-start(f32[32,1,3200]{2,1,0:T(1,128)S(1)} %all-to-all-done.same_ref), channel_id=1, source_target_pairs={{0,1},{1,0},{2,3},{3,2},{4,5},{5,4},{6,7},{7,6},{8,9},{9,8},{10,11... | collective-permute-start | bytes 1228808 | tf_op jit(solution)/shard_map/ppermute | solution.py:348
  31.5 1.3 %collective-permute-done.other_ref = f32[32,1,3200]{2,1,0:T(1,128)S(1)} collective-permute-done((f32[32,1,3200]{2,1,0:T(1,128)S(1)}, f32[32,1,3200]{2,1,0:T(1,128)S(1)}, u32[]{:S(2)}, u32[]{:S(2)}) %collective-permute-start) | collective-permute-done | bytes 409632 | tf_op jit(solution)/shard_map/ppermute | solution.py:348
  32.8 2.3 %first.1 = (f32[8,320]{1,0:T(8,128)S(1)}, f32[8,320]{1,0:T(8,128)S(1)}, f32[8,320]{1,0:T(8,128)S(1)}, f32[64,1,256]{2,1,0:T(1,128)}, f32[8,128]{1,0:T(8,128)S(1)...) custom-call(s32[3,6]{1,0:T(4,128)S(1)} %pad_add_fusion.place_ref, f32[32,1,3200]{2,1,0:T(1,128)S(1)} %all-to-all-done.same_ref, ...), custom_call_target="tpu_custom_call" | custom-call | flops 29491200 | bytes 2097152 | tf_op jit(solution)/shard_map/first/pallas_call | solution.py:375
  35.1 4.6 %all-to-all-start.1 = ((f32[64,1,256]{2,1,0:T(1,128)}), f32[64,1,256]{2,1,0:T(1,128)S(1)}, u32[]{:S(2)}, u32[]{:S(2)}) async-start(f32[64,1,256]{2,1,0:T(1,128)} %get-tuple-element.21), calls=%async_computation.1 | async-start | bytes 131072 | tf_op jit(solution)/shard_map/all_to_all | solution.py:361
  39.8 4.0 %collective-permute-start.1 = (f32[8,128]{1,0:T(8,128)S(1)}, f32[8,128]{1,0:T(8,128)S(1)}, u32[]{:S(2)}, u32[]{:S(2)}) collective-permute-start(f32[8,128]{1,0:T(8,128)S(1)} %get-tuple-element.22), channel_id=1, source_target_pairs={{0,64},{64,128},{128,192},{192,256},{256,320},{320,384},{384,448},... | collective-permute-start | bytes 12296 | tf_op jit(solution)/shard_map/ppermute | solution.py:359
  43.8 12.2 %collective-permute-start.2 = (f32[8,128]{1,0:T(8,128)S(1)}, f32[8,128]{1,0:T(8,128)S(1)}, u32[]{:S(2)}, u32[]{:S(2)}) collective-permute-start(f32[8,128]{1,0:T(8,128)S(1)} %get-tuple-element.23), channel_id=1, source_target_pairs={{64,0},{128,64},{192,128},{256,192},{320,256},{384,320},{448,384},... | collective-permute-start | bytes 12296 | tf_op jit(solution)/shard_map/ppermute | solution.py:360
  56.3 3.4 %diagonal_part.2.product_ref = f32[8,320]{1,0:T(8,128)S(1)} custom-call(f32[8,320]{1,0:T(8,128)S(1)} %get-tuple-element.20.values_ref, f32[6,320,320]{2,1,0:T(8,128)} %bitcast.19), custom_call_target="tpu_custom_call" | custom-call | flops 39321600 | bytes 4194304 | tf_op jit(solution)/shard_map/diagonal_part/pallas_call | solution.py:364
  59.8 3.1 %middle.1 = (f32[8,320]{1,0:T(8,128)S(1)}, f32[8,320]{1,0:T(8,128)S(1)}, f32[8,320]{1,0:T(8,128)S(1)}, f32[64,1,256]{2,1,0:T(1,128)}, f32[8,128]{1,0:T(8,128)S(1...) custom-call(f32[8,320]{1,0:T(8,128)S(1)} %diagonal_part.2.product_ref, f32[64,1,256]{2,1,0:T(1,128)S(1)} %all-to-all-done.1.recv_ref, ...), custom_call_target="tpu_custom_call" | custom-call | flops 58982400 | bytes 4194304 | tf_op jit(solution)/shard_map/middle/pallas_call | solution.py:388
  62.9 10.6 %all-to-all-start.2 = ((f32[64,1,256]{2,1,0:T(1,128)}), f32[64,1,256]{2,1,0:T(1,128)S(1)}, u32[]{:S(2)}, u32[]{:S(2)}) async-start(f32[64,1,256]{2,1,0:T(1,128)} %get-tuple-element.26), calls=%async_computation.2 | async-start | bytes 131072 | tf_op jit(solution)/shard_map/all_to_all | solution.py:361
  73.4 1.9 %collective-permute-start.3 = (f32[8,128]{1,0:T(8,128)S(1)}, f32[8,128]{1,0:T(8,128)S(1)}, u32[]{:S(2)}, u32[]{:S(2)}) collective-permute-start(f32[8,128]{1,0:T(8,128)S(1)} %get-tuple-element.27), channel_id=1, source_target_pairs={{0,64},{64,128},{128,192},{192,256},{256,320},{320,384},{384,448},... | collective-permute-start | bytes 12296 | tf_op jit(solution)/shard_map/ppermute | solution.py:359
  75.4 4.6 %collective-permute-start.4 = (f32[8,128]{1,0:T(8,128)S(1)}, f32[8,128]{1,0:T(8,128)S(1)}, u32[]{:S(2)}, u32[]{:S(2)}) collective-permute-start(f32[8,128]{1,0:T(8,128)S(1)} %get-tuple-element.28), channel_id=1, source_target_pairs={{64,0},{128,64},{192,128},{256,192},{320,256},{384,320},{448,384},... | collective-permute-start | bytes 12296 | tf_op jit(solution)/shard_map/ppermute | solution.py:360
  79.9 3.3 %diagonal_part.3.product_ref = f32[8,320]{1,0:T(8,128)S(1)} custom-call(f32[8,320]{1,0:T(8,128)S(1)} %get-tuple-element.25.values_ref, f32[6,320,320]{2,1,0:T(8,128)} %bitcast.20), custom_call_target="tpu_custom_call" | custom-call | flops 39321600 | bytes 4194304 | tf_op jit(solution)/shard_map/diagonal_part/pallas_call | solution.py:364
  83.3 0.2 all-to-all-done.2.recv_ref
  83.5 1.5 %last.1 = (f32[8,320]{1,0:T(8,128)S(1)}, f32[64,1,128]{2,1,0:T(1,128)S(1)}) custom-call(f32[8,320]{1,0:T(8,128)S(1)} %diagonal_part.3.product_ref, f32[64,1,256]{2,1,0:T(1,128)S(1)} %all-to-all-done.2.recv_ref, f32[8,128]{1,0:T(8,128)S(1)} %collective-permute-done.3.below_ref, f32[8,128]{1,0:T(8,128)S(1)} %collective-permute-done.4.above_ref, ...), custom_call_target="tpu_custom_call" | custom-call | flops 29491200 | bytes 2097152 | tf_op jit(solution)/shard_map/last/pallas_call | solution.py:401
  85.1 19.8 %all_to_all.25.parts_ref = f32[64,1,128]{2,1,0:T(1,128)S(1)} all-to-all(f32[64,1,128]{2,1,0:T(1,128)S(1)} %get-tuple-element.32), channel_id=1, replica_groups=mesh['reg'=12,'blk'=64] {'blk'}, dimensions={0} | all-to-all | bytes 65536 | tf_op jit(solution)/shard_map/all_to_all | solution.py:411
  104.9 13.8 %all_to_all.26.parts_ref = f32[12,1,128]{2,1,0:T(1,128)S(1)} all-to-all(f32[12,1,128]{2,1,0:T(1,128)S(1)} %spread.1), channel_id=1, replica_groups=mesh['reg'=12,'blk'=64] {'reg'}, dimensions={0} | all-to-all | bytes 12288 | tf_op jit(solution)/shard_map/all_to_all | solution.py:421
  118.7 1.0 finish.1
  (34 shorter events, 0.9 us)
Async XLA Ops:
  0.6 0.7 copy-start.1
  2.2 22.2 %all-to-all-start = ((f32[32,1,3200]{2,1,0:T(1,128)}), f32[32,1,3200]{2,1,0:T(1,128)S(1)}, u32[]{:S(2)}, u32[]{:S(2)}) async-start(f32[32,1,3200]{2,1,0:T(1,128)} %repeat.1), calls=%async_computation | async-start | bytes 819200 | tf_op jit(solution)/shard_map/all_to_all | solution.py:347
  16.9 39.1 %copy-start.2 = (s32[6,4]{0,1:T(4,128)S(1)}, s32[6,4]{0,1:T(4,128)}, u32[]{:S(2)}) copy-start(s32[6,4]{0,1:T(4,128)} %param.15) | copy-start | bytes 292
  24.4 8.4 %collective-permute-start = (f32[32,1,3200]{2,1,0:T(1,128)S(1)}, f32[32,1,3200]{2,1,0:T(1,128)S(1)}, u32[]{:S(2)}, u32[]{:S(2)}) collective-permute-start(f32[32,1,3200]{2,1,0:T(1,128)S(1)} %all-to-all-done.same_ref), channel_id=1, source_target_pairs={{0,1},{1,0},{2,3},{3,2},{4,5},{5,4},{6,7},{7,6},{8,9},{9,8},{10,11... | collective-permute-start | bytes 1228808 | tf_op jit(solution)/shard_map/ppermute | solution.py:348
  35.1 24.6 %all-to-all-start.1 = ((f32[64,1,256]{2,1,0:T(1,128)}), f32[64,1,256]{2,1,0:T(1,128)S(1)}, u32[]{:S(2)}, u32[]{:S(2)}) async-start(f32[64,1,256]{2,1,0:T(1,128)} %get-tuple-element.21), calls=%async_computation.1 | async-start | bytes 131072 | tf_op jit(solution)/shard_map/all_to_all | solution.py:361
  39.8 19.9 %collective-permute-start.1 = (f32[8,128]{1,0:T(8,128)S(1)}, f32[8,128]{1,0:T(8,128)S(1)}, u32[]{:S(2)}, u32[]{:S(2)}) collective-permute-start(f32[8,128]{1,0:T(8,128)S(1)} %get-tuple-element.22), channel_id=1, source_target_pairs={{0,64},{64,128},{128,192},{192,256},{256,320},{320,384},{384,448},... | collective-permute-start | bytes 12296 | tf_op jit(solution)/shard_map/ppermute | solution.py:359
  43.8 15.9 %collective-permute-start.2 = (f32[8,128]{1,0:T(8,128)S(1)}, f32[8,128]{1,0:T(8,128)S(1)}, u32[]{:S(2)}, u32[]{:S(2)}) collective-permute-start(f32[8,128]{1,0:T(8,128)S(1)} %get-tuple-element.23), channel_id=1, source_target_pairs={{64,0},{128,64},{192,128},{256,192},{320,256},{384,320},{448,384},... | collective-permute-start | bytes 12296 | tf_op jit(solution)/shard_map/ppermute | solution.py:360
  56.3 3.5 %copy-start = (f32[1,6,6,80,80]{4,3,2,1,0:T(8,128)S(1)}, f32[1,6,6,80,80]{4,3,2,1,0:T(8,128)}, u32[]{:S(2)}) copy-start(f32[1,6,6,80,80]{4,3,2,1,0:T(8,128)} %param.12) | copy-start | bytes 2764804
  62.9 20.7 %all-to-all-start.2 = ((f32[64,1,256]{2,1,0:T(1,128)}), f32[64,1,256]{2,1,0:T(1,128)S(1)}, u32[]{:S(2)}, u32[]{:S(2)}) async-start(f32[64,1,256]{2,1,0:T(1,128)} %get-tuple-element.26), calls=%async_computation.2 | async-start | bytes 131072 | tf_op jit(solution)/shard_map/all_to_all | solution.py:361
  73.4 9.8 %collective-permute-start.3 = (f32[8,128]{1,0:T(8,128)S(1)}, f32[8,128]{1,0:T(8,128)S(1)}, u32[]{:S(2)}, u32[]{:S(2)}) collective-permute-start(f32[8,128]{1,0:T(8,128)S(1)} %get-tuple-element.27), channel_id=1, source_target_pairs={{0,64},{64,128},{128,192},{192,256},{256,320},{320,384},{384,448},... | collective-permute-start | bytes 12296 | tf_op jit(solution)/shard_map/ppermute | solution.py:359
  75.4 7.9 %collective-permute-start.4 = (f32[8,128]{1,0:T(8,128)S(1)}, f32[8,128]{1,0:T(8,128)S(1)}, u32[]{:S(2)}, u32[]{:S(2)}) collective-permute-start(f32[8,128]{1,0:T(8,128)S(1)} %get-tuple-element.28), channel_id=1, source_target_pairs={{64,0},{128,64},{192,128},{256,192},{320,256},{384,320},{448,384},... | collective-permute-start | bytes 12296 | tf_op jit(solution)/shard_map/ppermute | solution.py:360

commit v6 on v5

--- a/solution.py
+++ b/solution.py
@@ -116,7 +116,10 @@
     send_ref[:, 0, :] = mul(pack_ref[...], high) + mul(pack_ref[...], low)
 
 
-def repeat_kernel(rows_ref, out_ref):
+def repeat_kernel(far_ref, out_ref, rows_ref, semaphore):
+    copy = pltpu.make_async_copy(far_ref, rows_ref, semaphore)
+    copy.start()
+    copy.wait()
     flat = jnp.concatenate([rows_ref[slot] for slot in range(SLOTS)], axis=1)
     for chip in range(out_ref.shape[0]):
         out_ref[chip] = flat
@@ -246,7 +249,8 @@
     sums = jnp.zeros((1, 128), F32)
     pairs = ((first, first), (first, second), (second, second), (first, rhs), (second, rhs))
     for place, (one, other) in enumerate(pairs):
-        sums = jnp.where(lane == place, jnp.sum(one * other), sums)
+        by_lane = jnp.sum(one * other, axis=0, keepdims=True)
+        sums = jnp.where(lane == place, jnp.sum(by_lane, axis=1, keepdims=True), sums)
     for copy in range(sums_ref.shape[0]):
         sums_ref[copy] = sums
 
@@ -337,12 +341,13 @@
     rows = pl.pallas_call(
         repeat_kernel,
         out_shape=shape(chips, 1, SLOTS * DOF),
-        in_specs=vmem(1),
+        in_specs=anywhere(1),
         out_specs=vmem(1)[0],
+        scratch_shapes=[pltpu.VMEM((SLOTS, 1, DOF), F32), pltpu.SemaphoreType.DMA],
         compiler_params=params(8),
         cost_estimate=cost(1000, 2**19),
         name="repeat",
-    )(rows)
+    )(in_hbm(rows))
     same_core = [[2 * chip + core for chip in range(chips)] for core in range(2)]
     same = lax.all_to_all(rows, "blk", 0, 0, axis_index_groups=same_core, tiled=True)
     other = lax.ppermute(same, "blk", [(device, device ^ 1) for device in range(devices)])

time: 120 us -> 120 us (level)
  no operation moved by 1% of the time
where the time goes in v6:
time: 120 us
  starting transfers between devices  55.4 us (46%)
  blocking collectives  33.6 us (28%)
  Pallas kernels  17.7 us (15%)
  waiting for transfers between devices  8.45 us (7%)
  other arithmetic  2.64 us (2%)
    all_to_all x1, blocking collectives, per_device(): sums = lax.all_to_all(sums, 'blk', 0, 0, tiled=True)  19.8 us
    ppermute x2, starting transfers between devices, exchange(): lax.ppermute(down, 'reg', [((i + 1) % layers, i) for i in range(layers)])  16.8 us
    all_to_all x2, starting transfers between devices, exchange(): return (lax.all_to_all(send, 'blk', 0, 0, tiled=True), below, above)  15.2 us
    all_to_all x1, blocking collectives, per_device(): sums = lax.all_to_all(sums, 'reg', 0, 0, tiled=True)  13.8 us
    all_to_all x1, starting transfers between devices, per_device(): lax.all_to_all(rows, 'blk', 0, 0, axis_index_groups=same_core, tiled=True)  10.5 us
    ppermute x1, starting transfers between devices, per_device(): lax.ppermute(same, 'blk', [(device, device ^ 1) for device in range(devic...  7.02 us
    all_to_all x1, waiting for transfers between devices, per_device(): lax.all_to_all(rows, 'blk', 0, 0, axis_index_groups=same_core, tiled=True)  6.87 us
    pallas_call x2, Pallas kernels, diagonal_part(): pl.pallas_call(diagonal_kernel, out_shape=vector, in_specs=vmem(1) + anyw...  6.73 us
  transfers between devices with their start and end apart: 8, of which 3 were waited for; matrix products, arithmetic and copies ran while one was open for 3% of the time, Pallas kernels for 7%

profile of v6, /device:TPU:1, one launch (start us, length us, event | category | flops | bytes accessed | tf_op | source)
XLA Modules:
  0.0 119.8 jit_solution(14614953789799433912)
XLA Ops:
  0.6 1.6 %repeat.1 = f32[32,1,3200]{2,1,0:T(1,128)} custom-call(f32[10,1,320]{2,1,0:T(1,128)} %bitcast.22), custom_call_target="tpu_custom_call" | custom-call | flops 1000 | bytes 524288 | tf_op jit(solution)/shard_map/repeat/pallas_call | solution.py:341
  2.2 10.5 %all-to-all-start = ((f32[32,1,3200]{2,1,0:T(1,128)}), f32[32,1,3200]{2,1,0:T(1,128)S(1)}, u32[]{:S(2)}, u32[]{:S(2)}) async-start(f32[32,1,3200]{2,1,0:T(1,128)} %repeat.1), calls=%async_computation | async-start | bytes 819200 | tf_op jit(solution)/shard_map/all_to_all | solution.py:352
  12.8 0.7 and_select_fusion.6
  13.4 0.7 pad_compare_fusion
  14.1 0.7 pad_multiply_fusion
  14.8 0.1 rem.109
  15.0 0.1 ne.167
  15.2 0.1 ge.12
  15.4 0.2 convert_reduce_fusion
  15.6 1.4 %hold.1.jacobi_ref = bf16[6,320,320]{2,1,0:T(8,128)(2,1)S(1)} custom-call(bf16[6,320,320]{2,1,0:T(8,128)(2,1)} %bitcast.20), custom_call_target="tpu_custom_call" | custom-call | flops 100000 | bytes 2097152 | tf_op jit(solution)/shard_map/hold/pallas_call | solution.py:326
  17.1 0.1 eq.129
  17.2 0.1 eq.118
  17.2 0.1 copy.11
  17.4 0.1 mul.37
  17.6 6.9 %all-to-all-done.same_ref = f32[32,1,3200]{2,1,0:T(1,128)S(1)} async-done(((f32[32,1,3200]{2,1,0:T(1,128)}), f32[32,1,3200]{2,1,0:T(1,128)S(1)}, u32[]{:S(2)}, u32[]{:S(2)}) %all-to-all-start) | async-done | bytes 409632 | tf_op jit(solution)/shard_map/all_to_all | solution.py:352
  24.4 7.0 %collective-permute-start = (f32[32,1,3200]{2,1,0:T(1,128)S(1)}, f32[32,1,3200]{2,1,0:T(1,128)S(1)}, u32[]{:S(2)}, u32[]{:S(2)}) collective-permute-start(f32[32,1,3200]{2,1,0:T(1,128)S(1)} %all-to-all-done.same_ref), channel_id=1, source_target_pairs={{0,1},{1,0},{2,3},{3,2},{4,5},{5,4},{6,7},{7,6},{8,9},{9,8},{10,11... | collective-permute-start | bytes 1228808 | tf_op jit(solution)/shard_map/ppermute | solution.py:353
  31.5 1.3 %collective-permute-done.other_ref = f32[32,1,3200]{2,1,0:T(1,128)S(1)} collective-permute-done((f32[32,1,3200]{2,1,0:T(1,128)S(1)}, f32[32,1,3200]{2,1,0:T(1,128)S(1)}, u32[]{:S(2)}, u32[]{:S(2)}) %collective-permute-start) | collective-permute-done | bytes 409632 | tf_op jit(solution)/shard_map/ppermute | solution.py:353
  32.8 2.3 %first.1 = (f32[8,320]{1,0:T(8,128)S(1)}, f32[8,320]{1,0:T(8,128)S(1)}, f32[8,320]{1,0:T(8,128)S(1)}, f32[64,1,256]{2,1,0:T(1,128)}, f32[8,128]{1,0:T(8,128)S(1)...) custom-call(s32[3,6]{1,0:T(4,128)S(1)} %pad_add_fusion.place_ref, f32[32,1,3200]{2,1,0:T(1,128)S(1)} %all-to-all-done.same_ref, ...), custom_call_target="tpu_custom_call" | custom-call | flops 29491200 | bytes 2097152 | tf_op jit(solution)/shard_map/first/pallas_call | solution.py:380
  35.1 4.6 %all-to-all-start.1 = ((f32[64,1,256]{2,1,0:T(1,128)}), f32[64,1,256]{2,1,0:T(1,128)S(1)}, u32[]{:S(2)}, u32[]{:S(2)}) async-start(f32[64,1,256]{2,1,0:T(1,128)} %get-tuple-element.21), calls=%async_computation.1 | async-start | bytes 131072 | tf_op jit(solution)/shard_map/all_to_all | solution.py:366
  39.9 4.0 %collective-permute-start.1 = (f32[8,128]{1,0:T(8,128)S(1)}, f32[8,128]{1,0:T(8,128)S(1)}, u32[]{:S(2)}, u32[]{:S(2)}) collective-permute-start(f32[8,128]{1,0:T(8,128)S(1)} %get-tuple-element.22), channel_id=1, source_target_pairs={{0,64},{64,128},{128,192},{192,256},{256,320},{320,384},{384,448},... | collective-permute-start | bytes 12296 | tf_op jit(solution)/shard_map/ppermute | solution.py:364
  43.9 12.2 %collective-permute-start.2 = (f32[8,128]{1,0:T(8,128)S(1)}, f32[8,128]{1,0:T(8,128)S(1)}, u32[]{:S(2)}, u32[]{:S(2)}) collective-permute-start(f32[8,128]{1,0:T(8,128)S(1)} %get-tuple-element.23), channel_id=1, source_target_pairs={{64,0},{128,64},{192,128},{256,192},{320,256},{384,320},{448,384},... | collective-permute-start | bytes 12296 | tf_op jit(solution)/shard_map/ppermute | solution.py:365
  56.3 3.4 %diagonal_part.2.product_ref = f32[8,320]{1,0:T(8,128)S(1)} custom-call(f32[8,320]{1,0:T(8,128)S(1)} %get-tuple-element.20.values_ref, f32[6,320,320]{2,1,0:T(8,128)} %bitcast.18), custom_call_target="tpu_custom_call" | custom-call | flops 39321600 | bytes 4194304 | tf_op jit(solution)/shard_map/diagonal_part/pallas_call | solution.py:369
  59.8 3.0 %middle.1 = (f32[8,320]{1,0:T(8,128)S(1)}, f32[8,320]{1,0:T(8,128)S(1)}, f32[8,320]{1,0:T(8,128)S(1)}, f32[64,1,256]{2,1,0:T(1,128)}, f32[8,128]{1,0:T(8,128)S(1...) custom-call(f32[8,320]{1,0:T(8,128)S(1)} %diagonal_part.2.product_ref, f32[64,1,256]{2,1,0:T(1,128)S(1)} %all-to-all-done.1.recv_ref, ...), custom_call_target="tpu_custom_call" | custom-call | flops 58982400 | bytes 4194304 | tf_op jit(solution)/shard_map/middle/pallas_call | solution.py:393
  62.9 10.6 %all-to-all-start.2 = ((f32[64,1,256]{2,1,0:T(1,128)}), f32[64,1,256]{2,1,0:T(1,128)S(1)}, u32[]{:S(2)}, u32[]{:S(2)}) async-start(f32[64,1,256]{2,1,0:T(1,128)} %get-tuple-element.26), calls=%async_computation.2 | async-start | bytes 131072 | tf_op jit(solution)/shard_map/all_to_all | solution.py:366
  73.5 1.9 %collective-permute-start.3 = (f32[8,128]{1,0:T(8,128)S(1)}, f32[8,128]{1,0:T(8,128)S(1)}, u32[]{:S(2)}, u32[]{:S(2)}) collective-permute-start(f32[8,128]{1,0:T(8,128)S(1)} %get-tuple-element.27), channel_id=1, source_target_pairs={{0,64},{64,128},{128,192},{192,256},{256,320},{320,384},{384,448},... | collective-permute-start | bytes 12296 | tf_op jit(solution)/shard_map/ppermute | solution.py:364
  75.4 4.6 %collective-permute-start.4 = (f32[8,128]{1,0:T(8,128)S(1)}, f32[8,128]{1,0:T(8,128)S(1)}, u32[]{:S(2)}, u32[]{:S(2)}) collective-permute-start(f32[8,128]{1,0:T(8,128)S(1)} %get-tuple-element.28), channel_id=1, source_target_pairs={{64,0},{128,64},{192,128},{256,192},{320,256},{384,320},{448,384},... | collective-permute-start | bytes 12296 | tf_op jit(solution)/shard_map/ppermute | solution.py:365
  80.0 3.3 %diagonal_part.3.product_ref = f32[8,320]{1,0:T(8,128)S(1)} custom-call(f32[8,320]{1,0:T(8,128)S(1)} %get-tuple-element.25.values_ref, f32[6,320,320]{2,1,0:T(8,128)} %bitcast.19), custom_call_target="tpu_custom_call" | custom-call | flops 39321600 | bytes 4194304 | tf_op jit(solution)/shard_map/diagonal_part/pallas_call | solution.py:369
  83.3 0.2 all-to-all-done.2.recv_ref
  83.5 1.5 %last.1 = (f32[8,320]{1,0:T(8,128)S(1)}, f32[64,1,128]{2,1,0:T(1,128)S(1)}) custom-call(f32[8,320]{1,0:T(8,128)S(1)} %diagonal_part.3.product_ref, f32[64,1,256]{2,1,0:T(1,128)S(1)} %all-to-all-done.2.recv_ref, f32[8,128]{1,0:T(8,128)S(1)} %collective-permute-done.3.below_ref, f32[8,128]{1,0:T(8,128)S(1)} %collective-permute-done.4.above_ref, ...), custom_call_target="tpu_custom_call" | custom-call | flops 29491200 | bytes 2097152 | tf_op jit(solution)/shard_map/last/pallas_call | solution.py:406
  85.1 19.8 %all_to_all.25.parts_ref = f32[64,1,128]{2,1,0:T(1,128)S(1)} all-to-all(f32[64,1,128]{2,1,0:T(1,128)S(1)} %get-tuple-element.32), channel_id=1, replica_groups=mesh['reg'=12,'blk'=64] {'blk'}, dimensions={0} | all-to-all | bytes 65536 | tf_op jit(solution)/shard_map/all_to_all | solution.py:416
  104.9 13.8 %all_to_all.26.parts_ref = f32[12,1,128]{2,1,0:T(1,128)S(1)} all-to-all(f32[12,1,128]{2,1,0:T(1,128)S(1)} %spread.1), channel_id=1, replica_groups=mesh['reg'=12,'blk'=64] {'reg'}, dimensions={0} | all-to-all | bytes 12288 | tf_op jit(solution)/shard_map/all_to_all | solution.py:426
  118.7 1.0 finish.1
  (32 shorter events, 0.8 us)
Async XLA Ops:
  2.2 22.2 %all-to-all-start = ((f32[32,1,3200]{2,1,0:T(1,128)}), f32[32,1,3200]{2,1,0:T(1,128)S(1)}, u32[]{:S(2)}, u32[]{:S(2)}) async-start(f32[32,1,3200]{2,1,0:T(1,128)} %repeat.1), calls=%async_computation | async-start | bytes 819200 | tf_op jit(solution)/shard_map/all_to_all | solution.py:352
  17.0 39.1 %copy-start.1 = (s32[6,4]{0,1:T(4,128)S(1)}, s32[6,4]{0,1:T(4,128)}, u32[]{:S(2)}) copy-start(s32[6,4]{0,1:T(4,128)} %param.15) | copy-start | bytes 292
  24.4 8.4 %collective-permute-start = (f32[32,1,3200]{2,1,0:T(1,128)S(1)}, f32[32,1,3200]{2,1,0:T(1,128)S(1)}, u32[]{:S(2)}, u32[]{:S(2)}) collective-permute-start(f32[32,1,3200]{2,1,0:T(1,128)S(1)} %all-to-all-done.same_ref), channel_id=1, source_target_pairs={{0,1},{1,0},{2,3},{3,2},{4,5},{5,4},{6,7},{7,6},{8,9},{9,8},{10,11... | collective-permute-start | bytes 1228808 | tf_op jit(solution)/shard_map/ppermute | solution.py:353
  35.1 24.6 %all-to-all-start.1 = ((f32[64,1,256]{2,1,0:T(1,128)}), f32[64,1,256]{2,1,0:T(1,128)S(1)}, u32[]{:S(2)}, u32[]{:S(2)}) async-start(f32[64,1,256]{2,1,0:T(1,128)} %get-tuple-element.21), calls=%async_computation.1 | async-start | bytes 131072 | tf_op jit(solution)/shard_map/all_to_all | solution.py:366
  39.9 19.9 %collective-permute-start.1 = (f32[8,128]{1,0:T(8,128)S(1)}, f32[8,128]{1,0:T(8,128)S(1)}, u32[]{:S(2)}, u32[]{:S(2)}) collective-permute-start(f32[8,128]{1,0:T(8,128)S(1)} %get-tuple-element.22), channel_id=1, source_target_pairs={{0,64},{64,128},{128,192},{192,256},{256,320},{320,384},{384,448},... | collective-permute-start | bytes 12296 | tf_op jit(solution)/shard_map/ppermute | solution.py:364
  43.9 15.9 %collective-permute-start.2 = (f32[8,128]{1,0:T(8,128)S(1)}, f32[8,128]{1,0:T(8,128)S(1)}, u32[]{:S(2)}, u32[]{:S(2)}) collective-permute-start(f32[8,128]{1,0:T(8,128)S(1)} %get-tuple-element.23), channel_id=1, source_target_pairs={{64,0},{128,64},{192,128},{256,192},{320,256},{384,320},{448,384},... | collective-permute-start | bytes 12296 | tf_op jit(solution)/shard_map/ppermute | solution.py:365
  56.3 3.5 %copy-start = (f32[1,6,6,80,80]{4,3,2,1,0:T(8,128)S(1)}, f32[1,6,6,80,80]{4,3,2,1,0:T(8,128)}, u32[]{:S(2)}) copy-start(f32[1,6,6,80,80]{4,3,2,1,0:T(8,128)} %param.12) | copy-start | bytes 2764804
  62.9 20.7 %all-to-all-start.2 = ((f32[64,1,256]{2,1,0:T(1,128)}), f32[64,1,256]{2,1,0:T(1,128)S(1)}, u32[]{:S(2)}, u32[]{:S(2)}) async-start(f32[64,1,256]{2,1,0:T(1,128)} %get-tuple-element.26), calls=%async_computation.2 | async-start | bytes 131072 | tf_op jit(solution)/shard_map/all_to_all | solution.py:366
  73.5 9.8 %collective-permute-start.3 = (f32[8,128]{1,0:T(8,128)S(1)}, f32[8,128]{1,0:T(8,128)S(1)}, u32[]{:S(2)}, u32[]{:S(2)}) collective-permute-start(f32[8,128]{1,0:T(8,128)S(1)} %get-tuple-element.27), channel_id=1, source_target_pairs={{0,64},{64,128},{128,192},{192,256},{256,320},{320,384},{384,448},... | collective-permute-start | bytes 12296 | tf_op jit(solution)/shard_map/ppermute | solution.py:364
  75.4 7.9 %collective-permute-start.4 = (f32[8,128]{1,0:T(8,128)S(1)}, f32[8,128]{1,0:T(8,128)S(1)}, u32[]{:S(2)}, u32[]{:S(2)}) collective-permute-start(f32[8,128]{1,0:T(8,128)S(1)} %get-tuple-element.28), channel_id=1, source_target_pairs={{64,0},{128,64},{192,128},{256,192},{320,256},{384,320},{448,384},... | collective-permute-start | bytes 12296 | tf_op jit(solution)/shard_map/ppermute | solution.py:365

commit v7 on v6

--- a/solution.py
+++ b/solution.py
@@ -168,7 +168,8 @@
     for element in range(ELEMS):
         arrive(element)
         high, low = two_parts(held_ref[element])
-        total = total + own_row(mul_t(parts, high) + mul_t(parts, low), element)
+        both = mul_t(parts, jnp.concatenate([high, low], axis=0))
+        total = total + own_row(both[:, :DOF] + both[:, DOF:], element)
     product_ref[...] = total
 
 

time: 120 us -> 120 us (level)
  no operation moved by 1% of the time
where the time goes in v7:
time: 120 us
  starting transfers between devices  55.4 us (46%)
  blocking collectives  33.6 us (28%)
  Pallas kernels  17.5 us (15%)
  waiting for transfers between devices  8.52 us (7%)
  other arithmetic  2.64 us (2%)
    all_to_all x1, blocking collectives, per_device(): sums = lax.all_to_all(sums, 'blk', 0, 0, tiled=True)  19.7 us
    ppermute x2, starting transfers between devices, exchange(): lax.ppermute(down, 'reg', [((i + 1) % layers, i) for i in range(layers)])  16.8 us
    all_to_all x2, starting transfers between devices, exchange(): return (lax.all_to_all(send, 'blk', 0, 0, tiled=True), below, above)  15.2 us
    all_to_all x1, blocking collectives, per_device(): sums = lax.all_to_all(sums, 'reg', 0, 0, tiled=True)  13.9 us
    all_to_all x1, starting transfers between devices, per_device(): lax.all_to_all(rows, 'blk', 0, 0, axis_index_groups=same_core, tiled=True)  10.5 us
    ppermute x1, starting transfers between devices, per_device(): lax.ppermute(same, 'blk', [(device, device ^ 1) for device in range(devic...  7.02 us
    all_to_all x1, waiting for transfers between devices, per_device(): lax.all_to_all(rows, 'blk', 0, 0, axis_index_groups=same_core, tiled=True)  6.87 us
    pallas_call x2, Pallas kernels, diagonal_part(): pl.pallas_call(diagonal_kernel, out_shape=vector, in_specs=vmem(1) + anyw...  6.58 us
  transfers between devices with their start and end apart: 8, of which 3 were waited for; matrix products, arithmetic and copies ran while one was open for 3% of the time, Pallas kernels for 7%

profile of v7, /device:TPU:1, one launch (start us, length us, event | category | flops | bytes accessed | tf_op | source)
XLA Modules:
  0.0 119.7 jit_solution(9143115673358149180)
XLA Ops:
  0.6 1.6 %repeat.1 = f32[32,1,3200]{2,1,0:T(1,128)} custom-call(f32[10,1,320]{2,1,0:T(1,128)} %bitcast.22), custom_call_target="tpu_custom_call" | custom-call | flops 1000 | bytes 524288 | tf_op jit(solution)/shard_map/repeat/pallas_call | solution.py:342
  2.2 10.5 %all-to-all-start = ((f32[32,1,3200]{2,1,0:T(1,128)}), f32[32,1,3200]{2,1,0:T(1,128)S(1)}, u32[]{:S(2)}, u32[]{:S(2)}) async-start(f32[32,1,3200]{2,1,0:T(1,128)} %repeat.1), calls=%async_computation | async-start | bytes 819200 | tf_op jit(solution)/shard_map/all_to_all | solution.py:353
  12.8 0.7 and_select_fusion.6
  13.4 0.7 pad_compare_fusion
  14.1 0.7 pad_multiply_fusion
  14.8 0.1 rem.109
  15.0 0.1 ne.167
  15.2 0.1 ge.12
  15.4 0.2 convert_reduce_fusion
  15.6 1.4 %hold.1.jacobi_ref = bf16[6,320,320]{2,1,0:T(8,128)(2,1)S(1)} custom-call(bf16[6,320,320]{2,1,0:T(8,128)(2,1)} %bitcast.20), custom_call_target="tpu_custom_call" | custom-call | flops 100000 | bytes 2097152 | tf_op jit(solution)/shard_map/hold/pallas_call | solution.py:327
  17.1 0.1 eq.129
  17.2 0.1 eq.118
  17.2 0.1 copy.11
  17.4 0.1 mul.37
  17.6 6.9 %all-to-all-done.same_ref = f32[32,1,3200]{2,1,0:T(1,128)S(1)} async-done(((f32[32,1,3200]{2,1,0:T(1,128)}), f32[32,1,3200]{2,1,0:T(1,128)S(1)}, u32[]{:S(2)}, u32[]{:S(2)}) %all-to-all-start) | async-done | bytes 409632 | tf_op jit(solution)/shard_map/all_to_all | solution.py:353
  24.4 7.0 %collective-permute-start = (f32[32,1,3200]{2,1,0:T(1,128)S(1)}, f32[32,1,3200]{2,1,0:T(1,128)S(1)}, u32[]{:S(2)}, u32[]{:S(2)}) collective-permute-start(f32[32,1,3200]{2,1,0:T(1,128)S(1)} %all-to-all-done.same_ref), channel_id=1, source_target_pairs={{0,1},{1,0},{2,3},{3,2},{4,5},{5,4},{6,7},{7,6},{8,9},{9,8},{10,11... | collective-permute-start | bytes 1228808 | tf_op jit(solution)/shard_map/ppermute | solution.py:354
  31.5 1.3 %collective-permute-done.other_ref = f32[32,1,3200]{2,1,0:T(1,128)S(1)} collective-permute-done((f32[32,1,3200]{2,1,0:T(1,128)S(1)}, f32[32,1,3200]{2,1,0:T(1,128)S(1)}, u32[]{:S(2)}, u32[]{:S(2)}) %collective-permute-start) | collective-permute-done | bytes 409632 | tf_op jit(solution)/shard_map/ppermute | solution.py:354
  32.8 2.3 %first.1 = (f32[8,320]{1,0:T(8,128)S(1)}, f32[8,320]{1,0:T(8,128)S(1)}, f32[8,320]{1,0:T(8,128)S(1)}, f32[64,1,256]{2,1,0:T(1,128)}, f32[8,128]{1,0:T(8,128)S(1)...) custom-call(s32[3,6]{1,0:T(4,128)S(1)} %pad_add_fusion.place_ref, f32[32,1,3200]{2,1,0:T(1,128)S(1)} %all-to-all-done.same_ref, ...), custom_call_target="tpu_custom_call" | custom-call | flops 29491200 | bytes 2097152 | tf_op jit(solution)/shard_map/first/pallas_call | solution.py:381
  35.1 4.6 %all-to-all-start.1 = ((f32[64,1,256]{2,1,0:T(1,128)}), f32[64,1,256]{2,1,0:T(1,128)S(1)}, u32[]{:S(2)}, u32[]{:S(2)}) async-start(f32[64,1,256]{2,1,0:T(1,128)} %get-tuple-element.21), calls=%async_computation.1 | async-start | bytes 131072 | tf_op jit(solution)/shard_map/all_to_all | solution.py:367
  39.9 4.0 %collective-permute-start.1 = (f32[8,128]{1,0:T(8,128)S(1)}, f32[8,128]{1,0:T(8,128)S(1)}, u32[]{:S(2)}, u32[]{:S(2)}) collective-permute-start(f32[8,128]{1,0:T(8,128)S(1)} %get-tuple-element.22), channel_id=1, source_target_pairs={{0,64},{64,128},{128,192},{192,256},{256,320},{320,384},{384,448},... | collective-permute-start | bytes 12296 | tf_op jit(solution)/shard_map/ppermute | solution.py:365
  43.9 12.2 %collective-permute-start.2 = (f32[8,128]{1,0:T(8,128)S(1)}, f32[8,128]{1,0:T(8,128)S(1)}, u32[]{:S(2)}, u32[]{:S(2)}) collective-permute-start(f32[8,128]{1,0:T(8,128)S(1)} %get-tuple-element.23), channel_id=1, source_target_pairs={{64,0},{128,64},{192,128},{256,192},{320,256},{384,320},{448,384},... | collective-permute-start | bytes 12296 | tf_op jit(solution)/shard_map/ppermute | solution.py:366
  56.3 3.3 %diagonal_part.2.product_ref = f32[8,320]{1,0:T(8,128)S(1)} custom-call(f32[8,320]{1,0:T(8,128)S(1)} %get-tuple-element.20.values_ref, f32[6,320,320]{2,1,0:T(8,128)} %bitcast.18), custom_call_target="tpu_custom_call" | custom-call | flops 39321600 | bytes 4194304 | tf_op jit(solution)/shard_map/diagonal_part/pallas_call | solution.py:370
  59.8 3.0 %middle.1 = (f32[8,320]{1,0:T(8,128)S(1)}, f32[8,320]{1,0:T(8,128)S(1)}, f32[8,320]{1,0:T(8,128)S(1)}, f32[64,1,256]{2,1,0:T(1,128)}, f32[8,128]{1,0:T(8,128)S(1...) custom-call(f32[8,320]{1,0:T(8,128)S(1)} %diagonal_part.2.product_ref, f32[64,1,256]{2,1,0:T(1,128)S(1)} %all-to-all-done.1.recv_ref, ...), custom_call_target="tpu_custom_call" | custom-call | flops 58982400 | bytes 4194304 | tf_op jit(solution)/shard_map/middle/pallas_call | solution.py:394
  62.8 10.6 %all-to-all-start.2 = ((f32[64,1,256]{2,1,0:T(1,128)}), f32[64,1,256]{2,1,0:T(1,128)S(1)}, u32[]{:S(2)}, u32[]{:S(2)}) async-start(f32[64,1,256]{2,1,0:T(1,128)} %get-tuple-element.26), calls=%async_computation.2 | async-start | bytes 131072 | tf_op jit(solution)/shard_map/all_to_all | solution.py:367
  73.4 1.9 %collective-permute-start.3 = (f32[8,128]{1,0:T(8,128)S(1)}, f32[8,128]{1,0:T(8,128)S(1)}, u32[]{:S(2)}, u32[]{:S(2)}) collective-permute-start(f32[8,128]{1,0:T(8,128)S(1)} %get-tuple-element.27), channel_id=1, source_target_pairs={{0,64},{64,128},{128,192},{192,256},{256,320},{320,384},{384,448},... | collective-permute-start | bytes 12296 | tf_op jit(solution)/shard_map/ppermute | solution.py:365
  75.3 4.6 %collective-permute-start.4 = (f32[8,128]{1,0:T(8,128)S(1)}, f32[8,128]{1,0:T(8,128)S(1)}, u32[]{:S(2)}, u32[]{:S(2)}) collective-permute-start(f32[8,128]{1,0:T(8,128)S(1)} %get-tuple-element.28), channel_id=1, source_target_pairs={{64,0},{128,64},{192,128},{256,192},{320,256},{384,320},{448,384},... | collective-permute-start | bytes 12296 | tf_op jit(solution)/shard_map/ppermute | solution.py:366
  79.9 3.2 %diagonal_part.3.product_ref = f32[8,320]{1,0:T(8,128)S(1)} custom-call(f32[8,320]{1,0:T(8,128)S(1)} %get-tuple-element.25.values_ref, f32[6,320,320]{2,1,0:T(8,128)} %bitcast.19), custom_call_target="tpu_custom_call" | custom-call | flops 39321600 | bytes 4194304 | tf_op jit(solution)/shard_map/diagonal_part/pallas_call | solution.py:370
  83.2 0.3 all-to-all-done.2.recv_ref
  83.5 1.5 %last.1 = (f32[8,320]{1,0:T(8,128)S(1)}, f32[64,1,128]{2,1,0:T(1,128)S(1)}) custom-call(f32[8,320]{1,0:T(8,128)S(1)} %diagonal_part.3.product_ref, f32[64,1,256]{2,1,0:T(1,128)S(1)} %all-to-all-done.2.recv_ref, f32[8,128]{1,0:T(8,128)S(1)} %collective-permute-done.3.below_ref, f32[8,128]{1,0:T(8,128)S(1)} %collective-permute-done.4.above_ref, ...), custom_call_target="tpu_custom_call" | custom-call | flops 29491200 | bytes 2097152 | tf_op jit(solution)/shard_map/last/pallas_call | solution.py:407
  85.0 19.7 %all_to_all.25.parts_ref = f32[64,1,128]{2,1,0:T(1,128)S(1)} all-to-all(f32[64,1,128]{2,1,0:T(1,128)S(1)} %get-tuple-element.32), channel_id=1, replica_groups=mesh['reg'=12,'blk'=64] {'blk'}, dimensions={0} | all-to-all | bytes 65536 | tf_op jit(solution)/shard_map/all_to_all | solution.py:417
  104.7 13.9 %all_to_all.26.parts_ref = f32[12,1,128]{2,1,0:T(1,128)S(1)} all-to-all(f32[12,1,128]{2,1,0:T(1,128)S(1)} %spread.1), channel_id=1, replica_groups=mesh['reg'=12,'blk'=64] {'reg'}, dimensions={0} | all-to-all | bytes 12288 | tf_op jit(solution)/shard_map/all_to_all | solution.py:427
  118.6 1.0 finish.1
  (32 shorter events, 0.8 us)
Async XLA Ops:
  2.2 22.2 %all-to-all-start = ((f32[32,1,3200]{2,1,0:T(1,128)}), f32[32,1,3200]{2,1,0:T(1,128)S(1)}, u32[]{:S(2)}, u32[]{:S(2)}) async-start(f32[32,1,3200]{2,1,0:T(1,128)} %repeat.1), calls=%async_computation | async-start | bytes 819200 | tf_op jit(solution)/shard_map/all_to_all | solution.py:353
  17.0 39.1 %copy-start.1 = (s32[6,4]{0,1:T(4,128)S(1)}, s32[6,4]{0,1:T(4,128)}, u32[]{:S(2)}) copy-start(s32[6,4]{0,1:T(4,128)} %param.15) | copy-start | bytes 292
  24.4 8.4 %collective-permute-start = (f32[32,1,3200]{2,1,0:T(1,128)S(1)}, f32[32,1,3200]{2,1,0:T(1,128)S(1)}, u32[]{:S(2)}, u32[]{:S(2)}) collective-permute-start(f32[32,1,3200]{2,1,0:T(1,128)S(1)} %all-to-all-done.same_ref), channel_id=1, source_target_pairs={{0,1},{1,0},{2,3},{3,2},{4,5},{5,4},{6,7},{7,6},{8,9},{9,8},{10,11... | collective-permute-start | bytes 1228808 | tf_op jit(solution)/shard_map/ppermute | solution.py:354
  35.1 24.5 %all-to-all-start.1 = ((f32[64,1,256]{2,1,0:T(1,128)}), f32[64,1,256]{2,1,0:T(1,128)S(1)}, u32[]{:S(2)}, u32[]{:S(2)}) async-start(f32[64,1,256]{2,1,0:T(1,128)} %get-tuple-element.21), calls=%async_computation.1 | async-start | bytes 131072 | tf_op jit(solution)/shard_map/all_to_all | solution.py:367
  39.9 19.8 %collective-permute-start.1 = (f32[8,128]{1,0:T(8,128)S(1)}, f32[8,128]{1,0:T(8,128)S(1)}, u32[]{:S(2)}, u32[]{:S(2)}) collective-permute-start(f32[8,128]{1,0:T(8,128)S(1)} %get-tuple-element.22), channel_id=1, source_target_pairs={{0,64},{64,128},{128,192},{192,256},{256,320},{320,384},{384,448},... | collective-permute-start | bytes 12296 | tf_op jit(solution)/shard_map/ppermute | solution.py:365
  43.9 15.8 %collective-permute-start.2 = (f32[8,128]{1,0:T(8,128)S(1)}, f32[8,128]{1,0:T(8,128)S(1)}, u32[]{:S(2)}, u32[]{:S(2)}) collective-permute-start(f32[8,128]{1,0:T(8,128)S(1)} %get-tuple-element.23), channel_id=1, source_target_pairs={{64,0},{128,64},{192,128},{256,192},{320,256},{384,320},{448,384},... | collective-permute-start | bytes 12296 | tf_op jit(solution)/shard_map/ppermute | solution.py:366
  56.3 3.5 %copy-start = (f32[1,6,6,80,80]{4,3,2,1,0:T(8,128)S(1)}, f32[1,6,6,80,80]{4,3,2,1,0:T(8,128)}, u32[]{:S(2)}) copy-start(f32[1,6,6,80,80]{4,3,2,1,0:T(8,128)} %param.12) | copy-start | bytes 2764804
  62.8 20.7 %all-to-all-start.2 = ((f32[64,1,256]{2,1,0:T(1,128)}), f32[64,1,256]{2,1,0:T(1,128)S(1)}, u32[]{:S(2)}, u32[]{:S(2)}) async-start(f32[64,1,256]{2,1,0:T(1,128)} %get-tuple-element.26), calls=%async_computation.2 | async-start | bytes 131072 | tf_op jit(solution)/shard_map/all_to_all | solution.py:367
  73.4 9.8 %collective-permute-start.3 = (f32[8,128]{1,0:T(8,128)S(1)}, f32[8,128]{1,0:T(8,128)S(1)}, u32[]{:S(2)}, u32[]{:S(2)}) collective-permute-start(f32[8,128]{1,0:T(8,128)S(1)} %get-tuple-element.27), channel_id=1, source_target_pairs={{0,64},{64,128},{128,192},{192,256},{256,320},{320,384},{384,448},... | collective-permute-start | bytes 12296 | tf_op jit(solution)/shard_map/ppermute | solution.py:365
  75.3 7.8 %collective-permute-start.4 = (f32[8,128]{1,0:T(8,128)S(1)}, f32[8,128]{1,0:T(8,128)S(1)}, u32[]{:S(2)}, u32[]{:S(2)}) collective-permute-start(f32[8,128]{1,0:T(8,128)S(1)} %get-tuple-element.28), channel_id=1, source_target_pairs={{64,0},{128,64},{192,128},{256,192},{320,256},{384,320},{448,384},... | collective-permute-start | bytes 12296 | tf_op jit(solution)/shard_map/ppermute | solution.py:366
